TPU v7x, 128 devices: a whole 4x4x4 slice. The times are simulated.
128 devices in a mesh: dp: 2 (over x_lo), ctx: 8 (over z, core), fsdp: 8 (over y, x_hi).
Axes of the slice: x: 4 (x_hi: 2, x_lo: 2; x = x_hi * 2 + x_lo), y: 4, z: 4, core: 2. Of those that a mesh axis runs over, the one named last changes fastest.
Arguments:
- hidden_in: bfloat16 [16, 1024, 1024], P(('dp', 'fsdp'), 'ctx'), may hold values from -6 to 6
- positions: int32 [16, 1024], P(('dp', 'fsdp')), may hold values from 0 to 1023, as said below
- cotangent: bfloat16 [16, 1024, 1024], P(('dp', 'fsdp'), 'ctx'), may hold values from -6 to 6
- attn_gain: float32 [1024], replicated, may hold values from 0.25 to 1.75
- w_query: bfloat16 [1024, 1024], P('fsdp'), may hold values from -0.1875 to 0.1875
- w_key: bfloat16 [1024, 512], P('fsdp'), may hold values from -0.1875 to 0.1875
- w_value: bfloat16 [1024, 512], P('fsdp'), may hold values from -0.1875 to 0.1875
- query_gain: float32 [64], replicated, may hold values from 0.25 to 1.75
- key_gain: float32 [64], replicated, may hold values from 0.25 to 1.75
- w_out: bfloat16 [1024, 1024], P('fsdp'), may hold values from -3 to 3
- ffn_gain: float32 [1024], replicated, may hold values from 0.25 to 1.75
- w_gate: bfloat16 [1024, 4608], P('fsdp'), may hold values from -0.1875 to 0.1875
- w_up: bfloat16 [1024, 4608], P('fsdp'), may hold values from -0.1875 to 0.1875
- w_down: bfloat16 [4608, 1024], P('fsdp'), may hold values from -0.09375 to 0.09375
Outputs:
- block_out: bfloat16 [16, 1024, 1024], P(('dp', 'fsdp'), 'ctx')
- grad_in: bfloat16 [16, 1024, 1024], P(('dp', 'fsdp'), 'ctx')
- grad_attn_gain: float32 [1024], replicated
- grad_w_query: float32 [1024, 1024], P('fsdp')
- grad_w_key: float32 [1024, 512], P('fsdp')
- grad_w_value: float32 [1024, 512], P('fsdp')
- grad_query_gain: float32 [64], replicated
- grad_key_gain: float32 [64], replicated
- grad_w_out: float32 [1024, 1024], P('fsdp')
- grad_ffn_gain: float32 [1024], replicated
- grad_w_gate: float32 [1024, 4608], P('fsdp')
- grad_w_up: float32 [1024, 4608], P('fsdp')
- grad_w_down: float32 [4608, 1024], P('fsdp')
Inputs may be any that keep to these rules, and one draw needn't show every extreme that they name: Each row holds every position once. The 128 entries that start at each multiple of 128 are two blocks of 64 consecutive increasing positions: block b and block 15 - b, in either order, where block b holds positions b * 64 to (b + 1) * 64 - 1.
All inputs are finite; a program needn't handle non-finite values.
Results may differ from a plain program's by a relative error of at most 0.024.
Values may be sent and summed in bfloat16 or wider, within the bound.
No kernel may reach another device: no remote copies, remote signals or barrier semaphores. Data moves between devices by JAX's collectives and lax.ppermute only.
A program may use at most 192 MiB of HBM per device.

v0:
```python
import jax
import jax.numpy as jnp
from jax import lax
from jax.sharding import PartitionSpec as P

NORM_EPSILON = 1e-05
ROPE_BASE = 1000000.0
MASKED_SCORE = -1e30


def rms_scale(values):
    return lax.rsqrt(jnp.mean(values * values, axis=-1, keepdims=True) + NORM_EPSILON)


def rope_tables(places, head_size):
    half_width = head_size // 2
    pair_index = jnp.arange(half_width, dtype=jnp.float32)
    frequency = ROPE_BASE ** (-2.0 * pair_index / head_size)
    angles = places.astype(jnp.float32)[:, None] * frequency[None, :]
    return (jnp.cos(angles)[:, None, :], jnp.sin(angles)[:, None, :])


def rotate(values, cosine_table, sine_table):
    half_width = values.shape[-1] // 2
    front = values[..., :half_width]
    back_half = values[..., half_width:]
    return jnp.concatenate(
        [
            front * cosine_table - back_half * sine_table,
            back_half * cosine_table + front * sine_table,
        ],
        axis=-1,
    )


def unrotate(grads_in, cosine_table, sine_table):
    half_width = grads_in.shape[-1] // 2
    front = grads_in[..., :half_width]
    back_half = grads_in[..., half_width:]
    return jnp.concatenate(
        [
            front * cosine_table + back_half * sine_table,
            back_half * cosine_table - front * sine_table,
        ],
        axis=-1,
    )


def norm_back(d_normed, normed_hat, scale_values, gain_vector):
    scaled = d_normed * gain_vector
    inner = jnp.mean(normed_hat * scaled, axis=-1, keepdims=True)
    return (scale_values * (scaled - normed_hat * inner), d_normed * normed_hat)


def times_transposed(left, right):
    return lax.dot_general(
        left, right, (((1,), (1,)), ((), ())), preferred_element_type=jnp.float32
    )


def outer_sum(left, right):
    return lax.dot_general(
        left, right, (((0,), (0,)), ((), ())), preferred_element_type=jnp.float32
    )


def row_folder(source, pieces):
    return tuple(
        (jnp.dot(source, piece_part, preferred_element_type=jnp.float32) for piece_part in pieces)
    )


def column_mapper(grad_parts, pieces):
    result = times_transposed(grad_parts[0], pieces[0])
    for grad_part, piece_part in zip(grad_parts[1:], pieces[1:]):
        result = result + times_transposed(grad_part, piece_part)
    return result


def attention_scores(query_group, key_all, allowed, score_scale):
    scores = (
        jnp.einsum("tkgd,lkd->kgtl", query_group, key_all, preferred_element_type=jnp.float32)
        * score_scale
    )
    return jnp.where(allowed, scores, MASKED_SCORE)


def body(
    hidden_in,
    positions,
    cotangent,
    attn_gain,
    w_query,
    w_key,
    w_value,
    query_gain,
    key_gain,
    w_out,
    ffn_gain,
    w_gate,
    w_up,
    w_down,
):
    tokens = hidden_in[0].astype(jnp.float32)
    token_count = tokens.shape[0]
    seq_places = positions[0]
    own_places = lax.dynamic_slice_in_dim(
        seq_places, lax.axis_index("ctx") * token_count, token_count
    )
    head_size = query_gain.shape[0]
    query_heads = w_query.shape[1] // head_size
    key_heads = w_key.shape[1] // head_size
    group_size = query_heads // key_heads
    score_scale = head_size ** (-0.5)
    cosine_table, sine_table = rope_tables(own_places, head_size)
    first_scale = rms_scale(tokens)
    first_hat = tokens * first_scale
    first_normed = (first_hat * attn_gain).astype(jnp.bfloat16)
    query_proj, key_proj, value_proj = row_folder(
        first_normed,
        (
            lax.all_gather(w_query, "fsdp", axis=0, tiled=True),
            lax.all_gather(w_key, "fsdp", axis=0, tiled=True),
            lax.all_gather(w_value, "fsdp", axis=0, tiled=True),
        ),
    )
    value_low = value_proj.astype(jnp.bfloat16)
    query_split = query_proj.reshape(token_count, query_heads, head_size)
    query_scale = rms_scale(query_split)
    query_hat = query_split * query_scale
    query_rot = rotate(query_hat * query_gain, cosine_table, sine_table).astype(jnp.bfloat16)
    key_split = key_proj.reshape(token_count, key_heads, head_size)
    key_scale = rms_scale(key_split)
    key_hat = key_split * key_scale
    key_rot = rotate(key_hat * key_gain, cosine_table, sine_table).astype(jnp.bfloat16)
    key_gathered, value_gathered = (
        lax.all_gather(
            key_rot.reshape(token_count, key_heads * head_size), "ctx", axis=0, tiled=True
        ),
        lax.all_gather(value_low, "ctx", axis=0, tiled=True),
    )
    seq_length = key_gathered.shape[0]
    key_all = key_gathered.reshape(seq_length, key_heads, head_size)
    value_all = value_gathered.reshape(seq_length, key_heads, head_size)
    query_group = query_rot.reshape(token_count, key_heads, group_size, head_size)
    allowed = seq_places[None, None, None, :] <= own_places[None, None, :, None]
    scores = attention_scores(query_group, key_all, allowed, score_scale)
    row_max = jnp.max(scores, axis=-1, keepdims=True)
    weights = jnp.exp(scores - row_max)
    row_total = jnp.sum(weights, axis=-1, keepdims=True)
    log_total = row_max + jnp.log(row_total)
    probs_low = (weights / row_total).astype(jnp.bfloat16)
    attn_mixed = jnp.einsum(
        "kgtl,lkd->tkgd", probs_low, value_all, preferred_element_type=jnp.float32
    )
    attn_mixed = attn_mixed.reshape(token_count, query_heads * head_size).astype(jnp.bfloat16)
    attn_proj = jnp.dot(
        attn_mixed,
        lax.all_gather(w_out, "fsdp", axis=0, tiled=True),
        preferred_element_type=jnp.float32,
    )
    residual = tokens + attn_proj
    second_scale = rms_scale(residual)
    second_hat = residual * second_scale
    second_normed = (second_hat * ffn_gain).astype(jnp.bfloat16)
    gate_pre, up_pre = row_folder(
        second_normed,
        (
            lax.all_gather(w_gate, "fsdp", axis=0, tiled=True),
            lax.all_gather(w_up, "fsdp", axis=0, tiled=True),
        ),
    )
    gate_act = jax.nn.silu(gate_pre)
    hidden = (gate_act * up_pre).astype(jnp.bfloat16)
    down_full = lax.all_gather(w_down, "fsdp", axis=0, tiled=True)
    block_out = (residual + jnp.dot(hidden, down_full, preferred_element_type=jnp.float32)).astype(
        jnp.bfloat16
    )
    seq_cotangent = cotangent[0]
    d_hidden = times_transposed(seq_cotangent, down_full)
    sigmoid_gate = jax.nn.sigmoid(gate_pre)
    d_gate = (d_hidden * up_pre * sigmoid_gate * (1.0 + gate_pre * (1.0 - sigmoid_gate))).astype(
        jnp.bfloat16
    )
    d_up = (d_hidden * gate_act).astype(jnp.bfloat16)
    d_second = column_mapper(
        (d_gate, d_up), lax.all_gather((w_gate, w_up), "fsdp", axis=0, tiled=True)
    )
    d_from_second, ffn_gain_part = norm_back(d_second, second_hat, second_scale, ffn_gain)
    d_resid = seq_cotangent.astype(jnp.float32) + d_from_second
    d_attn = d_resid.astype(jnp.bfloat16)
    d_mixed = times_transposed(d_attn, lax.all_gather(w_out, "fsdp", axis=0, tiled=True)).astype(
        jnp.bfloat16
    )
    d_mixed_group = d_mixed.reshape(token_count, key_heads, group_size, head_size)
    attn_probs = jnp.exp(attention_scores(query_group, key_all, allowed, score_scale) - log_total)
    probs_again = attn_probs.astype(jnp.bfloat16)
    d_value_part = jnp.einsum(
        "kgtl,tkgd->lkd", probs_again, d_mixed_group, preferred_element_type=jnp.float32
    )
    d_probs = jnp.einsum(
        "tkgd,lkd->kgtl", d_mixed_group, value_all, preferred_element_type=jnp.float32
    )
    d_scores = (
        attn_probs * (d_probs - jnp.sum(attn_probs * d_probs, axis=-1, keepdims=True))
    ).astype(jnp.bfloat16)
    d_query_rot = (
        jnp.einsum("kgtl,lkd->tkgd", d_scores, key_all, preferred_element_type=jnp.float32)
        * score_scale
    )
    d_key_part = (
        jnp.einsum("kgtl,tkgd->lkd", d_scores, query_group, preferred_element_type=jnp.float32)
        * score_scale
    )
    d_key_rot, d_value_sum = (
        lax.psum_scatter(
            d_key_part.reshape(seq_length, key_heads * head_size).astype(jnp.bfloat16),
            "ctx",
            scatter_dimension=0,
            tiled=True,
        ).astype(jnp.float32),
        lax.psum_scatter(
            d_value_part.reshape(seq_length, key_heads * head_size).astype(jnp.bfloat16),
            "ctx",
            scatter_dimension=0,
            tiled=True,
        ).astype(jnp.float32),
    )
    d_value = d_value_sum.astype(jnp.bfloat16)
    d_query_norm = unrotate(
        d_query_rot.reshape(token_count, query_heads, head_size), cosine_table, sine_table
    )
    d_query_heads, query_gain_part = norm_back(d_query_norm, query_hat, query_scale, query_gain)
    d_key_norm = unrotate(
        d_key_rot.reshape(token_count, key_heads, head_size), cosine_table, sine_table
    )
    d_key_heads, key_gain_part = norm_back(d_key_norm, key_hat, key_scale, key_gain)
    d_query = d_query_heads.reshape(token_count, query_heads * head_size).astype(jnp.bfloat16)
    d_key = d_key_heads.reshape(token_count, key_heads * head_size).astype(jnp.bfloat16)
    d_first = column_mapper(
        (d_query, d_key, d_value),
        lax.all_gather((w_query, w_key, w_value), "fsdp", axis=0, tiled=True),
    )
    d_from_first, attn_gain_part = norm_back(d_first, first_hat, first_scale, attn_gain)
    grad_in = (d_resid + d_from_first).astype(jnp.bfloat16)
    grad_attn_gain, grad_query_gain, grad_key_gain, grad_ffn_gain = lax.psum(
        (
            jnp.sum(attn_gain_part, axis=0),
            jnp.sum(query_gain_part, axis=(0, 1)),
            jnp.sum(key_gain_part, axis=(0, 1)),
            jnp.sum(ffn_gain_part, axis=0),
        ),
        ("dp", "ctx", "fsdp"),
    )
    query_width = w_query.shape[1]
    key_width = w_key.shape[1]
    gate_width = w_gate.shape[1]
    attn_right = jnp.concatenate([d_query, d_key, d_value], axis=1)
    ffn_right = jnp.concatenate([d_gate, d_up], axis=1)
    lefts = (
        lax.all_to_all(first_normed, "fsdp", split_axis=1, concat_axis=0, tiled=True),
        lax.all_to_all(second_normed, "fsdp", split_axis=1, concat_axis=0, tiled=True),
        lax.all_to_all(attn_mixed, "fsdp", split_axis=1, concat_axis=0, tiled=True),
        lax.all_to_all(hidden, "fsdp", split_axis=1, concat_axis=0, tiled=True),
    )
    pieces = (
        lax.all_gather(attn_right, "fsdp", axis=0, tiled=True),
        lax.all_gather(ffn_right, "fsdp", axis=0, tiled=True),
        lax.all_gather(d_attn, "fsdp", axis=0, tiled=True),
        lax.all_gather(seq_cotangent, "fsdp", axis=0, tiled=True),
    )
    parts = tuple((left_item for left_item in lefts))
    partial_value = tuple(
        (outer_sum(left_part, piece_part) for left_part, piece_part in zip(parts, pieces))
    )
    attn_grads, ffn_grads, grad_w_out, grad_w_down = (
        lax.psum(partial_value[0].astype(jnp.bfloat16), ("dp", "ctx")).astype(jnp.float32),
        lax.psum(partial_value[1].astype(jnp.bfloat16), ("dp", "ctx")).astype(jnp.float32),
        lax.psum(partial_value[2].astype(jnp.bfloat16), ("dp", "ctx")).astype(jnp.float32),
        lax.psum(partial_value[3].astype(jnp.bfloat16), ("dp", "ctx")).astype(jnp.float32),
    )
    grad_w_query = attn_grads[:, :query_width]
    grad_w_key = attn_grads[:, query_width : query_width + key_width]
    grad_w_value = attn_grads[:, query_width + key_width :]
    grad_w_gate = ffn_grads[:, :gate_width]
    grad_w_up = ffn_grads[:, gate_width:]
    return (
        block_out[None],
        grad_in[None],
        grad_attn_gain,
        grad_w_query,
        grad_w_key,
        grad_w_value,
        grad_query_gain,
        grad_key_gain,
        grad_w_out,
        grad_ffn_gain,
        grad_w_gate,
        grad_w_up,
        grad_w_down,
    )


def solution(mesh):
    in_specs = (
        P(("dp", "fsdp"), "ctx", None),
        P(("dp", "fsdp"), None),
        P(("dp", "fsdp"), "ctx", None),
        P(),
        P("fsdp", None),
        P("fsdp", None),
        P("fsdp", None),
        P(),
        P(),
        P("fsdp", None),
        P(),
        P("fsdp", None),
        P("fsdp", None),
        P("fsdp", None),
    )
    out_specs = (
        P(("dp", "fsdp"), "ctx", None),
        P(("dp", "fsdp"), "ctx", None),
        P(),
        P("fsdp", None),
        P("fsdp", None),
        P("fsdp", None),
        P(),
        P(),
        P("fsdp", None),
        P(),
        P("fsdp", None),
        P("fsdp", None),
        P("fsdp", None),
    )
    return jax.shard_map(body, mesh=mesh, in_specs=in_specs, out_specs=out_specs, check_vma=False)
```

profile of v0, /device:TPU:1, one launch (start us, length us, event | category | flops | bytes accessed | tf_op | source)
XLA Modules:
  0.0 1270.8 jit_solution(9632504240857041391)
XLA Ops:
  10.6 47.9 %all-gather.15.cloned.1.call-done = bf16[1024,512]{1,0:T(8,128)(2,1)} async-done(((bf16[128,512]{1,0:T(8,128)(2,1)}), bf16[1024,512]{1,0:T(8,128)(2,1)}) %all-gather.15.cloned.1.call-update) | async-done | bytes 1048592 | tf_op jit(solution)/shard_map/all_gather | solution.py:124
  61.1 44.8 %all-gather.19.cloned.1.call-done = bf16[1024,512]{1,0:T(8,128)(2,1)} async-done(((bf16[128,512]{1,0:T(8,128)(2,1)}), bf16[1024,512]{1,0:T(8,128)(2,1)}) %all-gather.19.cloned.1.call-update) | async-done | bytes 1048592 | tf_op jit(solution)/shard_map/all_gather | solution.py:123
  112.6 49.4 %all-gather.23.cloned.1.call-done = bf16[1024,1024]{1,0:T(8,128)(2,1)} async-done(((bf16[128,1024]{1,0:T(8,128)(2,1)}), bf16[1024,1024]{1,0:T(8,128)(2,1)}) %all-gather.23.cloned.1.call-update) | async-done | bytes 2097168 | tf_op jit(solution)/shard_map/all_gather | solution.py:122
  162.0 3.9 copy.52
  166.0 20.6 %all-gather.17.cloned.1.call-done = bf16[1024,512]{1,0:T(8,128)(2,1)} async-done(((bf16[128,512]{1,0:T(8,128)(2,1)}), bf16[1024,512]{1,0:T(8,128)(2,1)}) %all-gather.17.cloned.1.call-update) | async-done | bytes 1048592 | tf_op jit(solution)/shard_map/all_gather | solution.py:140
  190.9 21.2 %all-gather.21.cloned.1.call-done = bf16[1024,512]{0,1:T(8,128)(2,1)} async-done(((bf16[128,512]{0,1:T(8,128)(2,1)}), bf16[1024,512]{0,1:T(8,128)(2,1)}) %all-gather.21.cloned.1.call-update) | async-done | bytes 1048592 | tf_op jit(solution)/shard_map/all_gather | solution.py:137
  219.7 48.5 %all-gather.25.cloned.1.call-done = bf16[1024,1024]{1,0:T(8,128)(2,1)} async-done(((bf16[128,1024]{1,0:T(8,128)(2,1)}), bf16[1024,1024]{1,0:T(8,128)(2,1)}) %all-gather.25.cloned.1.call-update) | async-done | bytes 2097168 | tf_op jit(solution)/shard_map/all_gather | solution.py:159
  270.4 114.5 %all-gather.27.cloned.1.call-done = bf16[1024,4608]{1,0:T(8,128)(2,1)} async-done(((bf16[128,4608]{1,0:T(8,128)(2,1)}), bf16[1024,4608]{1,0:T(8,128)(2,1)}) %all-gather.27.cloned.1.call-update) | async-done | bytes 9437200 | tf_op jit(solution)/shard_map/all_gather | solution.py:169
  384.9 6.5 fusion.59
  391.5 110.1 %all-gather.29.cloned.1.call-done = bf16[1024,4608]{1,0:T(8,128)(2,1)} async-done(((bf16[128,4608]{1,0:T(8,128)(2,1)}), bf16[1024,4608]{1,0:T(8,128)(2,1)}) %all-gather.29.cloned.1.call-update) | async-done | bytes 9437200 | tf_op jit(solution)/shard_map/all_gather | solution.py:170
  501.6 6.5 fusion.60
  508.2 110.1 %all-gather.31.cloned.1.call-done = bf16[4608,1024]{1,0:T(8,128)(2,1)} async-done(((bf16[576,1024]{1,0:T(8,128)(2,1)}), bf16[4608,1024]{1,0:T(8,128)(2,1)}) %all-gather.31.cloned.1.call-update) | async-done | bytes 9437200 | tf_op jit(solution)/shard_map/all_gather | solution.py:175
  618.3 8.7 multiply_convert_fusion
  627.1 7.6 fusion.61
  634.8 3.9 multiply_reduce_fusion
  645.4 5.6 fusion
  656.4 5.9 bitcast_convert_fusion
  670.9 13.0 %reduce-scatter.7.cloned.1.call-done = bf16[128,512]{1,0:T(8,128)(2,1)} async-done(((bf16[1024,512]{1,0:T(8,128)(2,1)}), bf16[128,512]{1,0:T(8,128)(2,1)}) %reduce-scatter.7.cloned.1.call-update) | async-done | bytes 131088
  685.7 31.4 %reduce-scatter.9.cloned.1.call-done = bf16[128,512]{1,0:T(8,128)(2,1)} async-done(((bf16[1024,512]{1,0:T(8,128)(2,1)}), bf16[128,512]{1,0:T(8,128)(2,1)}) %reduce-scatter.9.cloned.1.call-update) | async-done | bytes 131088
  728.3 6.7 all-to-all-start.3
  737.7 12.1 all-to-all-done.3
  749.8 8.6 all-to-all-start.1
  758.4 25.7 %all-gather.39.cloned.1.call-done = bf16[1,1024,1024]{2,1,0:T(8,128)(2,1)} async-done(((bf16[1,128,1024]{2,1,0:T(8,128)(2,1)}), bf16[1,1024,1024]{2,1,0:T(8,128)(2,1)}) %all-gather.39.cloned.1.call-update) | async-done | bytes 2097168 | tf_op jit(solution)/shard_map/all_gather | solution.py:270
  784.1 4.0 fusion.15
  791.8 46.8 %all-gather.35.cloned.1.call-done = bf16[1024,1024]{1,0:T(8,128)(2,1)} async-done(((bf16[128,1024]{1,0:T(8,128)(2,1)}), bf16[1024,1024]{1,0:T(8,128)(2,1)}) %all-gather.35.cloned.1.call-update) | async-done | bytes 2097168 | tf_op jit(solution)/shard_map/all_gather | solution.py:269
  844.9 67.9 %all-gather.33.cloned.1.call-done = bf16[1024,2048]{0,1:T(8,128)(2,1)} async-done(((bf16[128,2048]{0,1:T(8,128)(2,1)}), bf16[1024,2048]{0,1:T(8,128)(2,1)}) %all-gather.33.cloned.1.call-update) | async-done | bytes 4194320 | tf_op jit(solution)/shard_map/all_gather | solution.py:267
  912.7 4.5 convolution_convert_fusion.1
  917.2 197.8 %all-gather.37.cloned.1.call-done = bf16[1024,9216]{1,0:T(8,128)(2,1)} async-done(((bf16[128,9216]{1,0:T(8,128)(2,1)}), bf16[1024,9216]{1,0:T(8,128)(2,1)}) %all-gather.37.cloned.1.call-update) | async-done | bytes 18874384 | tf_op jit(solution)/shard_map/all_gather | solution.py:268
  1115.0 10.5 convolution_convert_fusion
  1128.9 5.9 fusion.22
  1136.6 66.4 %all-reduce = (f32[1024]{0:T(1024)}, f32[64]{0:T(128)}, f32[64]{0:T(128)}, f32[1024]{0:T(1024)}) all-reduce(f32[1024]{0:T(1024)S(1)} %get-tuple-element.17, f32[64]{0:T(128)S(1)} %copy-done.45, f32[64]{0:T(128)S(1)} %copy-done.46, f32[1024]{0:T(1024)S(1)} %copy-done.40), channel_id=1, replica_groups=mesh['dp'=2,'ctx'=8,'fsdp'=8] {'dp','ctx','fsdp'}, use_global_device_ids=true, to_apply=%region_14.15 | all-reduce | flops 2176 | bytes 17408 | tf_op jit(solution)/shard_map/psum | solution.py:246
  1204.1 50.2 %all-reduce.4.cloned.1.call-done = (bf16[128,2048]{1,0:T(8,128)(2,1)}, bf16[128,1024]{1,0:T(8,128)(2,1)}, bf16[128,9216]{1,0:T(8,128)(2,1)}, bf16[576,1024]{1,0:T(8,128)(2,1)}) async-done(((bf16[128,2048]{1,0:T(8,128)(2,1)}, bf16[128,1024]{1,0:T(8,128)(2,1)}, bf16[128,9216]{1,0:T(8,128)(2,1)}, bf16[576,1024]{1,0:T(8,128)(2,1)}), (bf16[128,2048]{1,0:T(8,128)(2,1)}, bf16[128,1024]{1,0:T(8,128)(2,1)}, ...) | async-done | bytes 4325392 | tf_op jit(solution)/shard_map/psum | solution.py:277
  (203 shorter events, 88.6 us)
Async XLA Ops:
  7.2 100.2 %copy-start.3 = (bf16[1,128,1024]{2,1,0:T(8,128)(2,1)S(1)}, bf16[1,128,1024]{2,1,0:T(8,128)(2,1)}, u32[]{:S(2)}) copy-start(bf16[1,128,1024]{2,1,0:T(8,128)(2,1)} %param.14) | copy-start | bytes 786436
  7.2 100.2 %copy-start.31 = (f32[1024]{0:T(1024)S(1)}, f32[1024]{0:T(1024)}, u32[]{:S(2)}) copy-start(f32[1024]{0:T(1024)} %param.17) | copy-start | bytes 12292
  7.2 51.3 %all-gather.15.cloned.1.call-start = ((), (), s32[]{:S(2)}) async-start(), calls=%async_computation.6 | async-start | bytes 1179648 | tf_op jit(solution)/shard_map/all_gather | solution.py:124
  7.9 98.0 %all-gather.19.cloned.1.call-start = ((), (), s32[]{:S(2)}) async-start(), calls=%async_computation.8 | async-start | bytes 1179648 | tf_op jit(solution)/shard_map/all_gather | solution.py:123
  8.7 153.3 %all-gather.23.cloned.1.call-start = ((), (), s32[]{:S(2)}) async-start(), calls=%async_computation.10 | async-start | bytes 2359296 | tf_op jit(solution)/shard_map/all_gather | solution.py:122
  9.4 177.1 %all-gather.17.cloned.1.call-start = ((), (), s32[]{:S(2)}) async-start(), calls=%async_computation.7 | async-start | bytes 1179648 | tf_op jit(solution)/shard_map/all_gather | solution.py:140
  10.6 177.6 %copy-start.38 = (f32[128]{0:T(128)}, f32[128]{0:T(128)S(1)}, u32[]{:S(2)}) copy-start(f32[128]{0:T(128)S(1)} %add_rsqrt_fusion.3) | copy-start | bytes 1540
  10.6 98.1 %copy-start.44 = (f32[64]{0:T(128)S(1)}, f32[64]{0:T(128)}, u32[]{:S(2)}) copy-start(f32[64]{0:T(128)} %param.22) | copy-start | bytes 772
  60.8 151.3 %all-gather.21.cloned.1.call-start = ((), (), s32[]{:S(2)}) async-start(), calls=%async_computation.9 | async-start | bytes 1179648 | tf_op jit(solution)/shard_map/all_gather | solution.py:137
  61.1 129.7 %copy-start.27 = (f32[128,32]{0,1:T(8,128)}, f32[128,32]{0,1:T(8,128)S(1)}, u32[]{:S(2)}) copy-start(f32[128,32]{0,1:T(8,128)S(1)} %get-tuple-element.46) | copy-start | bytes 49156
  61.1 129.7 %copy-start.29 = (f32[128,32]{0,1:T(8,128)}, f32[128,32]{0,1:T(8,128)S(1)}, u32[]{:S(2)}) copy-start(f32[128,32]{0,1:T(8,128)S(1)} %get-tuple-element.47) | copy-start | bytes 49156
  109.5 158.7 %all-gather.25.cloned.1.call-start = ((), (), s32[]{:S(2)}) async-start(), calls=%async_computation.11 | async-start | bytes 2359296 | tf_op jit(solution)/shard_map/all_gather | solution.py:159
  110.1 274.8 %all-gather.27.cloned.1.call-start = ((), (), s32[]{:S(2)}) async-start(), calls=%async_computation.12 | async-start | bytes 10616832 | tf_op jit(solution)/shard_map/all_gather | solution.py:169
  110.9 390.8 %all-gather.29.cloned.1.call-start = ((), (), s32[]{:S(2)}) async-start(), calls=%async_computation.13 | async-start | bytes 10616832 | tf_op jit(solution)/shard_map/all_gather | solution.py:170
  111.6 506.7 %all-gather.31.cloned.1.call-start = ((), (), s32[]{:S(2)}) async-start(), calls=%async_computation.14 | async-start | bytes 10616832 | tf_op jit(solution)/shard_map/all_gather | solution.py:175
  112.3 571.6 %reduce-scatter.7.cloned.1.call-start = ((), (), s32[]{:S(2)}) async-start(), calls=%async_computation.19 | async-start | bytes 1179648
  219.7 171.8 %copy-start.23 = (bf16[8,64,2,128]{3,1,2,0:T(8,128)(2,1)}, bf16[8,64,2,128]{3,1,2,0:T(8,128)(2,1)S(1)}, u32[]{:S(2)}) copy-start(bf16[8,64,2,128]{3,1,2,0:T(8,128)(2,1)S(1)} %fusion.18) | copy-start | bytes 786436
  219.7 165.2 %copy-start.25 = (f32[1024]{0:T(1024)S(1)}, f32[1024]{0:T(1024)}, u32[]{:S(2)}) copy-start(f32[1024]{0:T(1024)} %param.24) | copy-start | bytes 12292
  270.4 231.2 %copy-start.35 = (f32[128]{0:T(128)}, f32[128]{0:T(128)S(1)}, u32[]{:S(2)}) copy-start(f32[128]{0:T(128)S(1)} %add_rsqrt_fusion.2) | copy-start | bytes 1540
  656.4 60.8 %reduce-scatter.9.cloned.1.call-start = ((), (), s32[]{:S(2)}) async-start(), calls=%async_computation.20 | async-start | bytes 1179648
  664.7 119.4 %all-gather.39.cloned.1.call-start = ((), (), s32[]{:S(2)}) async-start(), calls=%async_computation.18 | async-start | bytes 2359296 | tf_op jit(solution)/shard_map/all_gather | solution.py:270
  665.3 173.3 %all-gather.35.cloned.1.call-start = ((), (), s32[]{:S(2)}) async-start(), calls=%async_computation.16 | async-start | bytes 2359296 | tf_op jit(solution)/shard_map/all_gather | solution.py:269
  666.0 246.7 %all-gather.33.cloned.1.call-start = ((), (), s32[]{:S(2)}) async-start(), calls=%async_computation.15 | async-start | bytes 4718592 | tf_op jit(solution)/shard_map/all_gather | solution.py:267
  723.9 391.1 %all-gather.37.cloned.1.call-start = ((), (), s32[]{:S(2)}) async-start(), calls=%async_computation.17 | async-start | bytes 21233664 | tf_op jit(solution)/shard_map/all_gather | solution.py:268
  728.3 21.5 %all-to-all-start.3 = ((bf16[128,8,576]{0,2,1:T(8,128)(2,1)}), bf16[128,8,576]{0,2,1:T(8,128)(2,1)S(1)}, u32[]{:S(2)}, u32[]{:S(2)}) async-start(bf16[128,8,576]{0,2,1:T(8,128)(2,1)} %bitcast.53), calls=%async_computation.3 | async-start | bytes 2359296 | tf_op jit(solution)/shard_map/all_to_all | solution.py:264
  749.8 38.3 %all-to-all-start.1 = ((bf16[128,8,128]{2,0,1:T(8,128)(2,1)}), bf16[128,8,128]{2,0,1:T(8,128)(2,1)S(1)}, u32[]{:S(2)}, u32[]{:S(2)}) async-start(bf16[128,8,128]{2,0,1:T(8,128)(2,1)} %copy.59), calls=%async_computation.1 | async-start | bytes 524288 | tf_op jit(solution)/shard_map/all_to_all | solution.py:263
  788.1 53.3 %all-to-all-start = ((bf16[128,8,128]{2,0,1:T(8,128)(2,1)}), bf16[128,8,128]{2,0,1:T(8,128)(2,1)S(1)}, u32[]{:S(2)}, u32[]{:S(2)}) async-start(bf16[128,8,128]{2,0,1:T(8,128)(2,1)} %fusion.40), calls=%async_computation | async-start | bytes 524288 | tf_op jit(solution)/shard_map/all_to_all | solution.py:261
  841.4 75.8 %all-to-all-start.2 = ((bf16[128,8,128]{2,0,1:T(8,128)(2,1)}), bf16[128,8,128]{2,0,1:T(8,128)(2,1)S(1)}, u32[]{:S(2)}, u32[]{:S(2)}) async-start(bf16[128,8,128]{2,0,1:T(8,128)(2,1)} %copy_bitcast_fusion), calls=%async_computation.2 | async-start | bytes 524288 | tf_op jit(solution)/shard_map/all_to_all | solution.py:262
  844.8 409.5 %all-reduce.4.cloned.1.call-start = ((), (), s32[]{:S(2)}) async-start(), calls=%async_computation.21 | async-start | bytes 8650752 | tf_op jit(solution)/shard_map/psum | solution.py:277
  1134.8 68.2 %copy-start.7 = (f32[128,1024]{1,0:T(8,128)S(1)}, f32[128,1024]{1,0:T(8,128)}, u32[]{:S(2)}) copy-start(f32[128,1024]{1,0:T(8,128)} %copy-done.6) | copy-start | bytes 1572868
  1134.8 68.2 %copy-start.17 = (bf16[1,128,1024]{2,1,0:T(8,128)(2,1)S(1)}, bf16[1,128,1024]{2,1,0:T(8,128)(2,1)}, u32[]{:S(2)}) copy-start(bf16[1,128,1024]{2,1,0:T(8,128)(2,1)} %param.16) | copy-start | bytes 786436
  1134.8 68.2 %copy-start.48 = (f32[128]{0:T(128)S(1)}, f32[128]{0:T(128)}, u32[]{:S(2)}) copy-start(f32[128]{0:T(128)} %copy-done.47) | copy-start | bytes 1540
  (39 other events, 380.6 us)
Sparse Core Ops, SparseCore 0:
  10.4 48.0 all-gather.14
  60.8 45.0 all-gather.18
  108.3 53.7 all-gather.22
  164.2 22.3 all-gather.16
  188.6 23.4 all-gather.20
  214.3 53.8 all-gather.24
  270.5 114.3 all-gather.26
  387.2 114.3 all-gather.28
  503.9 114.3 all-gather.30
  656.5 27.4 reduce-scatter.6
  686.3 30.7 reduce-scatter.8
  719.3 64.7 all-gather.38
  787.0 51.5 all-gather.34
  841.2 71.4 all-gather.32
  915.4 199.5 all-gather.36
  1125.7 128.5 all-reduce.3
where the time goes:
time: 1270 us
  waiting for transfers between devices  1020 us (80%)
  matrix products  95.2 us (7%)
  blocking collectives  66.4 us (5%)
  local copies, waits for them, and re-layouts  30.4 us (2%)
  starting transfers between devices  23 us (2%)
  other arithmetic  22.9 us (2%)
  between operations  14.7 us (1%)
    all_gather x1, waiting for transfers between devices, body(): lax.all_gather(ffn_right, 'fsdp', axis=0, tiled=True)  198 us
    all_gather x1, waiting for transfers between devices, body(): lax.all_gather(w_gate, 'fsdp', axis=0, tiled=True)  115 us
    all_gather x1, waiting for transfers between devices, body(): down_full = lax.all_gather(w_down, 'fsdp', axis=0, tiled=True)  110 us
    all_gather x1, waiting for transfers between devices, body(): lax.all_gather(w_up, 'fsdp', axis=0, tiled=True)  110 us
    all_gather x1, waiting for transfers between devices, body(): lax.all_gather(attn_right, 'fsdp', axis=0, tiled=True)  67.9 us
    psum x1, blocking collectives, body(): lax.psum((jnp.sum(attn_gain_part, axis=0), jnp.sum(query_gain_part, axis=...  66.4 us
    unnamed x18, waiting for transfers between devices  50.4 us
    psum x1, waiting for transfers between devices, body(): lax.psum(partial_value[0].astype(jnp.bfloat16), ('dp', 'ctx'))  50.2 us
  transfers between devices with their start and end apart: 20, of which 17 were waited for; matrix products, arithmetic and copies ran while one was open for 7% of the time, Pallas kernels for 0%

commit v1 on v0

v1 whole, which is shorter than its diff:
```python
import jax
import jax.numpy as jnp
from jax import lax
from jax.sharding import PartitionSpec as P

NORM_EPSILON = 1e-05
ROPE_BASE = 1000000.0
MASKED_SCORE = -1e30
BF16 = jnp.bfloat16
F32 = jnp.float32
STEPS = (0, -1, 1, 2)


def rms_scale(values):
    return lax.rsqrt(jnp.mean(values * values, axis=-1, keepdims=True) + NORM_EPSILON)


def rope_tables(places, head_size):
    half_width = head_size // 2
    pair_index = jnp.arange(half_width, dtype=F32)
    frequency = ROPE_BASE ** (-2.0 * pair_index / head_size)
    angles = places.astype(F32)[:, None] * frequency[None, :]
    return (jnp.cos(angles)[:, None, :], jnp.sin(angles)[:, None, :])


def rotate(values, cosine_table, sine_table):
    half_width = values.shape[-1] // 2
    front = values[..., :half_width]
    back_half = values[..., half_width:]
    return jnp.concatenate(
        [
            front * cosine_table - back_half * sine_table,
            back_half * cosine_table + front * sine_table,
        ],
        axis=-1,
    )


def unrotate(grads_in, cosine_table, sine_table):
    return rotate(grads_in, cosine_table, -sine_table)


def norm_back(d_normed, normed_hat, scale_values, gain_vector):
    scaled = d_normed * gain_vector
    inner = jnp.mean(normed_hat * scaled, axis=-1, keepdims=True)
    return (scale_values * (scaled - normed_hat * inner), d_normed * normed_hat)


def mm(left, right):
    return jnp.dot(left, right, preferred_element_type=F32)


def mm_t(left, right):
    return lax.dot_general(left, right, (((1,), (1,)), ((), ())), preferred_element_type=F32)


def outer_sum(left, right):
    return lax.dot_general(left, right, (((0,), (0,)), ((), ())), preferred_element_type=F32)


def swap_core(value):
    return lax.ppermute(value, "ctx", [(i, i ^ 1) for i in range(8)])


def move_z(value, step):
    return lax.ppermute(value, "ctx", [(i, (i + 2 * step) % 8) for i in range(8)])


def gather_ctx(block):
    groups = []
    for step in STEPS:
        mine = block if step == 0 else move_z(block, -step)
        groups.append(jnp.concatenate([mine, swap_core(mine)], axis=0))
    return groups


def scatter_ctx(groups):
    total = None
    sums = {}
    for step in (2, 1, -1, 0):
        part = groups[STEPS.index(step)]
        half = part.shape[0] // 2
        other = swap_core(part[half:].astype(BF16))
        sums[step] = part[:half] + other.astype(F32)
    total = sums[0]
    for step in (1, -1, 2):
        total = total + move_z(sums[step].astype(BF16), step).astype(F32)
    return total


def transpose_mesh(value, flip=0):
    pairs = [
        ((d * 8 + c) * 8 + f, ((d ^ flip) * 8 + f) * 8 + c) for d in range(2) for c in range(8) for f in range(8)
    ]
    return lax.ppermute(value, ("dp", "ctx", "fsdp"), pairs)


def swap_dp(value):
    return lax.ppermute(value, "dp", [(0, 1), (1, 0)])


def after(value, *others):
    return lax.optimization_barrier((value, *others))[0]


def gather_fsdp_rows(block):
    copies = jnp.broadcast_to(block[None], (8, *block.shape))
    return lax.all_to_all(copies, "fsdp", split_axis=0, concat_axis=0, tiled=True).reshape(-1, block.shape[1])


def sum_fsdp_rows(partial):
    parts = lax.all_to_all(partial.astype(BF16), "fsdp", split_axis=0, concat_axis=0, tiled=True)
    return jnp.sum(parts.reshape(8, -1, partial.shape[1]).astype(F32), axis=0).astype(BF16)


def sum_dp(low):
    return (low.astype(F32) + swap_dp(low).astype(F32)).astype(BF16)


def sum_dp_transposed(low):
    return (transpose_mesh(low).astype(F32) + transpose_mesh(low, 1).astype(F32)).astype(BF16)


def gather_ctx_parts(block):
    parts = []
    for step in STEPS:
        mine = block if step == 0 else move_z(block, -step)
        parts += [mine, swap_core(mine)]
    stacked = jnp.stack(parts)
    ctx = lax.axis_index("ctx")
    ordered = []
    for owner in range(8):
        away = (owner // 2 - ctx // 2) % 4
        slot = jnp.array([0, 2, 3, 1])[away] * 2 + (owner % 2 ^ ctx % 2)
        ordered.append(lax.dynamic_index_in_dim(stacked, slot, 0, keepdims=False))
    return ordered


def sum_all(value):
    total = value + swap_core(value)
    total = total + move_z(total, 1) + move_z(total, -1) + move_z(total, 2)
    total = total + swap_dp(total)
    for step in (1, 2, 4):
        total = total + lax.ppermute(total, "fsdp", [(i, i ^ step) for i in range(8)])
    return total


def own_columns(weight, width, index):
    return lax.dynamic_slice_in_dim(weight, index * width, width, 1)


def body(
    hidden_in,
    positions,
    cotangent,
    attn_gain,
    w_query,
    w_key,
    w_value,
    query_gain,
    key_gain,
    w_out,
    ffn_gain,
    w_gate,
    w_up,
    w_down,
):
    ctx = lax.axis_index("ctx")
    tokens = hidden_in[0].astype(F32)
    count, width = tokens.shape
    head_size = query_gain.shape[0]
    q_width = w_query.shape[1] // 8
    k_width = w_key.shape[1] // 8
    ff_width = w_gate.shape[1] // 8
    group_size = q_width // k_width
    score_scale = head_size ** (-0.5)

    w_qkv = gather_fsdp_rows(
        jnp.concatenate(
            [own_columns(w_query, q_width, ctx), own_columns(w_key, k_width, ctx), own_columns(w_value, k_width, ctx)],
            axis=1,
        )
    )
    out_rows = transpose_mesh(w_out)
    down_chunk = transpose_mesh(jnp.transpose(own_columns(w_down, width // 8, ctx)))
    ffn_block = jnp.concatenate(
        [own_columns(w_gate, ff_width, ctx), own_columns(w_up, ff_width, ctx), down_chunk], axis=1
    )
    ffn_rows = gather_fsdp_rows(after(ffn_block, w_qkv))
    gate_up, down_t = ffn_rows[:, : 2 * ff_width], ffn_rows[:, 2 * ff_width :]

    z_index, core = ctx // 2, ctx % 2
    owners = jnp.stack(
        [((z_index + step) % 4) * 2 + (core ^ flip) for step in STEPS for flip in (0, 1)]
    )
    places = positions[0].reshape(8, count)[owners].reshape(8 * count)
    cosine_table, sine_table = rope_tables(places, head_size)

    first_scale = rms_scale(tokens)
    first_hat = tokens * first_scale
    first_normed = (first_hat * attn_gain).astype(BF16)
    first_groups = gather_ctx(first_normed)
    cot_groups = gather_ctx(after(cotangent[0], *first_groups))

    qkv = jnp.concatenate([mm(group, w_qkv) for group in first_groups], axis=0)
    length = qkv.shape[0]
    query_split = qkv[:, :q_width].reshape(length, group_size, head_size)
    key_split = qkv[:, q_width : q_width + k_width].reshape(length, 1, head_size)
    value_low = qkv[:, q_width + k_width :].astype(BF16)
    query_scale = rms_scale(query_split)
    query_hat = query_split * query_scale
    query_rot = rotate(query_hat * query_gain, cosine_table, sine_table).astype(BF16)
    key_scale = rms_scale(key_split)
    key_hat = key_split * key_scale
    key_rot = rotate(key_hat * key_gain, cosine_table, sine_table).astype(BF16)[:, 0]

    allowed = places[None, None, :] <= places[None, :, None]
    scores = jnp.einsum("tgd,ld->gtl", query_rot, key_rot, preferred_element_type=F32) * score_scale
    scores = jnp.where(allowed, scores, MASKED_SCORE)
    row_max = jnp.max(scores, axis=-1, keepdims=True)
    weights = jnp.exp(scores - row_max)
    row_total = jnp.sum(weights, axis=-1, keepdims=True)
    probs = weights / row_total
    probs_low = probs.astype(BF16)
    mixed = jnp.einsum("gtl,ld->tgd", probs_low, value_low, preferred_element_type=F32)
    mixed = mixed.reshape(length, q_width).astype(BF16)
    rows = 2 * count
    attn_proj = scatter_ctx([mm(mixed[i * rows : (i + 1) * rows], out_rows) for i in range(4)])

    residual = tokens + attn_proj
    second_scale = rms_scale(residual)
    second_hat = residual * second_scale
    second_normed = (second_hat * ffn_gain).astype(BF16)
    second_groups = gather_ctx(second_normed)

    hidden_groups, d_ffn_groups, block_parts, d_second_parts = [], [], [], []
    for second_group, cot_group in zip(second_groups, cot_groups):
        both = mm(second_group, gate_up)
        gate_pre, up_pre = both[:, :ff_width], both[:, ff_width:]
        sigmoid_gate = jax.nn.sigmoid(gate_pre)
        gate_act = gate_pre * sigmoid_gate
        hidden = (gate_act * up_pre).astype(BF16)
        d_hidden = mm(cot_group, down_t)
        d_gate = (d_hidden * up_pre * sigmoid_gate * (1.0 + gate_pre * (1.0 - sigmoid_gate))).astype(BF16)
        d_up = (d_hidden * gate_act).astype(BF16)
        d_ffn = jnp.concatenate([d_gate, d_up], axis=1)
        hidden_groups.append(hidden)
        d_ffn_groups.append(d_ffn)
        d_second_parts.append(mm_t(d_ffn, gate_up))
        block_parts.append(mm_t(hidden, down_t))
    d_second = scatter_ctx(d_second_parts)
    block_out = (residual + scatter_ctx(block_parts)).astype(BF16)

    ffn_partial = jnp.concatenate(
        [
            outer_sum(jnp.concatenate(second_groups, axis=0), jnp.concatenate(d_ffn_groups, axis=0)).astype(BF16),
            outer_sum(jnp.concatenate(cot_groups, axis=0), jnp.concatenate(hidden_groups, axis=0)).astype(BF16),
        ],
        axis=1,
    )
    ffn_sum = sum_fsdp_rows(ffn_partial)

    d_from_second, ffn_gain_part = norm_back(d_second, second_hat, second_scale, ffn_gain)
    d_resid = cotangent[0].astype(F32) + d_from_second
    d_attn = d_resid.astype(BF16)
    d_attn_all = jnp.concatenate(gather_ctx(d_attn), axis=0)

    d_mixed = mm_t(d_attn_all, out_rows).astype(BF16)
    d_mixed_split = d_mixed.reshape(length, group_size, head_size)
    d_value = jnp.einsum("gtl,tgd->ld", probs_low, d_mixed_split, preferred_element_type=F32).astype(BF16)
    d_probs = jnp.einsum("tgd,ld->gtl", d_mixed_split, value_low, preferred_element_type=F32)
    d_scores = (probs * (d_probs - jnp.sum(probs * d_probs, axis=-1, keepdims=True))).astype(BF16)
    d_query_rot = jnp.einsum("gtl,ld->tgd", d_scores, key_rot, preferred_element_type=F32) * score_scale
    d_key_rot = jnp.einsum("gtl,tgd->ld", d_scores, query_rot, preferred_element_type=F32) * score_scale
    d_query_heads, query_gain_part = norm_back(
        unrotate(d_query_rot, cosine_table, sine_table), query_hat, query_scale, query_gain
    )
    d_key_heads, key_gain_part = norm_back(
        unrotate(d_key_rot[:, None], cosine_table, sine_table), key_hat, key_scale, key_gain
    )
    d_qkv = jnp.concatenate(
        [d_query_heads.reshape(length, q_width).astype(BF16), d_key_heads[:, 0].astype(BF16), d_value], axis=1
    )
    d_qkv, ffn_sum = lax.optimization_barrier((d_qkv, ffn_sum))
    d_first = scatter_ctx([mm_t(d_qkv[i * rows : (i + 1) * rows], w_qkv) for i in range(4)])
    d_from_first, attn_gain_part = norm_back(d_first, first_hat, first_scale, attn_gain)
    grad_in = (d_resid + d_from_first).astype(BF16)

    gains = sum_all(
        jnp.concatenate(
            [
                jnp.sum(attn_gain_part, axis=0),
                jnp.sum(ffn_gain_part, axis=0),
                jnp.sum(query_gain_part, axis=(0, 1)),
                jnp.sum(key_gain_part, axis=(0, 1)),
            ]
        )[None]
    )[0]
    grad_attn_gain = gains[:width]
    grad_ffn_gain = gains[width : 2 * width]
    grad_query_gain = gains[2 * width : 2 * width + head_size]
    grad_key_gain = gains[2 * width + head_size :]

    attn_partial = jnp.concatenate(
        [
            outer_sum(jnp.concatenate(first_groups, axis=0), d_qkv).astype(BF16),
            outer_sum(d_attn_all, mixed).astype(BF16),
        ],
        axis=1,
    )
    attn_sum = sum_fsdp_rows(attn_partial)
    qkv_width = q_width + 2 * k_width
    ffn_parts = gather_ctx_parts(
        jnp.concatenate([sum_dp(ffn_sum[:, : 2 * ff_width]), sum_dp_transposed(ffn_sum[:, 2 * ff_width :])], axis=1)
    )
    attn_parts = gather_ctx_parts(
        jnp.concatenate([sum_dp(attn_sum[:, :qkv_width]), sum_dp_transposed(attn_sum[:, qkv_width:])], axis=1)
    )

    def side_by_side(parts, low, high):
        return jnp.concatenate([part[:, low:high] for part in parts], axis=1).astype(F32)

    def stacked_rows(parts, low):
        return jnp.transpose(jnp.concatenate([part[:, low:] for part in parts], axis=0)).astype(F32)

    return (
        block_out[None],
        grad_in[None],
        grad_attn_gain,
        side_by_side(attn_parts, 0, q_width),
        side_by_side(attn_parts, q_width, q_width + k_width),
        side_by_side(attn_parts, q_width + k_width, qkv_width),
        grad_query_gain,
        grad_key_gain,
        stacked_rows(attn_parts, qkv_width),
        grad_ffn_gain,
        side_by_side(ffn_parts, 0, ff_width),
        side_by_side(ffn_parts, ff_width, 2 * ff_width),
        stacked_rows(ffn_parts, 2 * ff_width),
    )


def solution(mesh):
    in_specs = (
        P(("dp", "fsdp"), "ctx", None),
        P(("dp", "fsdp"), None),
        P(("dp", "fsdp"), "ctx", None),
        P(),
        P("fsdp", None),
        P("fsdp", None),
        P("fsdp", None),
        P(),
        P(),
        P("fsdp", None),
        P(),
        P("fsdp", None),
        P("fsdp", None),
        P("fsdp", None),
    )
    out_specs = (
        P(("dp", "fsdp"), "ctx", None),
        P(("dp", "fsdp"), "ctx", None),
        P(),
        P("fsdp", None),
        P("fsdp", None),
        P("fsdp", None),
        P(),
        P(),
        P("fsdp", None),
        P(),
        P("fsdp", None),
        P("fsdp", None),
        P("fsdp", None),
    )
    return jax.shard_map(body, mesh=mesh, in_specs=in_specs, out_specs=out_specs, check_vma=False)
```

time: 1270 us -> 414 us (0.33)
  waiting for transfers between devices: 1020 us -> 41.6 us
  starting transfers between devices: 23 us -> 147 us
  blocking collectives: 66.4 us -> 0 us
  local copies, waits for them, and re-layouts: 30.4 us -> 90.8 us
  other arithmetic: 22.9 us -> 55.8 us
  matrix products: 95.2 us -> 64.4 us
    all_gather x13 -> x0, waiting for transfers between devices: 905 us -> none  [the longest x1 198 us: body(): lax.all_gather(ffn_right, 'fsdp', axis=0, tiled=True)]
    ppermute x0 -> x86, starting transfers between devices: none -> 121 us  [the longest x33 55 us: move_z(): lax.ppermute(value, 'ctx', [(i, (i + 2 * step) % 8) for i in range(8)])]
    psum x1 -> x0, blocking collectives: 66.4 us -> none  [body(): lax.psum((jnp.sum(attn_gain_part, axis=0), jnp.sum(query_gain_part, axis=...]
    unnamed x18 -> x0, waiting for transfers between devices: 50.4 us -> none
    psum x1 -> x0, waiting for transfers between devices: 50.2 us -> none  [body(): lax.psum(partial_value[0].astype(jnp.bfloat16), ('dp', 'ctx'))]
    ppermute x0 -> x86, waiting for transfers between devices: none -> 41.6 us  [the longest x33 29.1 us: move_z(): lax.ppermute(value, 'ctx', [(i, (i + 2 * step) % 8) for i in range(8)])]
    unnamed x107 -> x265, local copies, waits for them, and re-layouts: 12.8 us -> 41.7 us
    dot_general x20 -> x34, matrix products: 73.4 us -> 48.1 us  [the longest x13 17.1 us: mm_t(): lax.dot_general(left, right, (((1,), (1,)), ((), ())), preferred_element_...]
  transfers between devices with their start and end apart: 20 -> 90, of which waited for: 17 -> 18; matrix products, arithmetic and copies ran while one was open for 7% -> 36% of each run, Pallas kernels for 0% -> 0%
where the time goes in v1:
time: 414 us; the launch traced here: 405 us
  starting transfers between devices  147 us (36%)
  local copies, waits for them, and re-layouts  90.8 us (22%)
  matrix products  64.4 us (16%)
  other arithmetic  55.8 us (13%)
  waiting for transfers between devices  41.6 us (10%)
  between operations  5.57 us (1%)
    ppermute x33, starting transfers between devices, move_z(): lax.ppermute(value, 'ctx', [(i, (i + 2 * step) % 8) for i in range(8)])  55 us
    unnamed x265, local copies, waits for them, and re-layouts  41.7 us
    ppermute x41, starting transfers between devices, swap_core(): return lax.ppermute(value, 'ctx', [(i, i ^ 1) for i in range(8)])  35.7 us
    ppermute x33, waiting for transfers between devices, move_z(): lax.ppermute(value, 'ctx', [(i, (i + 2 * step) % 8) for i in range(8)])  29.1 us
    ppermute x6, starting transfers between devices, transpose_mesh(): return lax.ppermute(value, ('dp', 'ctx', 'fsdp'), pairs)  21.3 us
    dot_general x13, matrix products, mm_t(): lax.dot_general(left, right, (((1,), (1,)), ((), ())), preferred_element_...  17.1 us
    dot_general x16, matrix products, mm(): return jnp.dot(left, right, preferred_element_type=F32)  16.5 us
    all_to_all x2, starting transfers between devices, sum_fsdp_rows(): lax.all_to_all(partial.astype(BF16), 'fsdp', split_axis=0, concat_axis=0,...  14.1 us
  transfers between devices with their start and end apart: 90, of which 18 were waited for; matrix products, arithmetic and copies ran while one was open for 36% of the time, Pallas kernels for 0%

profile of v1, /device:TPU:1, one launch (start us, length us, event | category | flops | bytes accessed | tf_op | source)
XLA Modules:
  0.0 405.5 jit_solution(7233251063293624698)
XLA Ops:
  3.8 4.4 %collective-permute-start.5 = (bf16[128,1024]{1,0:T(8,128)(2,1)}, bf16[128,1024]{1,0:T(8,128)(2,1)S(1)}, u32[]{:S(2)}, u32[]{:S(2)}) collective-permute-start(bf16[128,1024]{1,0:T(8,128)(2,1)} %get-tuple-element.93), channel_id=1, source_target_pairs={{0,32},{8,40},{16,48},{24,56},{32,0},{40,8},{48,16},{56,24},{1,33}... | collective-permute-start | bytes 786440 | tf_op jit(solution)/shard_map/ppermute | solution.py:66
  11.2 4.5 %collective-permute-start.16 = (bf16[128,576]{0,1:T(8,128)(2,1)S(1)}, bf16[128,576]{0,1:T(8,128)(2,1)S(1)}, u32[]{:S(2)}, u32[]{:S(2)}) collective-permute-start(bf16[128,576]{0,1:T(8,128)(2,1)S(1)} %dynamic-slice_bitcast_fusion), channel_id=1, source_target_pairs={{0,0},{1,8},{2,16},{3,24},{4,32},{5,40},{6,48},{7,56},{8,1},{9,9},... | collective-permute-start | bytes 442376 | tf_op jit(solution)/shard_map/ppermute | solution.py:95
  18.3 5.1 %all-to-all-start = ((bf16[8,128,256]{2,1,0:T(8,128)(2,1)}), bf16[8,128,256]{2,1,0:T(8,128)(2,1)S(1)}, u32[]{:S(2)}, u32[]{:S(2)}) async-start(bf16[8,128,256]{2,1,0:T(8,128)(2,1)} %broadcast_in_dim.20), calls=%async_computation | async-start | bytes 1048576 | tf_op jit(solution)/shard_map/all_to_all | solution.py:108
  32.5 5.7 %collective-permute-start.7 = (bf16[128,1024]{1,0:T(8,128)(2,1)}, bf16[128,1024]{1,0:T(8,128)(2,1)S(1)}, u32[]{:S(2)}, u32[]{:S(2)}) collective-permute-start(bf16[128,1024]{1,0:T(8,128)(2,1)} %param.39), channel_id=1, source_target_pairs={{0,0},{1,8},{2,16},{3,24},{4,32},{5,40},{6,48},{7,56},{8,1},{9,9},... | collective-permute-start | bytes 786440 | tf_op jit(solution)/shard_map/ppermute | solution.py:95
  42.7 6.7 %all-to-all-start.1 = ((bf16[8,128,1728]{1,2,0:T(8,128)(2,1)}), bf16[8,128,1728]{1,2,0:T(8,128)(2,1)}, u32[]{:S(2)}, u32[]{:S(2)}) async-start(bf16[8,128,1728]{1,2,0:T(8,128)(2,1)} %broadcast_in_dim.27), calls=%async_computation.1 | async-start | bytes 7077888 | tf_op jit(solution)/shard_map/all_to_all | solution.py:108
  56.3 3.0 collective-permute-start.40
  62.7 3.1 fusion.147
  68.5 8.0 %fusion.200 = (f32[2,1024]{1,0:T(2,128)S(1)}, f32[2,1024,1024]{1,2,0:T(8,128)}) fusion(pred[1024,1024]{0,1:T(8,128)(4,1)} %broadcast_compare_fusion, bf16[1024,2,32]{0,2,1:T(8,128)(2,1)} %get-tuple-element.135, bf16[1024,2,32]{0,2,1:T(8,128)(2,1)} %get-tuple-element.134, bf16[1024,32]{1,0:T(8,128)(2,1)} %get-tuple-element.139, ...), kind=kOutput, calls=%fused_computation.447 | convolution fusion | flops 277611520 | bytes 9838592 | tf_op jit(solution)/shard_map/sub | solution.py:221
  76.5 4.3 %fusion.29 = bf16[64,2,1024]{2,0,1:T(8,128)(2,1)S(1)} fusion(f32[1024,256]{1,0:T(8,128)S(1)} %pad_maximum_fusion.1, f32[2,1024,1024]{1,2,0:T(8,128)} %get-tuple-element.228, f32[2,1024]{1,0:T(2,128)S(1)} %get-tuple-element.227), kind=kOutput, calls=%fused_computation.44 | convolution fusion | flops 272760832 | bytes 8921088 | tf_op jit(solution)/shard_map/gtl,ld->tgd/dot_general | solution.py:225
  100.7 2.9 collective-permute-done.10
  115.0 6.0 %collective-permute-done.22 = bf16[128,1024]{1,0:T(8,128)(2,1)S(1)} collective-permute-done((bf16[128,1024]{1,0:T(8,128)(2,1)S(1)}, bf16[128,1024]{1,0:T(8,128)(2,1)S(1)}, u32[]{:S(2)}, u32[]{:S(2)}) %collective-permute-start.22) | collective-permute-done | bytes 262176 | tf_op jit(solution)/shard_map/ppermute | solution.py:66
  156.6 3.7 fusion.137
  165.0 4.6 %convolution_convert_fusion = bf16[1024,1152]{1,0:T(8,128)(2,1)S(1)} fusion(bf16[1024,1024]{1,0:T(8,128)(2,1)} %constant_dynamic-update-slice_fusion.14, bf16[256,1152]{1,0:T(8,128)(2,1)S(1)} %pad_maximum_fusion.5, bf16[256,1152]{1,0:T(8,128)(2,1)S(1)} %pad_maximum_fusion.3, bf16[256,1152]{1,0:T(8,128)(2,1)S(1)} %pad_maximum_fusion.4, ...), kind=kOutput, calls=%fused_computation.14 | convolution fusion | flops 2426535936 | bytes 6815744 | tf_op jit(solution)/shard_map/dot_general | solution.py:58
  175.3 5.9 %copy.213 = bf16[8,128,1728]{1,2,0:T(8,128)(2,1)} copy(bf16[8,128,1728]{2,1,0:T(8,128)(2,1)} %bitcast.243) | data formatting | bytes 7077888 | tf_op jit(solution)/shard_map/all_to_all | solution.py:112
  181.3 6.8 %all-to-all-start.2 = ((bf16[8,128,1728]{1,2,0:T(8,128)(2,1)}), bf16[8,128,1728]{1,2,0:T(8,128)(2,1)}, u32[]{:S(2)}, u32[]{:S(2)}) async-start(bf16[8,128,1728]{1,2,0:T(8,128)(2,1)} %copy.213), calls=%async_computation.2 | async-start | bytes 7077888 | tf_op jit(solution)/shard_map/all_to_all | solution.py:112
  205.9 6.7 %collective-permute-done.35 = bf16[128,1024]{1,0:T(8,128)(2,1)S(1)} collective-permute-done((bf16[128,1024]{1,0:T(8,128)(2,1)S(1)}, bf16[128,1024]{1,0:T(8,128)(2,1)S(1)}, u32[]{:S(2)}, u32[]{:S(2)}) %collective-permute-start.35) | collective-permute-done | bytes 262176 | tf_op jit(solution)/shard_map/ppermute | solution.py:66
  223.2 6.5 %collective-permute-start.46 = (bf16[128,1024]{1,0:T(8,128)(2,1)S(1)}, bf16[128,1024]{1,0:T(8,128)(2,1)S(1)}, u32[]{:S(2)}, u32[]{:S(2)}) collective-permute-start(bf16[128,1024]{1,0:T(8,128)(2,1)S(1)} %collective-permute-done.45), channel_id=1, source_target_pairs={{0,8},{8,0},{16,24},{24,16},{32,40},{40,32},{48,56},{56,48},{1,9},... | collective-permute-start | bytes 786440 | tf_op jit(solution)/shard_map/ppermute | solution.py:62
  236.1 3.8 fusion.3
  243.7 3.3 fusion.28
  254.5 3.4 fusion.27
  278.2 7.2 %all-to-all-start.3 = ((bf16[8,128,384]{1,2,0:T(8,128)(2,1)}), bf16[8,128,384]{1,2,0:T(8,128)(2,1)}, u32[]{:S(2)}, u32[]{:S(2)}) async-start(bf16[8,128,384]{1,2,0:T(8,128)(2,1)} %copy_bitcast_fusion.1), calls=%async_computation.3 | async-start | bytes 1572864 | tf_op jit(solution)/shard_map/all_to_all | solution.py:112
  288.1 5.5 %collective-permute-start.78 = (bf16[128,576]{1,0:T(8,128)(2,1)}, bf16[128,576]{1,0:T(8,128)(2,1)}, u32[]{:S(2)}, u32[]{:S(2)}) collective-permute-start(bf16[128,576]{1,0:T(8,128)(2,1)} %slice.524), channel_id=1, source_target_pairs={{0,64},{1,72},{2,80},{3,88},{4,96},{5,104},{6,112},{7,120},{8,65},... | collective-permute-start | bytes 442376 | tf_op jit(solution)/shard_map/ppermute | solution.py:95
  300.1 3.7 collective-permute-done.77
  304.9 9.9 %collective-permute-start.61 = (f32[1,2176]{1,0:T(1,128)S(1)}, f32[1,2176]{1,0:T(1,128)S(1)}, u32[]{:S(2)}, u32[]{:S(2)}) collective-permute-start(f32[1,2176]{1,0:T(1,128)S(1)} %reshape_add_fusion), channel_id=1, source_target_pairs={{0,32},{8,40},{16,48},{24,56},{32,0},{40,8},{48,16},{56,24},{1,33}... | collective-permute-start | bytes 26120 | tf_op jit(solution)/shard_map/ppermute | solution.py:66
  323.4 3.8 collective-permute-start.63
  332.7 6.9 %collective-permute-start.79 = (bf16[128,1728]{1,0:T(8,128)(2,1)}, bf16[128,1728]{1,0:T(8,128)(2,1)}, u32[]{:S(2)}, u32[]{:S(2)}) collective-permute-start(bf16[128,1728]{1,0:T(8,128)(2,1)} %pad_maximum_fusion.10), channel_id=1, source_target_pairs={{0,8},{8,0},{16,24},{24,16},{32,40},{40,32},{48,56},{56,48},{1,9},... | collective-permute-start | bytes 1327112 | tf_op jit(solution)/shard_map/ppermute | solution.py:62
  339.6 3.5 collective-permute-start.65
  347.4 3.7 collective-permute-start.67
  352.0 5.3 %collective-permute-start.84 = (bf16[128,1728]{1,0:T(8,128)(2,1)}, bf16[128,1728]{1,0:T(8,128)(2,1)S(1)}, u32[]{:S(2)}, u32[]{:S(2)}) collective-permute-start(bf16[128,1728]{1,0:T(8,128)(2,1)} %pad_maximum_fusion.10), channel_id=1, source_target_pairs={{0,32},{8,40},{16,48},{24,56},{32,0},{40,8},{48,16},{56,24},{1,33}... | collective-permute-start | bytes 1327112 | tf_op jit(solution)/shard_map/ppermute | solution.py:66
  361.6 4.8 %collective-permute-start.72 = (bf16[128,384]{0,1:T(8,128)(2,1)S(1)}, bf16[128,384]{0,1:T(8,128)(2,1)S(1)}, u32[]{:S(2)}, u32[]{:S(2)}) collective-permute-start(bf16[128,384]{0,1:T(8,128)(2,1)S(1)} %pad_maximum_fusion.13), channel_id=1, source_target_pairs={{0,48},{8,56},{16,0},{24,8},{32,16},{40,24},{48,32},{56,40},{1,49}... | collective-permute-start | bytes 294920 | tf_op jit(solution)/shard_map/ppermute | solution.py:66
  366.7 5.1 %collective-permute-done.70 = bf16[128,384]{0,1:T(8,128)(2,1)S(1)} collective-permute-done((bf16[128,384]{0,1:T(8,128)(2,1)S(1)}, bf16[128,384]{0,1:T(8,128)(2,1)S(1)}, u32[]{:S(2)}, u32[]{:S(2)}) %collective-permute-start.70) | collective-permute-done | bytes 98336 | tf_op jit(solution)/shard_map/ppermute | solution.py:66
  389.2 3.0 constant_dynamic-slice_fusion.7
  (597 shorter events, 238.9 us)
Async XLA Ops:
  3.8 34.5 %collective-permute-start.5 = (bf16[128,1024]{1,0:T(8,128)(2,1)}, bf16[128,1024]{1,0:T(8,128)(2,1)S(1)}, u32[]{:S(2)}, u32[]{:S(2)}) collective-permute-start(bf16[128,1024]{1,0:T(8,128)(2,1)} %get-tuple-element.93), channel_id=1, source_target_pairs={{0,32},{8,40},{16,48},{24,56},{32,0},{40,8},{48,16},{56,24},{1,33}... | collective-permute-start | bytes 786440 | tf_op jit(solution)/shard_map/ppermute | solution.py:66
  8.2 30.2 %collective-permute-start.3 = (bf16[128,1024]{1,0:T(8,128)(2,1)}, bf16[128,1024]{1,0:T(8,128)(2,1)S(1)}, u32[]{:S(2)}, u32[]{:S(2)}) collective-permute-start(bf16[128,1024]{1,0:T(8,128)(2,1)} %get-tuple-element.93), channel_id=1, source_target_pairs={{0,48},{8,56},{16,0},{24,8},{32,16},{40,24},{48,32},{56,40},{1,49}... | collective-permute-start | bytes 786440 | tf_op jit(solution)/shard_map/ppermute | solution.py:66
  8.6 30.2 %collective-permute-start.1 = (bf16[128,1024]{1,0:T(8,128)(2,1)}, bf16[128,1024]{1,0:T(8,128)(2,1)S(1)}, u32[]{:S(2)}, u32[]{:S(2)}) collective-permute-start(bf16[128,1024]{1,0:T(8,128)(2,1)} %get-tuple-element.93), channel_id=1, source_target_pairs={{0,16},{8,24},{16,32},{24,40},{32,48},{40,56},{48,0},{56,8},{1,17}... | collective-permute-start | bytes 786440 | tf_op jit(solution)/shard_map/ppermute | solution.py:66
  9.6 29.3 %collective-permute-start = (bf16[128,1024]{1,0:T(8,128)(2,1)}, bf16[128,1024]{1,0:T(8,128)(2,1)S(1)}, u32[]{:S(2)}, u32[]{:S(2)}) collective-permute-start(bf16[128,1024]{1,0:T(8,128)(2,1)} %get-tuple-element.93), channel_id=1, source_target_pairs={{0,8},{8,0},{16,24},{24,16},{32,40},{40,32},{48,56},{56,48},{1,9},... | collective-permute-start | bytes 786440 | tf_op jit(solution)/shard_map/ppermute | solution.py:62
  11.2 21.3 %collective-permute-start.16 = (bf16[128,576]{0,1:T(8,128)(2,1)S(1)}, bf16[128,576]{0,1:T(8,128)(2,1)S(1)}, u32[]{:S(2)}, u32[]{:S(2)}) collective-permute-start(bf16[128,576]{0,1:T(8,128)(2,1)S(1)} %dynamic-slice_bitcast_fusion), channel_id=1, source_target_pairs={{0,0},{1,8},{2,16},{3,24},{4,32},{5,40},{6,48},{7,56},{8,1},{9,9},... | collective-permute-start | bytes 442376 | tf_op jit(solution)/shard_map/ppermute | solution.py:95
  18.3 22.1 %all-to-all-start = ((bf16[8,128,256]{2,1,0:T(8,128)(2,1)}), bf16[8,128,256]{2,1,0:T(8,128)(2,1)S(1)}, u32[]{:S(2)}, u32[]{:S(2)}) async-start(bf16[8,128,256]{2,1,0:T(8,128)(2,1)} %broadcast_in_dim.20), calls=%async_computation | async-start | bytes 1048576 | tf_op jit(solution)/shard_map/all_to_all | solution.py:108
  32.5 48.4 %collective-permute-start.7 = (bf16[128,1024]{1,0:T(8,128)(2,1)}, bf16[128,1024]{1,0:T(8,128)(2,1)S(1)}, u32[]{:S(2)}, u32[]{:S(2)}) collective-permute-start(bf16[128,1024]{1,0:T(8,128)(2,1)} %param.39), channel_id=1, source_target_pairs={{0,0},{1,8},{2,16},{3,24},{4,32},{5,40},{6,48},{7,56},{8,1},{9,9},... | collective-permute-start | bytes 786440 | tf_op jit(solution)/shard_map/ppermute | solution.py:95
  42.7 87.5 %all-to-all-start.1 = ((bf16[8,128,1728]{1,2,0:T(8,128)(2,1)}), bf16[8,128,1728]{1,2,0:T(8,128)(2,1)}, u32[]{:S(2)}, u32[]{:S(2)}) async-start(bf16[8,128,1728]{1,2,0:T(8,128)(2,1)} %broadcast_in_dim.27), calls=%async_computation.1 | async-start | bytes 7077888 | tf_op jit(solution)/shard_map/all_to_all | solution.py:108
  56.3 31.6 %collective-permute-start.40 = (bf16[128,1024]{1,0:T(8,128)(2,1)S(1)}, bf16[128,1024]{1,0:T(8,128)(2,1)}, u32[]{:S(2)}, u32[]{:S(2)}) collective-permute-start(bf16[128,1024]{1,0:T(8,128)(2,1)S(1)} %bitcast.246), channel_id=1, source_target_pairs={{0,32},{8,40},{16,48},{24,56},{32,0},{40,8},{48,16},{56,24},{1,33}... | collective-permute-start | bytes 786440 | tf_op jit(solution)/shard_map/ppermute | solution.py:66
  59.3 28.7 %collective-permute-start.36 = (bf16[128,1024]{1,0:T(8,128)(2,1)S(1)}, bf16[128,1024]{1,0:T(8,128)(2,1)}, u32[]{:S(2)}, u32[]{:S(2)}) collective-permute-start(bf16[128,1024]{1,0:T(8,128)(2,1)S(1)} %bitcast.247), channel_id=1, source_target_pairs={{0,16},{8,24},{16,32},{24,40},{32,48},{40,56},{48,0},{56,8},{1,17}... | collective-permute-start | bytes 786440 | tf_op jit(solution)/shard_map/ppermute | solution.py:66
  59.3 35.7 %collective-permute-start.32 = (bf16[128,1024]{1,0:T(8,128)(2,1)S(1)}, bf16[128,1024]{1,0:T(8,128)(2,1)}, u32[]{:S(2)}, u32[]{:S(2)}) collective-permute-start(bf16[128,1024]{1,0:T(8,128)(2,1)S(1)} %bitcast.248), channel_id=1, source_target_pairs={{0,48},{8,56},{16,0},{24,8},{32,16},{40,24},{48,32},{56,40},{1,49}... | collective-permute-start | bytes 786440 | tf_op jit(solution)/shard_map/ppermute | solution.py:66
  95.5 26.2 %collective-permute-start.41 = (bf16[128,1024]{1,0:T(8,128)(2,1)}, bf16[128,1024]{1,0:T(8,128)(2,1)S(1)}, u32[]{:S(2)}, u32[]{:S(2)}) collective-permute-start(bf16[128,1024]{1,0:T(8,128)(2,1)} %collective-permute-done.40), channel_id=1, source_target_pairs={{0,8},{8,0},{16,24},{24,16},{32,40},{40,32},{48,56},{56,48},{1,9},... | collective-permute-start | bytes 786440 | tf_op jit(solution)/shard_map/ppermute | solution.py:62
  106.2 17.0 %collective-permute-start.26 = (bf16[128,1024]{1,0:T(8,128)(2,1)S(1)}, bf16[128,1024]{1,0:T(8,128)(2,1)S(1)}, u32[]{:S(2)}, u32[]{:S(2)}) collective-permute-start(bf16[128,1024]{1,0:T(8,128)(2,1)S(1)} %get-tuple-element.96), channel_id=1, source_target_pairs={{0,32},{8,40},{16,48},{24,56},{32,0},{40,8},{48,16},{56,24},{1,33}... | collective-permute-start | bytes 786440 | tf_op jit(solution)/shard_map/ppermute | solution.py:66
  106.8 16.9 %collective-permute-start.18 = (bf16[128,1024]{1,0:T(8,128)(2,1)S(1)}, bf16[128,1024]{1,0:T(8,128)(2,1)S(1)}, u32[]{:S(2)}, u32[]{:S(2)}) collective-permute-start(bf16[128,1024]{1,0:T(8,128)(2,1)S(1)} %get-tuple-element.96), channel_id=1, source_target_pairs={{0,48},{8,56},{16,0},{24,8},{32,16},{40,24},{48,32},{56,40},{1,49}... | collective-permute-start | bytes 786440 | tf_op jit(solution)/shard_map/ppermute | solution.py:66
  170.3 25.1 %collective-permute-start.38 = (bf16[128,1024]{1,0:T(8,128)(2,1)}, bf16[128,1024]{1,0:T(8,128)(2,1)}, u32[]{:S(2)}, u32[]{:S(2)}) collective-permute-start(bf16[128,1024]{1,0:T(8,128)(2,1)} %slice.936), channel_id=1, source_target_pairs={{0,8},{8,0},{16,24},{24,16},{32,40},{40,32},{48,56},{56,48},{1,9},... | collective-permute-start | bytes 786440 | tf_op jit(solution)/shard_map/ppermute | solution.py:62
  171.1 26.1 %collective-permute-start.34 = (bf16[128,1024]{1,0:T(8,128)(2,1)}, bf16[128,1024]{1,0:T(8,128)(2,1)}, u32[]{:S(2)}, u32[]{:S(2)}) collective-permute-start(bf16[128,1024]{1,0:T(8,128)(2,1)} %slice.937), channel_id=1, source_target_pairs={{0,8},{8,0},{16,24},{24,16},{32,40},{40,32},{48,56},{56,48},{1,9},... | collective-permute-start | bytes 786440 | tf_op jit(solution)/shard_map/ppermute | solution.py:62
  181.3 81.1 %all-to-all-start.2 = ((bf16[8,128,1728]{1,2,0:T(8,128)(2,1)}), bf16[8,128,1728]{1,2,0:T(8,128)(2,1)}, u32[]{:S(2)}, u32[]{:S(2)}) async-start(bf16[8,128,1728]{1,2,0:T(8,128)(2,1)} %copy.213), calls=%async_computation.2 | async-start | bytes 7077888 | tf_op jit(solution)/shard_map/all_to_all | solution.py:112
  192.2 22.0 %collective-permute-start.24 = (bf16[128,1024]{1,0:T(8,128)(2,1)S(1)}, bf16[128,1024]{1,0:T(8,128)(2,1)S(1)}, u32[]{:S(2)}, u32[]{:S(2)}) collective-permute-start(bf16[128,1024]{1,0:T(8,128)(2,1)S(1)} %slice.940), channel_id=1, source_target_pairs={{0,8},{8,0},{16,24},{24,16},{32,40},{40,32},{48,56},{56,48},{1,9},... | collective-permute-start | bytes 786440 | tf_op jit(solution)/shard_map/ppermute | solution.py:62
  204.3 16.7 %collective-permute-start.28 = (bf16[128,1024]{1,0:T(8,128)(2,1)S(1)}, bf16[128,1024]{1,0:T(8,128)(2,1)S(1)}, u32[]{:S(2)}, u32[]{:S(2)}) collective-permute-start(bf16[128,1024]{1,0:T(8,128)(2,1)S(1)} %slice.939), channel_id=1, source_target_pairs={{0,8},{8,0},{16,24},{24,16},{32,40},{40,32},{48,56},{56,48},{1,9},... | collective-permute-start | bytes 786440 | tf_op jit(solution)/shard_map/ppermute | solution.py:62
  221.0 110.7 %collective-permute-start.17 = (bf16[128,1024]{1,0:T(8,128)(2,1)}, bf16[128,1024]{1,0:T(8,128)(2,1)}, u32[]{:S(2)}, u32[]{:S(2)}) collective-permute-start(bf16[128,1024]{1,0:T(8,128)(2,1)} %slice.942), channel_id=1, source_target_pairs={{0,8},{8,0},{16,24},{24,16},{32,40},{40,32},{48,56},{56,48},{1,9},... | collective-permute-start | bytes 786440 | tf_op jit(solution)/shard_map/ppermute | solution.py:62
  270.6 17.5 %collective-permute-start.57 = (bf16[128,1024]{1,0:T(8,128)(2,1)}, bf16[128,1024]{1,0:T(8,128)(2,1)}, u32[]{:S(2)}, u32[]{:S(2)}) collective-permute-start(bf16[128,1024]{1,0:T(8,128)(2,1)} %fusion.73), channel_id=1, source_target_pairs={{0,32},{8,40},{16,48},{24,56},{32,0},{40,8},{48,16},{56,24},{1,33}... | collective-permute-start | bytes 786440 | tf_op jit(solution)/shard_map/ppermute | solution.py:66
  272.3 21.2 %collective-permute-start.55 = (bf16[128,1024]{1,0:T(8,128)(2,1)}, bf16[128,1024]{1,0:T(8,128)(2,1)}, u32[]{:S(2)}, u32[]{:S(2)}) collective-permute-start(bf16[128,1024]{1,0:T(8,128)(2,1)} %fusion.74), channel_id=1, source_target_pairs={{0,48},{8,56},{16,0},{24,8},{32,16},{40,24},{48,32},{56,40},{1,49}... | collective-permute-start | bytes 786440 | tf_op jit(solution)/shard_map/ppermute | solution.py:66
  274.8 20.6 %collective-permute-start.53 = (bf16[128,1024]{1,0:T(8,128)(2,1)}, bf16[128,1024]{1,0:T(8,128)(2,1)}, u32[]{:S(2)}, u32[]{:S(2)}) collective-permute-start(bf16[128,1024]{1,0:T(8,128)(2,1)} %fusion.75), channel_id=1, source_target_pairs={{0,16},{8,24},{16,32},{24,40},{32,48},{40,56},{48,0},{56,8},{1,17}... | collective-permute-start | bytes 786440 | tf_op jit(solution)/shard_map/ppermute | solution.py:66
  278.2 67.9 %all-to-all-start.3 = ((bf16[8,128,384]{1,2,0:T(8,128)(2,1)}), bf16[8,128,384]{1,2,0:T(8,128)(2,1)}, u32[]{:S(2)}, u32[]{:S(2)}) async-start(bf16[8,128,384]{1,2,0:T(8,128)(2,1)} %copy_bitcast_fusion.1), calls=%async_computation.3 | async-start | bytes 1572864 | tf_op jit(solution)/shard_map/all_to_all | solution.py:112
  285.4 47.3 %collective-permute-start.25 = (bf16[128,1024]{1,0:T(8,128)(2,1)}, bf16[128,1024]{1,0:T(8,128)(2,1)}, u32[]{:S(2)}, u32[]{:S(2)}) collective-permute-start(bf16[128,1024]{1,0:T(8,128)(2,1)} %fusion.86), channel_id=1, source_target_pairs={{0,48},{8,56},{16,0},{24,8},{32,16},{40,24},{48,32},{56,40},{1,49}... | collective-permute-start | bytes 786440 | tf_op jit(solution)/shard_map/ppermute | solution.py:66
  295.5 19.3 %collective-permute-start.76 = (bf16[128,1152]{1,0:T(8,128)(2,1)}, bf16[128,1152]{1,0:T(8,128)(2,1)S(1)}, u32[]{:S(2)}, u32[]{:S(2)}) collective-permute-start(bf16[128,1152]{1,0:T(8,128)(2,1)} %slice.523), channel_id=1, source_target_pairs={{0,64},{64,0},{1,65},{65,1},{2,66},{66,2},{3,67},{67,3},{4,68},{68... | collective-permute-start | bytes 884744 | tf_op jit(solution)/shard_map/ppermute | solution.py:99
  318.0 21.6 %collective-permute-start.21 = (bf16[128,1024]{1,0:T(8,128)(2,1)}, bf16[128,1024]{1,0:T(8,128)(2,1)S(1)}, u32[]{:S(2)}, u32[]{:S(2)}) collective-permute-start(bf16[128,1024]{1,0:T(8,128)(2,1)} %fusion.87), channel_id=1, source_target_pairs={{0,16},{8,24},{16,32},{24,40},{32,48},{40,56},{48,0},{56,8},{1,17}... | collective-permute-start | bytes 786440 | tf_op jit(solution)/shard_map/ppermute | solution.py:66
  318.1 25.1 %collective-permute-start.29 = (bf16[128,1024]{1,0:T(8,128)(2,1)}, bf16[128,1024]{1,0:T(8,128)(2,1)S(1)}, u32[]{:S(2)}, u32[]{:S(2)}) collective-permute-start(bf16[128,1024]{1,0:T(8,128)(2,1)} %fusion.85), channel_id=1, source_target_pairs={{0,32},{8,40},{16,48},{24,56},{32,0},{40,8},{48,16},{56,24},{1,33}... | collective-permute-start | bytes 786440 | tf_op jit(solution)/shard_map/ppermute | solution.py:66
  331.1 44.2 %collective-permute-start.82 = (bf16[128,1728]{1,0:T(8,128)(2,1)}, bf16[128,1728]{1,0:T(8,128)(2,1)S(1)}, u32[]{:S(2)}, u32[]{:S(2)}) collective-permute-start(bf16[128,1728]{1,0:T(8,128)(2,1)} %pad_maximum_fusion.10), channel_id=1, source_target_pairs={{0,48},{8,56},{16,0},{24,8},{32,16},{40,24},{48,32},{56,40},{1,49}... | collective-permute-start | bytes 1327112 | tf_op jit(solution)/shard_map/ppermute | solution.py:66
  331.8 28.0 %collective-permute-start.80 = (bf16[128,1728]{1,0:T(8,128)(2,1)}, bf16[128,1728]{1,0:T(8,128)(2,1)}, u32[]{:S(2)}, u32[]{:S(2)}) collective-permute-start(bf16[128,1728]{1,0:T(8,128)(2,1)} %pad_maximum_fusion.10), channel_id=1, source_target_pairs={{0,16},{8,24},{16,32},{24,40},{32,48},{40,56},{48,0},{56,8},{1,17}... | collective-permute-start | bytes 1327112 | tf_op jit(solution)/shard_map/ppermute | solution.py:66
  332.7 25.2 %collective-permute-start.79 = (bf16[128,1728]{1,0:T(8,128)(2,1)}, bf16[128,1728]{1,0:T(8,128)(2,1)}, u32[]{:S(2)}, u32[]{:S(2)}) collective-permute-start(bf16[128,1728]{1,0:T(8,128)(2,1)} %pad_maximum_fusion.10), channel_id=1, source_target_pairs={{0,8},{8,0},{16,24},{24,16},{32,40},{40,32},{48,56},{56,48},{1,9},... | collective-permute-start | bytes 1327112 | tf_op jit(solution)/shard_map/ppermute | solution.py:62
  352.0 23.5 %collective-permute-start.84 = (bf16[128,1728]{1,0:T(8,128)(2,1)}, bf16[128,1728]{1,0:T(8,128)(2,1)S(1)}, u32[]{:S(2)}, u32[]{:S(2)}) collective-permute-start(bf16[128,1728]{1,0:T(8,128)(2,1)} %pad_maximum_fusion.10), channel_id=1, source_target_pairs={{0,32},{8,40},{16,48},{24,56},{32,0},{40,8},{48,16},{56,24},{1,33}... | collective-permute-start | bytes 1327112 | tf_op jit(solution)/shard_map/ppermute | solution.py:66
  (158 other events, 1398.3 us)

commit v2 on v1

v2 whole, which is shorter than its diff:
```python
import math

import jax
import jax.numpy as jnp
from jax import lax
from jax.experimental import pallas as pl
from jax.experimental.pallas import tpu as pltpu
from jax.sharding import PartitionSpec as P

NORM_EPSILON = 1e-05
ROPE_BASE = 1000000.0
MASKED_SCORE = -1e30
BF16 = jnp.bfloat16
F32 = jnp.float32
STEPS = (0, -1, 1, 2)
Y_STEPS = (1, 3, 2, 0)


def rms_scale(values):
    return lax.rsqrt(jnp.mean(values * values, axis=-1, keepdims=True) + NORM_EPSILON)


def rope_tables(places, head_size):
    half_width = head_size // 2
    pair_index = jnp.arange(half_width, dtype=F32)
    frequency = ROPE_BASE ** (-2.0 * pair_index / head_size)
    angles = frequency[:, None] * places.astype(F32)[None, :]
    return jnp.cos(angles), jnp.sin(angles)


def call(kernel, out_shapes, args, flops, scratch=(), scalars=0):
    vmem = pl.BlockSpec(memory_space=pltpu.VMEM)
    smem = pl.BlockSpec(memory_space=pltpu.SMEM)
    out_bytes = sum(math.prod(o.shape) * o.dtype.itemsize for o in out_shapes)
    in_bytes = sum(math.prod(a.shape) * a.dtype.itemsize for a in args)
    return pl.pallas_call(
        kernel,
        out_shape=out_shapes,
        in_specs=[smem] * scalars + [vmem] * (len(args) - scalars),
        out_specs=[vmem] * len(out_shapes),
        scratch_shapes=list(scratch),
        compiler_params=pltpu.CompilerParams(vmem_limit_bytes=40 * 2**20),
        cost_estimate=pl.CostEstimate(flops=flops, bytes_accessed=in_bytes + out_bytes, transcendentals=0),
    )(*args)


def shape(dims, kind):
    return jax.ShapeDtypeStruct(dims, kind)


def head_forward(values, gain, cosine, sine):
    scale = lax.rsqrt(jnp.mean(values * values, axis=0, keepdims=True) + NORM_EPSILON)
    hat = values * scale
    normed = hat * gain
    half = values.shape[0] // 2
    front, back = normed[:half], normed[half:]
    rotated = jnp.concatenate([front * cosine - back * sine, back * cosine + front * sine], axis=0)
    return scale, hat, rotated


def head_backward(grads, hat, scale, gain, cosine, sine):
    half = grads.shape[0] // 2
    front, back = grads[:half], grads[half:]
    d_normed = jnp.concatenate([front * cosine + back * sine, back * cosine - front * sine], axis=0)
    scaled = d_normed * gain
    inner = jnp.mean(hat * scaled, axis=0, keepdims=True)
    return scale * (scaled - hat * inner), jnp.sum(d_normed * hat, axis=1, keepdims=True)


def attend_forward(*refs):
    pieces, refs = refs[:8], refs[8:]
    w_qkv, out_rows, cos_ref, sin_ref, column_ref, row_ref, q_gain, k_gain = refs[:8]
    mixed_ref, qkv_ref, lse_ref, send_ref, *mine_refs = refs[8:]
    length = qkv_ref.shape[1]
    head = q_gain.shape[0]
    for pair in range(4):
        x = jnp.concatenate([pieces[2 * pair][...], pieces[2 * pair + 1][...]], axis=0)
        qkv_ref[:, pair * 256 : (pair + 1) * 256] = jnp.transpose(mm(x, w_qkv[...]))
    cosine, sine = cos_ref[...], sin_ref[...]
    queries = [
        (head_forward(qkv_ref[h * head : (h + 1) * head], q_gain[...], cosine, sine)[2]).astype(BF16) * BF16(head**-0.5)
        for h in range(2)
    ]
    key = jnp.transpose(head_forward(qkv_ref[2 * head : 3 * head], k_gain[...], cosine, sine)[2]).astype(BF16)
    value = qkv_ref[3 * head :].astype(BF16)
    width = column_ref.shape[1]
    for tile in range(length // width):
        lanes = slice(tile * width, (tile + 1) * width)
        allowed = column_ref[...] <= row_ref[:, lanes]
        outs = []
        for h in range(2):
            scores = jnp.where(allowed, mm(key, queries[h][:, lanes]), MASKED_SCORE)
            top = jnp.max(scores, axis=0, keepdims=True)
            weights = jnp.exp(scores - top)
            total = jnp.sum(weights, axis=0, keepdims=True)
            lse_ref[h : h + 1, lanes] = top + jnp.log(total)
            outs.append(mm(value, (weights * (1.0 / total)).astype(BF16)))
        mixed = jnp.transpose(jnp.concatenate(outs, axis=0)).astype(BF16)
        mixed_ref[lanes] = mixed
        proj = mm(mixed, out_rows[...])
        mine_refs[tile][...] = proj[: width // 2]
        send_ref[tile] = proj[width // 2 :].astype(BF16)


def attend_backward(*refs):
    place, pieces, d_pieces, refs = refs[0], refs[1:9], refs[9:17], refs[17:]
    w_qkv, out_rows, cos_ref, sin_ref, column_ref, row_ref, q_gain, k_gain, mixed_ref, qkv_ref, lse_ref = refs[:11]
    q_gain_ref, k_gain_ref, attn_gain_ref, send_ref = refs[11:15]
    mine_refs, part_refs = refs[15:19], refs[19:27]
    d_attn_ref, x_ref, d_qkv_ref, grads_ref = refs[27:]
    length = qkv_ref.shape[1]
    head = q_gain.shape[0]
    count = pieces[0].shape[0]
    for i in range(8):
        d_attn_ref[i * count : (i + 1) * count] = d_pieces[i][...]
        x_ref[i * count : (i + 1) * count] = pieces[i][...]
    cosine, sine = cos_ref[...], sin_ref[...]
    scales, hats, queries = [], [], []
    for h in range(2):
        scale, hat, rotated = head_forward(qkv_ref[h * head : (h + 1) * head], q_gain[...], cosine, sine)
        scales.append(scale)
        hats.append(hat)
        queries.append(rotated.astype(BF16) * BF16(head**-0.5))
    k_scale, k_hat, rotated = head_forward(qkv_ref[2 * head : 3 * head], k_gain[...], cosine, sine)
    key_rows = rotated.astype(BF16)
    key = jnp.transpose(rotated).astype(BF16)
    value = jnp.transpose(qkv_ref[3 * head :]).astype(BF16)
    width = column_ref.shape[1]
    d_key = jnp.zeros((length, head), F32)
    d_value = jnp.zeros((length, head), F32)
    for tile in range(length // width):
        lanes = slice(tile * width, (tile + 1) * width)
        allowed = column_ref[...] <= row_ref[:, lanes]
        d_mixed = jnp.transpose(mm_t(d_attn_ref[lanes], out_rows[...])).astype(BF16)
        for h in range(2):
            rows = slice(h * head, (h + 1) * head)
            query = queries[h][:, lanes]
            probs = jnp.where(allowed, jnp.exp(mm(key, query) - lse_ref[h : h + 1, lanes]), 0.0)
            d_probs = mm(value, d_mixed[rows])
            inner = jnp.sum(probs * d_probs, axis=0, keepdims=True)
            d_scores = (probs * (d_probs - inner)).astype(BF16)
            d_value += mm_t(probs.astype(BF16), d_mixed[rows])
            d_key += mm_t(d_scores, query)
            d_qkv_ref[rows, lanes] = mm(key_rows, d_scores) * head**-0.5
    for h in range(2):
        rows = slice(h * head, (h + 1) * head)
        d_query, gain_part = head_backward(d_qkv_ref[rows], hats[h], scales[h], q_gain[...], cosine, sine)
        d_qkv_ref[rows] = d_query
        if h == 0:
            q_gain_ref[...] = gain_part
        else:
            q_gain_ref[...] += gain_part
    d_keys, gain_part = head_backward(jnp.transpose(d_key), k_hat, k_scale, k_gain[...], cosine, sine)
    k_gain_ref[...] = gain_part
    d_qkv_ref[2 * head : 3 * head] = d_keys
    d_qkv_ref[3 * head :] = jnp.transpose(d_value)
    for tile in range(4):
        lanes = slice(tile * 2 * count, (tile + 1) * 2 * count)
        d_qkv = jnp.transpose(d_qkv_ref[:, lanes]).astype(BF16)
        d_first = mm_t(d_qkv, w_qkv[...])
        mine_refs[tile][...] = d_first[:count]
        send_ref[tile] = d_first[count:].astype(BF16)
    grad_qkv = jnp.transpose(mm(d_qkv_ref[...].astype(BF16), x_ref[...]))
    attn_gain_ref[...] = jnp.sum(grad_qkv * w_qkv[...].astype(F32), axis=1, keepdims=True)
    grads_ref[:, : 4 * head] = grad_qkv.astype(BF16)
    grads_ref[:, 4 * head :] = jnp.transpose(
        lax.dot_general(mixed_ref[...], d_attn_ref[...], (((0,), (0,)), ((), ())), preferred_element_type=F32)
    ).astype(BF16)
    for i, step in enumerate(Y_STEPS):
        for flip in (0, 1):
            owner = (place[0] + step) % 4 * 2 + (place[1] ^ flip)
            part_refs[2 * i + flip][...] = grads_ref[pl.ds(pl.multiple_of(owner * count, count), count)]


def ffn_group(first, second, cot_first, cot_second, weights, hidden_ref, d_ffn_ref, d_mine, d_send, mine, send):
    width = hidden_ref.shape[1]
    count = first.shape[0]
    x = jnp.concatenate([first[...], second[...]], axis=0)
    cot = jnp.concatenate([cot_first[...], cot_second[...]], axis=0)
    both = mm(x, weights[:, : 2 * width])
    gate, up = both[:, :width], both[:, width:]
    sigmoid = 1.0 / (1.0 + jnp.exp(-gate))
    act = gate * sigmoid
    hidden = (act * up).astype(BF16)
    hidden_ref[...] = hidden
    d_hidden = mm(cot, weights[:, 2 * width :])
    d_gate = d_hidden * up * sigmoid * (1.0 + gate * (1.0 - sigmoid))
    d_ffn = jnp.concatenate([d_gate, d_hidden * act], axis=1).astype(BF16)
    d_ffn_ref[...] = d_ffn
    d_second = mm_t(d_ffn, weights[:, : 2 * width])
    d_mine[...] = d_second[:count]
    d_send[...] = d_second[count:].astype(BF16)
    out = mm_t(hidden, weights[:, 2 * width :])
    mine[...] = out[:count]
    send[...] = out[count:].astype(BF16)


def ffn_weights(*refs):
    place, seconds, cots, hiddens, d_ffns = refs[0], refs[1:9], refs[9:17], refs[17:21], refs[21:25]
    part_refs, x_ref, h_ref = refs[25:33], refs[33], refs[34]
    count = seconds[0].shape[0]
    for pieces, others, columns in ((seconds, d_ffns, 0), (cots, hiddens, d_ffns[0].shape[1])):
        for i in range(8):
            x_ref[i * count : (i + 1) * count] = pieces[i][...]
        width = others[0].shape[1]
        for i in range(4):
            h_ref[2 * i * count : 2 * (i + 1) * count, :width] = others[i][...]
        for i, step in enumerate(Y_STEPS):
            rows = pl.ds(pl.multiple_of((place[0] + step) % 4 * (2 * count), 2 * count), 2 * count)
            both = outer_sum(x_ref[:, rows], h_ref[:, :width])
            low, high = both[:count], both[count:]
            first = place[1] == 0
            part_refs[2 * i][:, columns : columns + width] = jnp.where(first, low, high).astype(BF16)
            part_refs[2 * i + 1][:, columns : columns + width] = jnp.where(first, high, low).astype(BF16)


def assemble_ffn(*refs):
    order, pieces, (gate_ref, up_ref, down_ref, held) = refs[0], refs[1:9], refs[9:]
    width = down_ref.shape[0]
    count = pieces[0].shape[0]
    for i in range(8):
        held[order[i]] = pieces[i][...]
    for owner in range(8):
        columns = slice(owner * width, (owner + 1) * width)
        gate_ref[:, columns] = held[owner, :, :width].astype(F32)
        up_ref[:, columns] = held[owner, :, width : 2 * width].astype(F32)
        down = held[owner, :, 2 * width :].astype(F32)
        down_ref[:, owner * count : (owner + 1) * count] = jnp.transpose(down)


def assemble_attn(*refs):
    order, pieces, (query_ref, key_ref, value_ref, out_ref, held) = refs[0], refs[1:9], refs[9:]
    count = pieces[0].shape[0]
    half = count // 2
    for i in range(8):
        held[order[i]] = pieces[i][...]
    for owner in range(8):
        columns = slice(owner * count, (owner + 1) * count)
        narrow = slice(owner * half, (owner + 1) * half)
        part = held[owner].astype(F32)
        query_ref[:, columns] = part[:, :count]
        key_ref[:, narrow] = part[:, count : count + half]
        value_ref[:, narrow] = part[:, count + half : 2 * count]
        out_ref[:, columns] = jnp.transpose(part[:, 2 * count :])


def norm_back(d_normed, normed_hat, scale_values, gain_vector):
    scaled = d_normed * gain_vector
    inner = jnp.mean(normed_hat * scaled, axis=-1, keepdims=True)
    return (scale_values * (scaled - normed_hat * inner), d_normed * normed_hat)


def mm(left, right):
    return jnp.dot(left, right, preferred_element_type=F32)


def mm_t(left, right):
    return lax.dot_general(left, right, (((1,), (1,)), ((), ())), preferred_element_type=F32)


def outer_sum(left, right):
    return lax.dot_general(left, right, (((0,), (0,)), ((), ())), preferred_element_type=F32)


def swap_core(value):
    return lax.ppermute(value, "ctx", [(i, i ^ 1) for i in range(8)])


def move_z(value, step):
    return lax.ppermute(value, "ctx", [(i, (i + 2 * step) % 8) for i in range(8)])


def gather_ctx(block):
    pieces = []
    for step in STEPS:
        mine = block if step == 0 else move_z(block, -step)
        pieces += [mine, swap_core(mine)]
    return pieces


def start_scatter_ctx(mine, received):
    sums = [own + other.astype(F32) for own, other in zip(mine, received)]
    return [sums[0]] + [move_z(sums[slot].astype(BF16), STEPS[slot]) for slot in (3, 1, 2)]


def end_scatter(moves):
    return sum(move.astype(F32) for move in moves)


def scatter_ctx(mine, received):
    return end_scatter(start_scatter_ctx(mine, received))


def transpose_mesh(value, flip=0):
    pairs = [
        ((d * 8 + c) * 8 + f, ((d ^ flip) * 8 + f) * 8 + c) for d in range(2) for c in range(8) for f in range(8)
    ]
    return lax.ppermute(value, ("dp", "ctx", "fsdp"), pairs)


def swap_dp(value):
    return lax.ppermute(value, "dp", [(0, 1), (1, 0)])


def after(value, *others):
    return lax.optimization_barrier((value, *others))[0]


def move_y(value, step, flip=0):
    pairs = [(y * 2 + x, (y + step) % 4 * 2 + (x ^ flip)) for y in range(4) for x in range(2)]
    return lax.ppermute(value, "fsdp", pairs)


def gather_fsdp_rows(block):
    me = lax.axis_index("fsdp")
    rows = block.shape[0]
    whole = jnp.zeros((8 * rows, block.shape[1]), block.dtype)
    for flip, held in ((0, block), (1, move_y(block, 0, 1))):
        for step in (0, 1, 3, 2):
            piece = move_y(held, step) if step else held
            owner = (me // 2 - step) % 4 * 2 + (me % 2 ^ flip)
            whole = lax.dynamic_update_slice_in_dim(whole, piece, owner * rows, 0)
    return whole


def start_sum_fsdp(pieces):
    return [
        [pieces[2 * i + flip] if step == 0 else move_y(pieces[2 * i + flip], step) for flip in (1, 0)]
        for i, step in enumerate(Y_STEPS)
    ]


def end_sum_fsdp(moved):
    other, own = (sum(pair[i].astype(F32) for pair in moved) for i in (0, 1))
    return (own + move_y(other.astype(BF16), 0, 1).astype(F32)).astype(BF16)


def sum_dp(low):
    return (low.astype(F32) + swap_dp(low).astype(F32)).astype(BF16)


def sum_dp_transposed(low):
    return (transpose_mesh(low).astype(F32) + transpose_mesh(low, 1).astype(F32)).astype(BF16)


def sum_all(value):
    total = value + swap_core(value)
    total = total + move_z(total, 1) + move_z(total, -1) + move_z(total, 2)
    total = total + move_y(total, 1) + move_y(total, 3) + move_y(total, 2)
    total = total + swap_dp(total)
    return total + move_y(total, 0, 1)


def own_columns(weight, width, index):
    return lax.dynamic_slice_in_dim(weight, index * width, width, 1)


def body(
    hidden_in,
    positions,
    cotangent,
    attn_gain,
    w_query,
    w_key,
    w_value,
    query_gain,
    key_gain,
    w_out,
    ffn_gain,
    w_gate,
    w_up,
    w_down,
):
    ctx = lax.axis_index("ctx")
    tokens = hidden_in[0].astype(F32)
    count, width = tokens.shape
    head_size = query_gain.shape[0]
    q_width = w_query.shape[1] // 8
    k_width = w_key.shape[1] // 8
    ff_width = w_gate.shape[1] // 8

    w_qkv = gather_fsdp_rows(
        jnp.concatenate(
            [own_columns(w_query, q_width, ctx), own_columns(w_key, k_width, ctx), own_columns(w_value, k_width, ctx)],
            axis=1,
        )
    )
    out_rows = transpose_mesh(w_out)
    down_chunk = transpose_mesh(jnp.transpose(own_columns(w_down, width // 8, ctx)))
    ffn_block = jnp.concatenate(
        [own_columns(w_gate, ff_width, ctx), own_columns(w_up, ff_width, ctx), down_chunk], axis=1
    )
    ffn_rows = gather_fsdp_rows(after(ffn_block, w_qkv))
    place = jnp.stack([lax.axis_index("fsdp") // 2, lax.axis_index("fsdp") % 2])

    z_index, core = ctx // 2, ctx % 2
    owners = jnp.stack(
        [((z_index + step) % 4) * 2 + (core ^ flip) for step in STEPS for flip in (0, 1)]
    )
    places = positions[0].reshape(8, count)[owners].reshape(8 * count)
    length = 8 * count
    cosine_table, sine_table = rope_tables(places, head_size)
    column = jnp.broadcast_to(places[:, None], (length, 2 * count))
    row = places[None]
    gains = (query_gain[:, None], key_gain[:, None])

    first_scale = rms_scale(tokens)
    first_hat = tokens * first_scale
    first_normed = (first_hat * attn_gain).astype(BF16)
    first_pieces = gather_ctx(first_normed)
    cot_pieces = gather_ctx(after(cotangent[0], *first_pieces))

    mixed, qkv, lse, send, *mine = call(
        attend_forward,
        [
            shape((length, q_width), BF16),
            shape((4 * head_size, length), F32),
            shape((8, length), F32),
            shape((4, count, width), BF16),
        ]
        + [shape((count, width), F32)] * 4,
        (*first_pieces, w_qkv, out_rows, cosine_table, sine_table, column, row, *gains),
        4 * 10**9,
    )
    received = swap_core(send)
    residual = tokens + scatter_ctx(mine, received)
    second_scale = rms_scale(residual)
    second_hat = residual * second_scale
    second_normed = (second_hat * ffn_gain).astype(BF16)
    second_pieces = gather_ctx(second_normed)

    hiddens, d_ffns, d_mine, d_received, mine, received = [], [], [], [], [], []
    for group in range(4):
        pair = slice(2 * group, 2 * group + 2)
        hidden, d_ffn, own, other, block_own, block_other = call(
            ffn_group,
            [
                shape((2 * count, ff_width), BF16),
                shape((2 * count, 2 * ff_width), BF16),
                shape((count, width), F32),
                shape((count, width), BF16),
                shape((count, width), F32),
                shape((count, width), BF16),
            ],
            (*second_pieces[pair], *cot_pieces[pair], ffn_rows),
            2 * 10**9,
        )
        hiddens.append(hidden)
        d_ffns.append(d_ffn)
        d_mine.append(own)
        d_received.append(swap_core(other))
        mine.append(block_own)
        received.append(block_other)
    ffn_partial = call(
        ffn_weights,
        [shape((count, 3 * ff_width), BF16)] * 8,
        (place, *second_pieces, *cot_pieces, *hiddens, *d_ffns),
        4 * 10**9,
        [pltpu.VMEM((length, width), BF16), pltpu.VMEM((length, 2 * ff_width), BF16)],
        1,
    )
    d_moves = start_scatter_ctx(d_mine, d_received)
    d_moves, ffn_partial = lax.optimization_barrier((d_moves, ffn_partial))
    d_second = end_scatter(d_moves)
    ffn_moved = start_sum_fsdp(ffn_partial)

    d_from_second, ffn_gain_part = norm_back(d_second, second_hat, second_scale, ffn_gain)
    d_resid = cotangent[0].astype(F32) + d_from_second
    d_attn = d_resid.astype(BF16)
    d_pieces = gather_ctx(d_attn)
    received = [swap_core(part) for part in after(received, *d_pieces)]
    block_moves = start_scatter_ctx(mine, received)
    d_pieces, ffn_moved = lax.optimization_barrier((d_pieces, ffn_moved))
    ffn_sum = end_sum_fsdp(ffn_moved)
    ffn_gate_up, ffn_down = ffn_sum[:, : 2 * ff_width], ffn_sum[:, 2 * ff_width :]
    ffn_steps = [ffn_gate_up, swap_dp(ffn_gate_up), transpose_mesh(ffn_down), transpose_mesh(ffn_down, 1)]

    qkv_width = q_width + 2 * k_width
    q_gain_part, k_gain_part, attn_gain_part, send, *parts = call(
        attend_backward,
        [
            shape((head_size, 1), F32),
            shape((head_size, 1), F32),
            shape((width, 1), F32),
            shape((4, count, width), BF16),
        ]
        + [shape((count, width), F32)] * 4
        + [shape((count, qkv_width + q_width), BF16)] * 8,
        (place, *first_pieces, *d_pieces, w_qkv, out_rows, cosine_table, sine_table, column, row, *gains, mixed, qkv, lse),
        8 * 10**9,
        [
            pltpu.VMEM((length, width), BF16),
            pltpu.VMEM((length, width), BF16),
            pltpu.VMEM((qkv_width, length), F32),
            pltpu.VMEM((width, qkv_width + q_width), BF16),
        ],
        1,
    )
    mine, attn_partial = parts[:4], parts[4:]
    send, attn_partial, block_moves, ffn_steps = lax.optimization_barrier((send, attn_partial, block_moves, ffn_steps))
    block_out = (residual + end_scatter(block_moves)).astype(BF16)
    d_first = scatter_ctx(mine, swap_core(send))
    d_from_first, _ = norm_back(d_first, first_hat, first_scale, attn_gain)
    grad_in = (d_resid + d_from_first).astype(BF16)

    totals = sum_all(
        jnp.concatenate(
            [
                attn_gain_part[:, 0] / attn_gain,
                jnp.sum(ffn_gain_part, axis=0),
                q_gain_part[:, 0],
                k_gain_part[:, 0],
            ]
        ).reshape(-1, 128)
    ).reshape(-1)
    grad_attn_gain = totals[:width]
    grad_ffn_gain = totals[width : 2 * width]
    grad_query_gain = totals[2 * width : 2 * width + head_size]
    grad_key_gain = totals[2 * width + head_size :]

    ffn_steps = [step.astype(F32) for step in ffn_steps]
    ffn_parts = gather_ctx(
        jnp.concatenate([ffn_steps[0] + ffn_steps[1], ffn_steps[2] + ffn_steps[3]], axis=1).astype(BF16)
    )
    attn_sum = end_sum_fsdp(start_sum_fsdp(attn_partial))
    attn_parts = gather_ctx(
        jnp.concatenate([sum_dp(attn_sum[:, :qkv_width]), sum_dp_transposed(attn_sum[:, qkv_width:])], axis=1)
    )
    grad_gate, grad_up, grad_down = call(
        assemble_ffn,
        [shape((count, 8 * ff_width), F32)] * 2 + [shape((ff_width, width), F32)],
        (owners, *ffn_parts),
        10**6,
        [pltpu.VMEM((8, count, 3 * ff_width), BF16)],
        1,
    )
    grad_query, grad_key, grad_value, grad_out = call(
        assemble_attn,
        [shape((count, width), F32)] + [shape((count, 8 * k_width), F32)] * 2 + [shape((q_width, width), F32)],
        (owners, *attn_parts),
        10**6,
        [pltpu.VMEM((8, count, qkv_width + q_width), BF16)],
        1,
    )
    return (
        block_out[None],
        grad_in[None],
        grad_attn_gain,
        grad_query,
        grad_key,
        grad_value,
        grad_query_gain,
        grad_key_gain,
        grad_out,
        grad_ffn_gain,
        grad_gate,
        grad_up,
        grad_down,
    )


def solution(mesh):
    in_specs = (
        P(("dp", "fsdp"), "ctx", None),
        P(("dp", "fsdp"), None),
        P(("dp", "fsdp"), "ctx", None),
        P(),
        P("fsdp", None),
        P("fsdp", None),
        P("fsdp", None),
        P(),
        P(),
        P("fsdp", None),
        P(),
        P("fsdp", None),
        P("fsdp", None),
        P("fsdp", None),
    )
    out_specs = (
        P(("dp", "fsdp"), "ctx", None),
        P(("dp", "fsdp"), "ctx", None),
        P(),
        P("fsdp", None),
        P("fsdp", None),
        P("fsdp", None),
        P(),
        P(),
        P("fsdp", None),
        P(),
        P("fsdp", None),
        P("fsdp", None),
        P("fsdp", None),
    )
    return jax.shard_map(body, mesh=mesh, in_specs=in_specs, out_specs=out_specs, check_vma=False)
```

time: 414 us -> 431 us (1.041)
  waiting for transfers between devices: 41.6 us -> 147 us
  matrix products: 64.4 us -> 0 us
  local copies, waits for them, and re-layouts: 90.8 us -> 36.7 us
  Pallas kernels: 0 us -> 46.6 us
  other arithmetic: 55.8 us -> 21 us
  starting transfers between devices: 147 us -> 171 us
    ppermute x3 -> x32, waiting for transfers between devices: 2.57 us -> 73.1 us  [move_y(): return lax.ppermute(value, 'fsdp', pairs)]
    dot_general x38 -> x0, matrix products: 56.4 us -> none  [the longest x13 17.1 us: mm_t(): lax.dot_general(left, right, (((1,), (1,)), ((), ())), preferred_element_...]
    ppermute x3 -> x32, starting transfers between devices: 7.89 us -> 63.9 us  [move_y(): return lax.ppermute(value, 'fsdp', pairs)]
    pallas_call x0 -> x9, Pallas kernels: none -> 46.6 us  [call(): pl.pallas_call(kernel, out_shape=out_shapes, in_specs=[smem] * scalars +...]
    ppermute x33, waiting for transfers between devices: 29.1 us -> 61 us  [move_z(): lax.ppermute(value, 'ctx', [(i, (i + 2 * step) % 8) for i in range(8)])]
    all_to_all x4 -> x0, starting transfers between devices: 25.9 us -> none  [the longest x2 14.1 us: sum_fsdp_rows(): lax.all_to_all(partial.astype(BF16), 'fsdp', split_axis=0, concat_axis=0,...]
    unnamed x265 -> x219, local copies, waits for them, and re-layouts: 41.7 us -> 24.9 us
    concatenate x13 -> x1, other arithmetic: 11.9 us -> 0.04 us  [body(): jnp.concatenate([ffn_steps[0] + ffn_steps[1], ffn_steps[2] + ffn_steps[3]...]
  transfers between devices with their start and end apart: 90 -> 109, of which waited for: 18 -> 34; matrix products, arithmetic and copies ran while one was open for 36% -> 7% of each run, Pallas kernels for 0% -> 11%
where the time goes in v2:
time: 431 us; the launch traced here: 425 us
  starting transfers between devices  171 us (40%)
  waiting for transfers between devices  147 us (34%)
  Pallas kernels  46.6 us (11%)
  local copies, waits for them, and re-layouts  36.7 us (9%)
  other arithmetic  21 us (5%)
    ppermute x32, waiting for transfers between devices, move_y(): return lax.ppermute(value, 'fsdp', pairs)  73.1 us
    ppermute x32, starting transfers between devices, move_y(): return lax.ppermute(value, 'fsdp', pairs)  63.9 us
    ppermute x33, waiting for transfers between devices, move_z(): lax.ppermute(value, 'ctx', [(i, (i + 2 * step) % 8) for i in range(8)])  61 us
    ppermute x33, starting transfers between devices, move_z(): lax.ppermute(value, 'ctx', [(i, (i + 2 * step) % 8) for i in range(8)])  54.1 us
    pallas_call x9, Pallas kernels, call(): pl.pallas_call(kernel, out_shape=out_shapes, in_specs=[smem] * scalars +...  46.6 us
    ppermute x35, starting transfers between devices, swap_core(): return lax.ppermute(value, 'ctx', [(i, i ^ 1) for i in range(8)])  27.8 us
    ppermute x6, starting transfers between devices, transpose_mesh(): return lax.ppermute(value, ('dp', 'ctx', 'fsdp'), pairs)  25.2 us
    unnamed x219, local copies, waits for them, and re-layouts  24.9 us
  transfers between devices with their start and end apart: 109, of which 34 were waited for; matrix products, arithmetic and copies ran while one was open for 7% of the time, Pallas kernels for 11%

profile of v2, /device:TPU:1, one launch (start us, length us, event | category | flops | bytes accessed | tf_op | source)
XLA Modules:
  0.0 424.7 jit_solution(6443716117286146056)
XLA Ops:
  30.4 4.5 %collective-permute-start = (bf16[128,1024]{1,0:T(8,128)(2,1)S(1)}, bf16[128,1024]{1,0:T(8,128)(2,1)S(1)}, u32[]{:S(2)}, u32[]{:S(2)}) collective-permute-start(bf16[128,1024]{1,0:T(8,128)(2,1)S(1)} %fusion.3.refs_0_.refs_1_), channel_id=1, source_target_pairs={{0,8},{8,0},{16,24},{24,16},{32,40},{40,32},{48,56},{56,48},{1,9},... | collective-permute-start | bytes 786440 | tf_op jit(solution)/shard_map/ppermute | solution.py:266
  34.9 8.4 %collective-permute-start.14 = (bf16[128,1024]{1,0:T(8,128)(2,1)S(1)}, bf16[128,1024]{1,0:T(8,128)(2,1)S(1)}, u32[]{:S(2)}, u32[]{:S(2)}) collective-permute-start(bf16[128,1024]{1,0:T(8,128)(2,1)S(1)} %copy-done.108), channel_id=1, source_target_pairs={{0,0},{1,8},{2,16},{3,24},{4,32},{5,40},{6,48},{7,56},{8,1},{9,9},... | collective-permute-start | bytes 786440 | tf_op jit(solution)/shard_map/ppermute | solution.py:298
  53.9 9.7 %shard_map.237 = (bf16[1024,128]{1,0:T(8,128)(2,1)S(1)}, f32[256,1024]{1,0:T(8,128)S(1)}, f32[8,1024]{1,0:T(8,128)S(1)}, bf16[4,128,1024]{2,1,0:T(8,128)(2,1)}, ...) custom-call(bf16[128,1024]{1,0:T(8,128)(2,1)S(1)} %fusion.3.refs_0_.refs_1, ...), custom_call_target="tpu_custom_call" | custom-call | flops 4000000000 | bytes 8688128 | tf_op jit(solution)/shard_map/pallas_call | solution.py:36
  70.8 7.0 %collective-permute-start.22 = (bf16[128,1728]{1,0:T(8,128)(2,1)}, bf16[128,1728]{1,0:T(8,128)(2,1)S(1)}, u32[]{:S(2)}, u32[]{:S(2)}) collective-permute-start(bf16[128,1728]{1,0:T(8,128)(2,1)} %concatenate.36), channel_id=1, source_target_pairs={{0,2},{1,3},{2,4},{3,5},{4,6},{5,7},{6,0},{7,1},{8,10},{9,11},{10,... | collective-permute-start | bytes 1327112 | tf_op jit(solution)/shard_map/ppermute | solution.py:311
  77.9 9.8 %collective-permute-start.23 = (bf16[128,1728]{1,0:T(8,128)(2,1)}, bf16[128,1728]{1,0:T(8,128)(2,1)S(1)}, u32[]{:S(2)}, u32[]{:S(2)}) collective-permute-start(bf16[128,1728]{1,0:T(8,128)(2,1)} %concatenate.36), channel_id=1, source_target_pairs={{0,6},{1,7},{2,0},{3,1},{4,2},{5,3},{6,4},{7,5},{8,14},{9,15},{10,... | collective-permute-start | bytes 1327112 | tf_op jit(solution)/shard_map/ppermute | solution.py:311
  89.3 9.5 %collective-permute-done.22 = bf16[128,1728]{1,0:T(8,128)(2,1)S(1)} collective-permute-done((bf16[128,1728]{1,0:T(8,128)(2,1)}, bf16[128,1728]{1,0:T(8,128)(2,1)S(1)}, u32[]{:S(2)}, u32[]{:S(2)}) %collective-permute-start.22) | collective-permute-done | bytes 442400 | tf_op jit(solution)/shard_map/ppermute | solution.py:311
  99.4 8.3 %collective-permute-done.23 = bf16[128,1728]{1,0:T(8,128)(2,1)S(1)} collective-permute-done((bf16[128,1728]{1,0:T(8,128)(2,1)}, bf16[128,1728]{1,0:T(8,128)(2,1)S(1)}, u32[]{:S(2)}, u32[]{:S(2)}) %collective-permute-start.23) | collective-permute-done | bytes 442400 | tf_op jit(solution)/shard_map/ppermute | solution.py:311
  109.3 3.9 collective-permute-start.17
  116.3 3.5 collective-permute-done.18
  119.8 10.4 %collective-permute-done.17 = bf16[128,1024]{1,0:T(8,128)(2,1)S(1)} collective-permute-done((bf16[128,1024]{1,0:T(8,128)(2,1)S(1)}, bf16[128,1024]{1,0:T(8,128)(2,1)S(1)}, u32[]{:S(2)}, u32[]{:S(2)}) %collective-permute-start.17) | collective-permute-done | bytes 262176 | tf_op jit(solution)/shard_map/ppermute | solution.py:270
  134.5 3.5 collective-permute-start.44
  138.0 14.7 %collective-permute-done.26 = bf16[128,1728]{1,0:T(8,128)(2,1)S(1)} collective-permute-done((bf16[128,1728]{1,0:T(8,128)(2,1)S(1)}, bf16[128,1728]{1,0:T(8,128)(2,1)S(1)}, u32[]{:S(2)}, u32[]{:S(2)}) %collective-permute-start.26) | collective-permute-done | bytes 442400 | tf_op jit(solution)/shard_map/ppermute | solution.py:311
  154.5 4.3 %collective-permute-start.36 = (bf16[128,1024]{1,0:T(8,128)(2,1)S(1)}, bf16[128,1024]{1,0:T(8,128)(2,1)S(1)}, u32[]{:S(2)}, u32[]{:S(2)}) collective-permute-start(bf16[128,1024]{1,0:T(8,128)(2,1)S(1)} %multiply_convert_fusion.first.refs_1_), channel_id=1, source_target_pairs={{0,16},{8,24},{16,32},{24,40},{32,48},{40,56},{48,0},{56,8},{1,17}... | collective-permute-start | bytes 786440 | tf_op jit(solution)/shard_map/ppermute | solution.py:270
  160.3 4.7 %collective-permute-start.31 = (bf16[128,1024]{1,0:T(8,128)(2,1)S(1)}, bf16[128,1024]{1,0:T(8,128)(2,1)S(1)}, u32[]{:S(2)}, u32[]{:S(2)}) collective-permute-start(bf16[128,1024]{1,0:T(8,128)(2,1)S(1)} %collective-permute-done.30.first.refs_7_), channel_id=1, source_target_pairs={{0,8},{8,0},{16,24},{24,16},{32,40},{40,32},{48,56},{56,48},{1,9},... | collective-permute-start | bytes 786440 | tf_op jit(solution)/shard_map/ppermute | solution.py:266
  186.9 5.6 %shard_map.242 = (bf16[128,1728]{1,0:T(8,128)(2,1)S(1)}, bf16[128,1728]{1,0:T(8,128)(2,1)S(1)}, bf16[128,1728]{1,0:T(8,128)(2,1)S(1)}, bf16[128,1728]{1,0:T(8,12...) custom-call(s32[2]{0:T(128)S(1)} %pad_add_fusion.refs_0_, ...), custom_call_target="tpu_custom_call" | custom-call | flops 4000000000 | bytes 11272200 | tf_op jit(solution)/shard_map/pallas_call | solution.py:36
  194.5 3.5 collective-permute-done.41
  205.2 11.9 %collective-permute-done.49.refs_11_ = bf16[128,1024]{1,0:T(8,128)(2,1)S(1)} collective-permute-done((bf16[128,1024]{1,0:T(8,128)(2,1)S(1)}, bf16[128,1024]{1,0:T(8,128)(2,1)S(1)}, u32[]{:S(2)}, u32[]{:S(2)}) %collective-permute-start.49) | collective-permute-done | bytes 262176 | tf_op jit(solution)/shard_map/ppermute | solution.py:270
  217.1 3.2 collective-permute-start.59
  221.2 26.1 %collective-permute-done.56 = bf16[128,1728]{1,0:T(8,128)(2,1)S(1)} collective-permute-done((bf16[128,1728]{1,0:T(8,128)(2,1)S(1)}, bf16[128,1728]{1,0:T(8,128)(2,1)S(1)}, u32[]{:S(2)}, u32[]{:S(2)}) %collective-permute-start.56) | collective-permute-done | bytes 442400 | tf_op jit(solution)/shard_map/ppermute | solution.py:311
  252.0 11.4 %shard_map.243 = (f32[64,1]{1,0:T(8,128)S(1)}, f32[64,1]{1,0:T(8,128)S(1)}, f32[1024,1]{1,0:T(8,128)S(1)}, bf16[4,128,1024]{2,1,0:T(8,128)(2,1)}, f32[128,1024]{...) custom-call(s32[2]{0:T(128)S(1)} %pad_add_fusion.refs_0_, ...), custom_call_target="tpu_custom_call" | custom-call | flops 8000000000 | bytes 11576328 | tf_op jit(solution)/shard_map/pallas_call | solution.py:36
  282.4 8.3 %collective-permute-done.68 = bf16[128,1728]{1,0:T(8,128)(2,1)S(1)} collective-permute-done((bf16[128,1728]{1,0:T(8,128)(2,1)S(1)}, bf16[128,1728]{1,0:T(8,128)(2,1)S(1)}, u32[]{:S(2)}, u32[]{:S(2)}) %collective-permute-start.68) | collective-permute-done | bytes 442400 | tf_op jit(solution)/shard_map/ppermute | solution.py:311
  292.7 3.4 collective-permute-start.70
  306.1 8.7 %collective-permute-start.90 = (bf16[128,384]{1,0:T(8,128)(2,1)S(1)}, bf16[128,384]{1,0:T(8,128)(2,1)S(1)}, u32[]{:S(2)}, u32[]{:S(2)}) collective-permute-start(bf16[128,384]{1,0:T(8,128)(2,1)S(1)} %copy-done.69), channel_id=1, source_target_pairs={{0,4},{1,5},{2,6},{3,7},{4,0},{5,1},{6,2},{7,3},{8,12},{9,13},{10,... | collective-permute-start | bytes 294920 | tf_op jit(solution)/shard_map/ppermute | solution.py:311
  314.8 11.1 %collective-permute-start.89 = (bf16[128,384]{1,0:T(8,128)(2,1)S(1)}, bf16[128,384]{1,0:T(8,128)(2,1)S(1)}, u32[]{:S(2)}, u32[]{:S(2)}) collective-permute-start(bf16[128,384]{1,0:T(8,128)(2,1)S(1)} %copy-done.67), channel_id=1, source_target_pairs={{0,6},{1,7},{2,0},{3,1},{4,2},{5,3},{6,4},{7,5},{8,14},{9,15},{10,... | collective-permute-start | bytes 294920 | tf_op jit(solution)/shard_map/ppermute | solution.py:311
  337.1 8.0 %collective-permute-start.94 = (bf16[128,128]{1,0:T(8,128)(2,1)S(1)}, bf16[128,128]{1,0:T(8,128)(2,1)S(1)}, u32[]{:S(2)}, u32[]{:S(2)}) collective-permute-start(bf16[128,128]{1,0:T(8,128)(2,1)S(1)} %slice.46), channel_id=1, source_target_pairs={{0,64},{1,72},{2,80},{3,88},{4,96},{5,104},{6,112},{7,120},{8,65},... | collective-permute-start | bytes 98312 | tf_op jit(solution)/shard_map/ppermute | solution.py:298
  347.5 4.4 %collective-permute-done.93 = bf16[128,128]{1,0:T(8,128)(2,1)S(1)} collective-permute-done((bf16[128,128]{1,0:T(8,128)(2,1)S(1)}, bf16[128,128]{1,0:T(8,128)(2,1)S(1)}, u32[]{:S(2)}, u32[]{:S(2)}) %collective-permute-start.93) | collective-permute-done | bytes 32800 | tf_op jit(solution)/shard_map/ppermute | solution.py:298
  361.1 6.3 %collective-permute-start.96 = (bf16[128,384]{1,0:T(8,128)(2,1)S(1)}, bf16[128,384]{1,0:T(8,128)(2,1)S(1)}, u32[]{:S(2)}, u32[]{:S(2)}) collective-permute-start(bf16[128,384]{1,0:T(8,128)(2,1)S(1)} %pad_maximum_fusion.1.refs_1_), channel_id=1, source_target_pairs={{0,16},{8,24},{16,32},{24,40},{32,48},{40,56},{48,0},{56,8},{1,17}... | collective-permute-start | bytes 294920 | tf_op jit(solution)/shard_map/ppermute | solution.py:270
  368.6 5.2 %collective-permute-start.105 = (bf16[128,1728]{1,0:T(8,128)(2,1)S(1)}, bf16[128,1728]{1,0:T(8,128)(2,1)}, u32[]{:S(2)}, u32[]{:S(2)}) collective-permute-start(bf16[128,1728]{1,0:T(8,128)(2,1)S(1)} %pad_maximum_fusion.refs_1_), channel_id=1, source_target_pairs={{0,48},{8,56},{16,0},{24,8},{32,16},{40,24},{48,32},{56,40},{1,49}... | collective-permute-start | bytes 1327112 | tf_op jit(solution)/shard_map/ppermute | solution.py:270
  373.9 3.5 collective-permute-done.96.refs_3_
  378.7 7.8 %collective-permute-done.98.refs_5_ = bf16[128,384]{1,0:T(8,128)(2,1)S(1)} collective-permute-done((bf16[128,384]{1,0:T(8,128)(2,1)S(1)}, bf16[128,384]{1,0:T(8,128)(2,1)S(1)}, u32[]{:S(2)}, u32[]{:S(2)}) %collective-permute-start.98) | collective-permute-done | bytes 98336 | tf_op jit(solution)/shard_map/ppermute | solution.py:270
  399.6 3.7 collective-permute-done.107.refs_7_
  415.4 5.4 %shard_map.245 = (f32[128,4608]{1,0:T(8,128)}, f32[128,4608]{1,0:T(8,128)}, f32[576,1024]{1,0:T(8,128)}) custom-call(s32[8]{0:T(128)S(1)} %stack.74.refs_0_, bf16[128,1728]{1,0:T(8,128)(2,1)S(1)} %pad_maximum_fusion.refs_1_, bf16[128,1728]{1,0:T(8,128)(2,1)S(1)} %collective-permute-done.102.refs_2_, bf16[128,1728]{1,0:T(8,128)(2,1)S(1)} %collective-permute-done.103.refs_3_, ...), custom_call_target="tpu_custom_call" | custom-call | flops 1000000 | bytes 10616864 | tf_op jit(solution)/shard_map/pallas_call | solution.py:36
  (497 shorter events, 182.6 us)
Async XLA Ops:
  3.0 40.3 %collective-permute-start.1 = (bf16[128,1024]{1,0:T(8,128)(2,1)S(1)}, bf16[128,1024]{1,0:T(8,128)(2,1)S(1)}, u32[]{:S(2)}, u32[]{:S(2)}) collective-permute-start(bf16[128,1024]{1,0:T(8,128)(2,1)S(1)} %fusion.3.refs_0_.refs_1_), channel_id=1, source_target_pairs={{0,16},{8,24},{16,32},{24,40},{32,48},{40,56},{48,0},{56,8},{1,17}... | collective-permute-start | bytes 786440 | tf_op jit(solution)/shard_map/ppermute | solution.py:270
  5.5 37.9 %collective-permute-start.3 = (bf16[128,1024]{1,0:T(8,128)(2,1)S(1)}, bf16[128,1024]{1,0:T(8,128)(2,1)S(1)}, u32[]{:S(2)}, u32[]{:S(2)}) collective-permute-start(bf16[128,1024]{1,0:T(8,128)(2,1)S(1)} %fusion.3.refs_0_.refs_1_), channel_id=1, source_target_pairs={{0,48},{8,56},{16,0},{24,8},{32,16},{40,24},{48,32},{56,40},{1,49}... | collective-permute-start | bytes 786440 | tf_op jit(solution)/shard_map/ppermute | solution.py:270
  7.7 36.2 %collective-permute-start.5 = (bf16[128,1024]{1,0:T(8,128)(2,1)S(1)}, bf16[128,1024]{1,0:T(8,128)(2,1)S(1)}, u32[]{:S(2)}, u32[]{:S(2)}) collective-permute-start(bf16[128,1024]{1,0:T(8,128)(2,1)S(1)} %fusion.3.refs_0_.refs_1_), channel_id=1, source_target_pairs={{0,32},{8,40},{16,48},{24,56},{32,0},{40,8},{48,16},{56,24},{1,33}... | collective-permute-start | bytes 786440 | tf_op jit(solution)/shard_map/ppermute | solution.py:270
  44.1 24.7 %collective-permute-start.21 = (bf16[128,576]{1,0:T(8,128)(2,1)}, bf16[128,576]{1,0:T(8,128)(2,1)}, u32[]{:S(2)}, u32[]{:S(2)}) collective-permute-start(bf16[128,576]{1,0:T(8,128)(2,1)} %bitcast.23), channel_id=1, source_target_pairs={{0,0},{1,8},{2,16},{3,24},{4,32},{5,40},{6,48},{7,56},{8,1},{9,9},... | collective-permute-start | bytes 442376 | tf_op jit(solution)/shard_map/ppermute | solution.py:298
  66.7 41.1 %collective-permute-start.15 = (bf16[4,128,1024]{2,1,0:T(8,128)(2,1)}, bf16[4,128,1024]{2,1,0:T(8,128)(2,1)}, u32[]{:S(2)}, u32[]{:S(2)}) collective-permute-start(bf16[4,128,1024]{2,1,0:T(8,128)(2,1)} %get-tuple-element.128), channel_id=1, source_target_pairs={{0,8},{8,0},{16,24},{24,16},{32,40},{40,32},{48,56},{56,48},{1,9},... | collective-permute-start | bytes 3145736 | tf_op jit(solution)/shard_map/ppermute | solution.py:266
  70.8 27.9 %collective-permute-start.22 = (bf16[128,1728]{1,0:T(8,128)(2,1)}, bf16[128,1728]{1,0:T(8,128)(2,1)S(1)}, u32[]{:S(2)}, u32[]{:S(2)}) collective-permute-start(bf16[128,1728]{1,0:T(8,128)(2,1)} %concatenate.36), channel_id=1, source_target_pairs={{0,2},{1,3},{2,4},{3,5},{4,6},{5,7},{6,0},{7,1},{8,10},{9,11},{10,... | collective-permute-start | bytes 1327112 | tf_op jit(solution)/shard_map/ppermute | solution.py:311
  77.9 29.8 %collective-permute-start.23 = (bf16[128,1728]{1,0:T(8,128)(2,1)}, bf16[128,1728]{1,0:T(8,128)(2,1)S(1)}, u32[]{:S(2)}, u32[]{:S(2)}) collective-permute-start(bf16[128,1728]{1,0:T(8,128)(2,1)} %concatenate.36), channel_id=1, source_target_pairs={{0,6},{1,7},{2,0},{3,1},{4,2},{5,3},{6,4},{7,5},{8,14},{9,15},{10,... | collective-permute-start | bytes 1327112 | tf_op jit(solution)/shard_map/ppermute | solution.py:311
  87.7 25.5 %collective-permute-start.24 = (bf16[128,1728]{1,0:T(8,128)(2,1)}, bf16[128,1728]{1,0:T(8,128)(2,1)S(1)}, u32[]{:S(2)}, u32[]{:S(2)}) collective-permute-start(bf16[128,1728]{1,0:T(8,128)(2,1)} %concatenate.36), channel_id=1, source_target_pairs={{0,4},{1,5},{2,6},{3,7},{4,0},{5,1},{6,2},{7,3},{8,12},{9,13},{10,... | collective-permute-start | bytes 1327112 | tf_op jit(solution)/shard_map/ppermute | solution.py:311
  88.9 25.4 %collective-permute-start.25 = (bf16[128,1728]{1,0:T(8,128)(2,1)}, bf16[128,1728]{1,0:T(8,128)(2,1)S(1)}, u32[]{:S(2)}, u32[]{:S(2)}) collective-permute-start(bf16[128,1728]{1,0:T(8,128)(2,1)} %concatenate.36), channel_id=1, source_target_pairs={{0,1},{1,0},{2,3},{3,2},{4,5},{5,4},{6,7},{7,6},{8,9},{9,8},{10,11... | collective-permute-start | bytes 1327112 | tf_op jit(solution)/shard_map/ppermute | solution.py:311
  98.7 35.8 %collective-permute-start.20 = (bf16[128,1024]{1,0:T(8,128)(2,1)S(1)}, bf16[128,1024]{1,0:T(8,128)(2,1)S(1)}, u32[]{:S(2)}, u32[]{:S(2)}) collective-permute-start(bf16[128,1024]{1,0:T(8,128)(2,1)S(1)} %bitcast.96), channel_id=1, source_target_pairs={{0,8},{8,0},{16,24},{24,16},{32,40},{40,32},{48,56},{56,48},{1,9},... | collective-permute-start | bytes 786440 | tf_op jit(solution)/shard_map/ppermute | solution.py:266
  114.4 23.7 %collective-permute-start.32 = (bf16[128,1024]{1,0:T(8,128)(2,1)S(1)}, bf16[128,1024]{1,0:T(8,128)(2,1)S(1)}, u32[]{:S(2)}, u32[]{:S(2)}) collective-permute-start(bf16[128,1024]{1,0:T(8,128)(2,1)S(1)} %bitcast.97), channel_id=1, source_target_pairs={{0,32},{8,40},{16,48},{24,56},{32,0},{40,8},{48,16},{56,24},{1,33}... | collective-permute-start | bytes 786440 | tf_op jit(solution)/shard_map/ppermute | solution.py:270
  119.8 32.9 %collective-permute-start.38 = (bf16[128,1024]{1,0:T(8,128)(2,1)S(1)}, bf16[128,1024]{1,0:T(8,128)(2,1)S(1)}, u32[]{:S(2)}, u32[]{:S(2)}) collective-permute-start(bf16[128,1024]{1,0:T(8,128)(2,1)S(1)} %bitcast.98), channel_id=1, source_target_pairs={{0,16},{8,24},{16,32},{24,40},{32,48},{40,56},{48,0},{56,8},{1,17}... | collective-permute-start | bytes 786440 | tf_op jit(solution)/shard_map/ppermute | solution.py:270
  130.2 22.5 %collective-permute-start.26 = (bf16[128,1728]{1,0:T(8,128)(2,1)S(1)}, bf16[128,1728]{1,0:T(8,128)(2,1)S(1)}, u32[]{:S(2)}, u32[]{:S(2)}) collective-permute-start(bf16[128,1728]{1,0:T(8,128)(2,1)S(1)} %collective-permute-done.25), channel_id=1, source_target_pairs={{0,2},{1,3},{2,4},{3,5},{4,6},{5,7},{6,0},{7,1},{8,10},{9,11},{10,... | collective-permute-start | bytes 1327112 | tf_op jit(solution)/shard_map/ppermute | solution.py:311
  130.4 24.1 %collective-permute-start.27 = (bf16[128,1728]{1,0:T(8,128)(2,1)S(1)}, bf16[128,1728]{1,0:T(8,128)(2,1)S(1)}, u32[]{:S(2)}, u32[]{:S(2)}) collective-permute-start(bf16[128,1728]{1,0:T(8,128)(2,1)S(1)} %collective-permute-done.25), channel_id=1, source_target_pairs={{0,6},{1,7},{2,0},{3,1},{4,2},{5,3},{6,4},{7,5},{8,14},{9,15},{10,... | collective-permute-start | bytes 1327112 | tf_op jit(solution)/shard_map/ppermute | solution.py:311
  134.5 24.4 %collective-permute-start.44 = (bf16[128,1024]{1,0:T(8,128)(2,1)S(1)}, bf16[128,1024]{1,0:T(8,128)(2,1)S(1)}, u32[]{:S(2)}, u32[]{:S(2)}) collective-permute-start(bf16[128,1024]{1,0:T(8,128)(2,1)S(1)} %bitcast.99), channel_id=1, source_target_pairs={{0,48},{8,56},{16,0},{24,8},{32,16},{40,24},{48,32},{56,40},{1,49}... | collective-permute-start | bytes 786440 | tf_op jit(solution)/shard_map/ppermute | solution.py:270
  205.1 42.1 %collective-permute-start.56 = (bf16[128,1728]{1,0:T(8,128)(2,1)S(1)}, bf16[128,1728]{1,0:T(8,128)(2,1)S(1)}, u32[]{:S(2)}, u32[]{:S(2)}) collective-permute-start(bf16[128,1728]{1,0:T(8,128)(2,1)S(1)} %get-tuple-element.163), channel_id=1, source_target_pairs={{0,2},{1,3},{2,4},{3,5},{4,6},{5,7},{6,0},{7,1},{8,10},{9,11},{10,... | collective-permute-start | bytes 1327112 | tf_op jit(solution)/shard_map/ppermute | solution.py:311
  217.1 31.8 %collective-permute-start.57 = (bf16[128,1728]{1,0:T(8,128)(2,1)S(1)}, bf16[128,1728]{1,0:T(8,128)(2,1)S(1)}, u32[]{:S(2)}, u32[]{:S(2)}) collective-permute-start(bf16[128,1728]{1,0:T(8,128)(2,1)S(1)} %get-tuple-element.164), channel_id=1, source_target_pairs={{0,6},{1,7},{2,0},{3,1},{4,2},{5,3},{6,4},{7,5},{8,14},{9,15},{10,... | collective-permute-start | bytes 1327112 | tf_op jit(solution)/shard_map/ppermute | solution.py:311
  217.1 31.9 %collective-permute-start.58 = (bf16[128,1728]{1,0:T(8,128)(2,1)S(1)}, bf16[128,1728]{1,0:T(8,128)(2,1)S(1)}, u32[]{:S(2)}, u32[]{:S(2)}) collective-permute-start(bf16[128,1728]{1,0:T(8,128)(2,1)S(1)} %get-tuple-element.165), channel_id=1, source_target_pairs={{0,6},{1,7},{2,0},{3,1},{4,2},{5,3},{6,4},{7,5},{8,14},{9,15},{10,... | collective-permute-start | bytes 1327112 | tf_op jit(solution)/shard_map/ppermute | solution.py:311
  217.1 32.3 %collective-permute-start.59 = (bf16[128,1728]{1,0:T(8,128)(2,1)S(1)}, bf16[128,1728]{1,0:T(8,128)(2,1)S(1)}, u32[]{:S(2)}, u32[]{:S(2)}) collective-permute-start(bf16[128,1728]{1,0:T(8,128)(2,1)S(1)} %get-tuple-element.166), channel_id=1, source_target_pairs={{0,4},{1,5},{2,6},{3,7},{4,0},{5,1},{6,2},{7,3},{8,12},{9,13},{10,... | collective-permute-start | bytes 1327112 | tf_op jit(solution)/shard_map/ppermute | solution.py:311
  220.4 29.0 %collective-permute-start.60 = (bf16[128,1728]{1,0:T(8,128)(2,1)S(1)}, bf16[128,1728]{1,0:T(8,128)(2,1)S(1)}, u32[]{:S(2)}, u32[]{:S(2)}) collective-permute-start(bf16[128,1728]{1,0:T(8,128)(2,1)S(1)} %get-tuple-element.167), channel_id=1, source_target_pairs={{0,4},{1,5},{2,6},{3,7},{4,0},{5,1},{6,2},{7,3},{8,12},{9,13},{10,... | collective-permute-start | bytes 1327112 | tf_op jit(solution)/shard_map/ppermute | solution.py:311
  250.8 41.9 %collective-permute-start.61 = (bf16[128,1024]{1,0:T(8,128)(2,1)}, bf16[128,1024]{1,0:T(8,128)(2,1)}, u32[]{:S(2)}, u32[]{:S(2)}) collective-permute-start(bf16[128,1024]{1,0:T(8,128)(2,1)} %get-tuple-element.195), channel_id=1, source_target_pairs={{0,8},{8,0},{16,24},{24,16},{32,40},{40,32},{48,56},{56,48},{1,9},... | collective-permute-start | bytes 786440 | tf_op jit(solution)/shard_map/ppermute | solution.py:266
  251.2 26.2 %collective-permute-start.62 = (bf16[128,1024]{1,0:T(8,128)(2,1)}, bf16[128,1024]{1,0:T(8,128)(2,1)}, u32[]{:S(2)}, u32[]{:S(2)}) collective-permute-start(bf16[128,1024]{1,0:T(8,128)(2,1)} %get-tuple-element.197), channel_id=1, source_target_pairs={{0,8},{8,0},{16,24},{24,16},{32,40},{40,32},{48,56},{56,48},{1,9},... | collective-permute-start | bytes 786440 | tf_op jit(solution)/shard_map/ppermute | solution.py:266
  251.3 27.2 %collective-permute-start.64 = (bf16[128,1024]{1,0:T(8,128)(2,1)}, bf16[128,1024]{1,0:T(8,128)(2,1)}, u32[]{:S(2)}, u32[]{:S(2)}) collective-permute-start(bf16[128,1024]{1,0:T(8,128)(2,1)} %get-tuple-element.199), channel_id=1, source_target_pairs={{0,8},{8,0},{16,24},{24,16},{32,40},{40,32},{48,56},{56,48},{1,9},... | collective-permute-start | bytes 786440 | tf_op jit(solution)/shard_map/ppermute | solution.py:266
  251.7 29.1 %collective-permute-start.66 = (bf16[128,1024]{1,0:T(8,128)(2,1)}, bf16[128,1024]{1,0:T(8,128)(2,1)}, u32[]{:S(2)}, u32[]{:S(2)}) collective-permute-start(bf16[128,1024]{1,0:T(8,128)(2,1)} %get-tuple-element.201), channel_id=1, source_target_pairs={{0,8},{8,0},{16,24},{24,16},{32,40},{40,32},{48,56},{56,48},{1,9},... | collective-permute-start | bytes 786440 | tf_op jit(solution)/shard_map/ppermute | solution.py:266
  302.7 55.0 %collective-permute-start.82 = (f32[17,128]{1,0:T(8,128)S(1)}, f32[17,128]{1,0:T(8,128)S(1)}, u32[]{:S(2)}, u32[]{:S(2)}) collective-permute-start(f32[17,128]{1,0:T(8,128)S(1)} %add_add_fusion.1), channel_id=1, source_target_pairs={{0,4},{1,5},{2,6},{3,7},{4,0},{5,1},{6,2},{7,3},{8,12},{9,13},{10,... | collective-permute-start | bytes 26120 | tf_op jit(solution)/shard_map/ppermute | solution.py:311
  306.1 22.2 %collective-permute-start.90 = (bf16[128,384]{1,0:T(8,128)(2,1)S(1)}, bf16[128,384]{1,0:T(8,128)(2,1)S(1)}, u32[]{:S(2)}, u32[]{:S(2)}) collective-permute-start(bf16[128,384]{1,0:T(8,128)(2,1)S(1)} %copy-done.69), channel_id=1, source_target_pairs={{0,4},{1,5},{2,6},{3,7},{4,0},{5,1},{6,2},{7,3},{8,12},{9,13},{10,... | collective-permute-start | bytes 294920 | tf_op jit(solution)/shard_map/ppermute | solution.py:311
  332.3 26.1 %collective-permute-start.81 = (f32[17,128]{1,0:T(8,128)S(1)}, f32[17,128]{1,0:T(8,128)S(1)}, u32[]{:S(2)}, u32[]{:S(2)}) collective-permute-start(f32[17,128]{1,0:T(8,128)S(1)} %add_add_fusion.1), channel_id=1, source_target_pairs={{0,6},{1,7},{2,0},{3,1},{4,2},{5,3},{6,4},{7,5},{8,14},{9,15},{10,... | collective-permute-start | bytes 26120 | tf_op jit(solution)/shard_map/ppermute | solution.py:311
  334.4 24.1 %collective-permute-start.80 = (f32[17,128]{1,0:T(8,128)S(1)}, f32[17,128]{1,0:T(8,128)S(1)}, u32[]{:S(2)}, u32[]{:S(2)}) collective-permute-start(f32[17,128]{1,0:T(8,128)S(1)} %add_add_fusion.1), channel_id=1, source_target_pairs={{0,2},{1,3},{2,4},{3,5},{4,6},{5,7},{6,0},{7,1},{8,10},{9,11},{10,... | collective-permute-start | bytes 26120 | tf_op jit(solution)/shard_map/ppermute | solution.py:311
  347.1 50.7 %collective-permute-start.72 = (bf16[4,128,1024]{2,1,0:T(8,128)(2,1)}, bf16[4,128,1024]{2,1,0:T(8,128)(2,1)}, u32[]{:S(2)}, u32[]{:S(2)}) collective-permute-start(bf16[4,128,1024]{2,1,0:T(8,128)(2,1)} %get-tuple-element.215), channel_id=1, source_target_pairs={{0,8},{8,0},{16,24},{24,16},{32,40},{40,32},{48,56},{56,48},{1,9},... | collective-permute-start | bytes 3145736 | tf_op jit(solution)/shard_map/ppermute | solution.py:266
  355.0 39.2 %collective-permute-start.103 = (bf16[128,1728]{1,0:T(8,128)(2,1)S(1)}, bf16[128,1728]{1,0:T(8,128)(2,1)S(1)}, u32[]{:S(2)}, u32[]{:S(2)}) collective-permute-start(bf16[128,1728]{1,0:T(8,128)(2,1)S(1)} %pad_maximum_fusion.refs_1_), channel_id=1, source_target_pairs={{0,16},{8,24},{16,32},{24,40},{32,48},{40,56},{48,0},{56,8},{1,17}... | collective-permute-start | bytes 1327112 | tf_op jit(solution)/shard_map/ppermute | solution.py:270
  367.5 29.8 %collective-permute-start.102 = (bf16[128,1728]{1,0:T(8,128)(2,1)S(1)}, bf16[128,1728]{1,0:T(8,128)(2,1)S(1)}, u32[]{:S(2)}, u32[]{:S(2)}) collective-permute-start(bf16[128,1728]{1,0:T(8,128)(2,1)S(1)} %pad_maximum_fusion.refs_1_), channel_id=1, source_target_pairs={{0,8},{8,0},{16,24},{24,16},{32,40},{40,32},{48,56},{56,48},{1,9},... | collective-permute-start | bytes 1327112 | tf_op jit(solution)/shard_map/ppermute | solution.py:266
  368.6 28.7 %collective-permute-start.105 = (bf16[128,1728]{1,0:T(8,128)(2,1)S(1)}, bf16[128,1728]{1,0:T(8,128)(2,1)}, u32[]{:S(2)}, u32[]{:S(2)}) collective-permute-start(bf16[128,1728]{1,0:T(8,128)(2,1)S(1)} %pad_maximum_fusion.refs_1_), channel_id=1, source_target_pairs={{0,48},{8,56},{16,0},{24,8},{32,16},{40,24},{48,32},{56,40},{1,49}... | collective-permute-start | bytes 1327112 | tf_op jit(solution)/shard_map/ppermute | solution.py:270
  (186 other events, 3591.5 us)

commit v3 on v2

--- a/solution.py
+++ b/solution.py
@@ -69,16 +69,17 @@
 
 def attend_forward(*refs):
     pieces, refs = refs[:8], refs[8:]
-    w_qkv, out_rows, cos_ref, sin_ref, column_ref, row_ref, q_gain, k_gain = refs[:8]
-    mixed_ref, qkv_ref, lse_ref, send_ref, *mine_refs = refs[8:]
+    w_qkv, cos_ref, sin_ref, column_ref, row_ref, q_gain, k_gain = refs[:7]
+    qkv_ref, lse_ref, *mixed_refs = refs[7:]
     length = qkv_ref.shape[1]
+    count = length // 8
     head = q_gain.shape[0]
     for pair in range(4):
         x = jnp.concatenate([pieces[2 * pair][...], pieces[2 * pair + 1][...]], axis=0)
-        qkv_ref[:, pair * 256 : (pair + 1) * 256] = jnp.transpose(mm(x, w_qkv[...]))
+        qkv_ref[:, pair * 2 * count : (pair + 1) * 2 * count] = jnp.transpose(mm(x, w_qkv[...]))
     cosine, sine = cos_ref[...], sin_ref[...]
     queries = [
-        (head_forward(qkv_ref[h * head : (h + 1) * head], q_gain[...], cosine, sine)[2]).astype(BF16) * BF16(head**-0.5)
+        head_forward(qkv_ref[h * head : (h + 1) * head], q_gain[...], cosine, sine)[2].astype(BF16) * BF16(head**-0.5)
         for h in range(2)
     ]
     key = jnp.transpose(head_forward(qkv_ref[2 * head : 3 * head], k_gain[...], cosine, sine)[2]).astype(BF16)
@@ -96,24 +97,47 @@
             lse_ref[h : h + 1, lanes] = top + jnp.log(total)
             outs.append(mm(value, (weights * (1.0 / total)).astype(BF16)))
         mixed = jnp.transpose(jnp.concatenate(outs, axis=0)).astype(BF16)
-        mixed_ref[lanes] = mixed
-        proj = mm(mixed, out_rows[...])
-        mine_refs[tile][...] = proj[: width // 2]
-        send_ref[tile] = proj[width // 2 :].astype(BF16)
+        mixed_refs[2 * tile][...] = mixed[:count]
+        mixed_refs[2 * tile + 1][...] = mixed[count:]
+
+
+def out_project(order, *refs):
+    blocks, (w_out, tokens, gain, resid_ref, normed_ref, mixed_ref) = refs[:8], refs[8:]
+    count = blocks[0].shape[1]
+    for i in range(8):
+        mixed_ref[:, pl.ds(pl.multiple_of(order[i] * count, count), count)] = blocks[i][...]
+    resid = tokens[...].astype(F32) + mm(mixed_ref[...], w_out[...])
+    resid_ref[...] = resid
+    normed_ref[...] = (resid * rms_scale(resid) * gain[...]).astype(BF16)
+
+
+def resid_backward(order, *refs):
+    total, move_a, move_b, move_c, resid_ref, cot_ref, gain_ref, w_out = refs[:8]
+    d_resid_ref, d_attn_ref, gain_part_ref = refs[8:11]
+    block_refs, d_mixed_ref = refs[11:19], refs[19]
+    d_second = total[...] + move_a[...].astype(F32) + move_b[...].astype(F32) + move_c[...].astype(F32)
+    resid = resid_ref[...]
+    scale = rms_scale(resid)
+    d_from, gain_part = norm_back(d_second, resid * scale, scale, gain_ref[...])
+    gain_part_ref[...] = jnp.sum(gain_part, axis=0, keepdims=True)
+    d_resid = cot_ref[...].astype(F32) + d_from
+    d_resid_ref[...] = d_resid
+    d_attn = d_resid.astype(BF16)
+    d_attn_ref[...] = d_attn
+    d_mixed_ref[...] = mm_t(d_attn, w_out[...]).astype(BF16)
+    count = block_refs[0].shape[1]
+    for i in range(8):
+        block_refs[i][...] = d_mixed_ref[:, pl.ds(pl.multiple_of(order[i] * count, count), count)]
 
 
 def attend_backward(*refs):
-    place, pieces, d_pieces, refs = refs[0], refs[1:9], refs[9:17], refs[17:]
-    w_qkv, out_rows, cos_ref, sin_ref, column_ref, row_ref, q_gain, k_gain, mixed_ref, qkv_ref, lse_ref = refs[:11]
-    q_gain_ref, k_gain_ref, attn_gain_ref, send_ref = refs[11:15]
-    mine_refs, part_refs = refs[15:19], refs[19:27]
-    d_attn_ref, x_ref, d_qkv_ref, grads_ref = refs[27:]
+    d_blocks, refs = refs[:8], refs[8:]
+    w_qkv, cos_ref, sin_ref, column_ref, row_ref, q_gain, k_gain, qkv_ref, lse_ref = refs[:9]
+    q_gain_ref, k_gain_ref, d_low_ref, send_ref = refs[9:13]
+    mine_refs, d_qkv_ref = refs[13:17], refs[17]
     length = qkv_ref.shape[1]
     head = q_gain.shape[0]
-    count = pieces[0].shape[0]
-    for i in range(8):
-        d_attn_ref[i * count : (i + 1) * count] = d_pieces[i][...]
-        x_ref[i * count : (i + 1) * count] = pieces[i][...]
+    count = length // 8
     cosine, sine = cos_ref[...], sin_ref[...]
     scales, hats, queries = [], [], []
     for h in range(2):
@@ -131,7 +155,8 @@
     for tile in range(length // width):
         lanes = slice(tile * width, (tile + 1) * width)
         allowed = column_ref[...] <= row_ref[:, lanes]
-        d_mixed = jnp.transpose(mm_t(d_attn_ref[lanes], out_rows[...])).astype(BF16)
+        d_mixed = jnp.concatenate([d_blocks[2 * tile][...], d_blocks[2 * tile + 1][...]], axis=0)
+        d_mixed = jnp.transpose(d_mixed.astype(F32)).astype(BF16)
         for h in range(2):
             rows = slice(h * head, (h + 1) * head)
             query = queries[h][:, lanes]
@@ -157,57 +182,72 @@
     for tile in range(4):
         lanes = slice(tile * 2 * count, (tile + 1) * 2 * count)
         d_qkv = jnp.transpose(d_qkv_ref[:, lanes]).astype(BF16)
+        d_low_ref[lanes] = d_qkv
         d_first = mm_t(d_qkv, w_qkv[...])
         mine_refs[tile][...] = d_first[:count]
         send_ref[tile] = d_first[count:].astype(BF16)
-    grad_qkv = jnp.transpose(mm(d_qkv_ref[...].astype(BF16), x_ref[...]))
-    attn_gain_ref[...] = jnp.sum(grad_qkv * w_qkv[...].astype(F32), axis=1, keepdims=True)
-    grads_ref[:, : 4 * head] = grad_qkv.astype(BF16)
-    grads_ref[:, 4 * head :] = jnp.transpose(
-        lax.dot_general(mixed_ref[...], d_attn_ref[...], (((0,), (0,)), ((), ())), preferred_element_type=F32)
-    ).astype(BF16)
+
+
+def attend_weights(*refs):
+    place, pieces, d_pieces, blocks = refs[0], refs[1:9], refs[9:17], refs[17:25]
+    d_low_ref, w_qkv, attn_gain_ref = refs[25:28]
+    part_refs, x_ref, mixed_ref, grads_ref = refs[28:36], refs[36], refs[37], refs[38]
+    count = pieces[0].shape[0]
+    width = d_low_ref.shape[1]
+    for i in range(8):
+        x_ref[i * count : (i + 1) * count] = pieces[i][...]
+        mixed_ref[i * count : (i + 1) * count] = blocks[i][...]
+    grad_qkv = outer_sum(d_low_ref[...], x_ref[...])
+    attn_gain_ref[...] = jnp.sum(grad_qkv * jnp.transpose(w_qkv[...].astype(F32)), axis=0, keepdims=True)
+    grads_ref[:, :width] = jnp.transpose(grad_qkv).astype(BF16)
+    for i in range(8):
+        x_ref[i * count : (i + 1) * count] = d_pieces[i][...]
+    grads_ref[:, width:] = jnp.transpose(outer_sum(mixed_ref[...], x_ref[...])).astype(BF16)
     for i, step in enumerate(Y_STEPS):
         for flip in (0, 1):
             owner = (place[0] + step) % 4 * 2 + (place[1] ^ flip)
             part_refs[2 * i + flip][...] = grads_ref[pl.ds(pl.multiple_of(owner * count, count), count)]
 
 
-def ffn_group(first, second, cot_first, cot_second, weights, hidden_ref, d_ffn_ref, d_mine, d_send, mine, send):
+def ffn(*refs):
+    seconds, cots, weights = refs[:8], refs[8:16], refs[16]
+    hidden_ref, d_ffn_ref, d_send, send = refs[17:21]
+    d_mine, mine = refs[21:25], refs[25:29]
     width = hidden_ref.shape[1]
-    count = first.shape[0]
-    x = jnp.concatenate([first[...], second[...]], axis=0)
-    cot = jnp.concatenate([cot_first[...], cot_second[...]], axis=0)
-    both = mm(x, weights[:, : 2 * width])
-    gate, up = both[:, :width], both[:, width:]
-    sigmoid = 1.0 / (1.0 + jnp.exp(-gate))
-    act = gate * sigmoid
-    hidden = (act * up).astype(BF16)
-    hidden_ref[...] = hidden
-    d_hidden = mm(cot, weights[:, 2 * width :])
-    d_gate = d_hidden * up * sigmoid * (1.0 + gate * (1.0 - sigmoid))
-    d_ffn = jnp.concatenate([d_gate, d_hidden * act], axis=1).astype(BF16)
-    d_ffn_ref[...] = d_ffn
-    d_second = mm_t(d_ffn, weights[:, : 2 * width])
-    d_mine[...] = d_second[:count]
-    d_send[...] = d_second[count:].astype(BF16)
-    out = mm_t(hidden, weights[:, 2 * width :])
-    mine[...] = out[:count]
-    send[...] = out[count:].astype(BF16)
+    count = seconds[0].shape[0]
+    for group in (3, 1, 2, 0):
+        rows = slice(2 * group * count, 2 * (group + 1) * count)
+        x = jnp.concatenate([seconds[2 * group][...], seconds[2 * group + 1][...]], axis=0)
+        cot = jnp.concatenate([cots[2 * group][...], cots[2 * group + 1][...]], axis=0)
+        both = mm(x, weights[:, : 2 * width])
+        gate, up = both[:, :width], both[:, width:]
+        sigmoid = 1.0 / (1.0 + jnp.exp(-gate))
+        act = gate * sigmoid
+        hidden = (act * up).astype(BF16)
+        hidden_ref[rows] = hidden
+        d_hidden = mm(cot, weights[:, 2 * width :])
+        d_gate = d_hidden * up * sigmoid * (1.0 + gate * (1.0 - sigmoid))
+        d_ffn = jnp.concatenate([d_gate, d_hidden * act], axis=1).astype(BF16)
+        d_ffn_ref[rows] = d_ffn
+        d_second = mm_t(d_ffn, weights[:, : 2 * width])
+        d_mine[group][...] = d_second[:count]
+        d_send[group] = d_second[count:].astype(BF16)
+        out = mm_t(hidden, weights[:, 2 * width :])
+        mine[group][...] = out[:count]
+        send[group] = out[count:].astype(BF16)
 
 
 def ffn_weights(*refs):
-    place, seconds, cots, hiddens, d_ffns = refs[0], refs[1:9], refs[9:17], refs[17:21], refs[21:25]
-    part_refs, x_ref, h_ref = refs[25:33], refs[33], refs[34]
+    place, seconds, cots, hidden_ref, d_ffn_ref = refs[0], refs[1:9], refs[9:17], refs[17], refs[18]
+    part_refs, x_ref = refs[19:27], refs[27]
     count = seconds[0].shape[0]
-    for pieces, others, columns in ((seconds, d_ffns, 0), (cots, hiddens, d_ffns[0].shape[1])):
+    for pieces, other_ref, columns in ((seconds, d_ffn_ref, 0), (cots, hidden_ref, d_ffn_ref.shape[1])):
         for i in range(8):
             x_ref[i * count : (i + 1) * count] = pieces[i][...]
-        width = others[0].shape[1]
-        for i in range(4):
-            h_ref[2 * i * count : 2 * (i + 1) * count, :width] = others[i][...]
+        width = other_ref.shape[1]
         for i, step in enumerate(Y_STEPS):
             rows = pl.ds(pl.multiple_of((place[0] + step) % 4 * (2 * count), 2 * count), 2 * count)
-            both = outer_sum(x_ref[:, rows], h_ref[:, :width])
+            both = outer_sum(x_ref[:, rows], other_ref[...])
             low, high = both[:count], both[count:]
             first = place[1] == 0
             part_refs[2 * i][:, columns : columns + width] = jnp.where(first, low, high).astype(BF16)
@@ -291,6 +331,28 @@
     return end_scatter(start_scatter_ctx(mine, received))
 
 
+def exchange_ctx(blocks):
+    out = [None] * 8
+    for i, step in enumerate(STEPS):
+        back = (0, 2, 1, 3)[i]
+        for flip in (0, 1):
+            pairs = [(c, (c // 2 + step) % 4 * 2 + (c % 2 ^ flip)) for c in range(8)]
+            block = blocks[2 * i + flip]
+            out[2 * back + flip] = lax.ppermute(block, "ctx", pairs) if step or flip else block
+    return out
+
+
+def stage(*values):
+    return lax.optimization_barrier(values)
+
+
+def swap_pieces(moved):
+    pieces = []
+    for piece in moved:
+        pieces += [piece, swap_core(piece)]
+    return pieces
+
+
 def transpose_mesh(value, flip=0):
     pairs = [
         ((d * 8 + c) * 8 + f, ((d ^ flip) * 8 + f) * 8 + c) for d in range(2) for c in range(8) for f in range(8)
@@ -311,13 +373,16 @@
     return lax.ppermute(value, "fsdp", pairs)
 
 
-def gather_fsdp_rows(block):
+def spread_y(held):
+    return [move_y(held, step) if step else held for step in (0, 1, 3, 2)]
+
+
+def join_fsdp(own_side, other_side):
     me = lax.axis_index("fsdp")
-    rows = block.shape[0]
-    whole = jnp.zeros((8 * rows, block.shape[1]), block.dtype)
-    for flip, held in ((0, block), (1, move_y(block, 0, 1))):
-        for step in (0, 1, 3, 2):
-            piece = move_y(held, step) if step else held
+    rows, columns = own_side[0].shape
+    whole = jnp.zeros((8 * rows, columns), BF16)
+    for flip, side in ((0, own_side), (1, other_side)):
+        for step, piece in zip((0, 1, 3, 2), side):
             owner = (me // 2 - step) % 4 * 2 + (me % 2 ^ flip)
             whole = lax.dynamic_update_slice_in_dim(whole, piece, owner * rows, 0)
     return whole
@@ -379,150 +444,159 @@
     k_width = w_key.shape[1] // 8
     ff_width = w_gate.shape[1] // 8
 
-    w_qkv = gather_fsdp_rows(
-        jnp.concatenate(
-            [own_columns(w_query, q_width, ctx), own_columns(w_key, k_width, ctx), own_columns(w_value, k_width, ctx)],
-            axis=1,
-        )
-    )
-    out_rows = transpose_mesh(w_out)
-    down_chunk = transpose_mesh(jnp.transpose(own_columns(w_down, width // 8, ctx)))
-    ffn_block = jnp.concatenate(
-        [own_columns(w_gate, ff_width, ctx), own_columns(w_up, ff_width, ctx), down_chunk], axis=1
-    )
-    ffn_rows = gather_fsdp_rows(after(ffn_block, w_qkv))
-    place = jnp.stack([lax.axis_index("fsdp") // 2, lax.axis_index("fsdp") % 2])
-
     z_index, core = ctx // 2, ctx % 2
     owners = jnp.stack(
         [((z_index + step) % 4) * 2 + (core ^ flip) for step in STEPS for flip in (0, 1)]
     )
+    place = jnp.stack([lax.axis_index("fsdp") // 2, lax.axis_index("fsdp") % 2])
     places = positions[0].reshape(8, count)[owners].reshape(8 * count)
     length = 8 * count
     cosine_table, sine_table = rope_tables(places, head_size)
     column = jnp.broadcast_to(places[:, None], (length, 2 * count))
     row = places[None]
     gains = (query_gain[:, None], key_gain[:, None])
+    tables = (cosine_table, sine_table, column, row)
+    block = shape((count, q_width), BF16)
+    low_rows, rows = shape((count, width), BF16), shape((count, width), F32)
+    qkv_width = q_width + 2 * k_width
 
     first_scale = rms_scale(tokens)
     first_hat = tokens * first_scale
     first_normed = (first_hat * attn_gain).astype(BF16)
     first_pieces = gather_ctx(first_normed)
-    cot_pieces = gather_ctx(after(cotangent[0], *first_pieces))
-
-    mixed, qkv, lse, send, *mine = call(
+    qkv_block = jnp.concatenate(
+        [own_columns(w_query, q_width, ctx), own_columns(w_key, k_width, ctx), own_columns(w_value, k_width, ctx)],
+        axis=1,
+    )
+    w_qkv = join_fsdp(spread_y(qkv_block), spread_y(move_y(qkv_block, 0, 1)))
+    out_other = move_y(w_out, 0, 1)
+    down_chunk = transpose_mesh(jnp.transpose(own_columns(w_down, width // 8, ctx)))
+    ffn_block = jnp.concatenate(
+        [own_columns(w_gate, ff_width, ctx), own_columns(w_up, ff_width, ctx), down_chunk], axis=1
+    )
+    first_pieces, w_qkv, tables, w_out, out_other, ffn_block, cot = stage(
+        first_pieces, w_qkv, tables, w_out, out_other, ffn_block, cotangent[0]
+    )
+
+    out_sides = (spread_y(w_out), spread_y(out_other))
+    cot_near = [move_z(cot, 1), move_z(cot, -1)]
+    qkv, lse, *mixed_blocks = call(
         attend_forward,
+        [shape((qkv_width, length), F32), shape((8, length), F32)] + [block] * 8,
+        (*first_pieces, w_qkv, *tables, *gains),
+        4 * 10**9,
+    )
+    mixed_blocks, out_sides, cot_near, ffn_block = stage(mixed_blocks, out_sides, cot_near, ffn_block)
+
+    ffn_other = move_y(ffn_block, 0, 1)
+    ffn_own = spread_y(ffn_block)
+    w_out_whole = join_fsdp(*out_sides)
+    own_blocks = exchange_ctx(mixed_blocks)
+    own_blocks, w_out_whole, ffn_other, cot = stage(own_blocks, w_out_whole, ffn_other, cot)
+    residual, second_normed = call(
+        out_project,
+        [rows, low_rows],
+        (owners, *own_blocks, w_out_whole, hidden_in[0], ffn_gain[None]),
+        3 * 10**8,
+        [pltpu.VMEM((count, width), BF16)],
+        1,
+    )
+
+    second_pieces = gather_ctx(second_normed)
+    ffn_sides = (ffn_own, spread_y(ffn_other))
+    cot_pieces = swap_pieces([cot, *cot_near, move_z(cot, 2)])
+    second_pieces, ffn_sides, cot_pieces = stage(second_pieces, ffn_sides, cot_pieces)
+    hidden, d_ffn, d_send, send, *parts = call(
+        ffn,
         [
-            shape((length, q_width), BF16),
-            shape((4 * head_size, length), F32),
-            shape((8, length), F32),
+            shape((length, ff_width), BF16),
+            shape((length, 2 * ff_width), BF16),
+            shape((4, count, width), BF16),
             shape((4, count, width), BF16),
         ]
-        + [shape((count, width), F32)] * 4,
-        (*first_pieces, w_qkv, out_rows, cosine_table, sine_table, column, row, *gains),
-        4 * 10**9,
-    )
-    received = swap_core(send)
-    residual = tokens + scatter_ctx(mine, received)
-    second_scale = rms_scale(residual)
-    second_hat = residual * second_scale
-    second_normed = (second_hat * ffn_gain).astype(BF16)
-    second_pieces = gather_ctx(second_normed)
-
-    hiddens, d_ffns, d_mine, d_received, mine, received = [], [], [], [], [], []
-    for group in range(4):
-        pair = slice(2 * group, 2 * group + 2)
-        hidden, d_ffn, own, other, block_own, block_other = call(
-            ffn_group,
-            [
-                shape((2 * count, ff_width), BF16),
-                shape((2 * count, 2 * ff_width), BF16),
-                shape((count, width), F32),
-                shape((count, width), BF16),
-                shape((count, width), F32),
-                shape((count, width), BF16),
-            ],
-            (*second_pieces[pair], *cot_pieces[pair], ffn_rows),
-            2 * 10**9,
-        )
-        hiddens.append(hidden)
-        d_ffns.append(d_ffn)
-        d_mine.append(own)
-        d_received.append(swap_core(other))
-        mine.append(block_own)
-        received.append(block_other)
+        + [rows] * 8,
+        (*second_pieces, *cot_pieces, join_fsdp(*ffn_sides)),
+        8 * 10**9,
+    )
+
+    d_mine, mine = parts[:4], parts[4:]
+    d_moves = start_scatter_ctx(d_mine, swap_core(d_send))
     ffn_partial = call(
         ffn_weights,
         [shape((count, 3 * ff_width), BF16)] * 8,
-        (place, *second_pieces, *cot_pieces, *hiddens, *d_ffns),
+        (place, *second_pieces, *cot_pieces, hidden, d_ffn),
         4 * 10**9,
-        [pltpu.VMEM((length, width), BF16), pltpu.VMEM((length, 2 * ff_width), BF16)],
+        [pltpu.VMEM((length, width), BF16)],
         1,
     )
-    d_moves = start_scatter_ctx(d_mine, d_received)
-    d_moves, ffn_partial = lax.optimization_barrier((d_moves, ffn_partial))
-    d_second = end_scatter(d_moves)
+    d_moves, ffn_partial, send = stage(d_moves, ffn_partial, send)
+    d_resid, d_attn, ffn_gain_part, *d_blocks = call(
+        resid_backward,
+        [rows, low_rows, shape((1, width), F32)] + [block] * 8,
+        (owners, *d_moves, residual, cot, ffn_gain[None], w_out_whole),
+        3 * 10**8,
+        [pltpu.VMEM((count, width), BF16)],
+        1,
+    )
+
     ffn_moved = start_sum_fsdp(ffn_partial)
-
-    d_from_second, ffn_gain_part = norm_back(d_second, second_hat, second_scale, ffn_gain)
-    d_resid = cotangent[0].astype(F32) + d_from_second
-    d_attn = d_resid.astype(BF16)
-    d_pieces = gather_ctx(d_attn)
-    received = [swap_core(part) for part in after(received, *d_pieces)]
-    block_moves = start_scatter_ctx(mine, received)
-    d_pieces, ffn_moved = lax.optimization_barrier((d_pieces, ffn_moved))
+    received = swap_core(send)
+    d_blocks = exchange_ctx(d_blocks)
+    d_blocks, ffn_moved, received, d_attn = stage(d_blocks, ffn_moved, received, d_attn)
+
+    d_near = [move_z(d_attn, 1), move_z(d_attn, -1)]
     ffn_sum = end_sum_fsdp(ffn_moved)
-    ffn_gate_up, ffn_down = ffn_sum[:, : 2 * ff_width], ffn_sum[:, 2 * ff_width :]
-    ffn_steps = [ffn_gate_up, swap_dp(ffn_gate_up), transpose_mesh(ffn_down), transpose_mesh(ffn_down, 1)]
-
-    qkv_width = q_width + 2 * k_width
-    q_gain_part, k_gain_part, attn_gain_part, send, *parts = call(
+    q_gain_part, k_gain_part, d_qkv, send, *d_first_mine = call(
         attend_backward,
         [
             shape((head_size, 1), F32),
             shape((head_size, 1), F32),
-            shape((width, 1), F32),
+            shape((length, qkv_width), BF16),
             shape((4, count, width), BF16),
         ]
-        + [shape((count, width), F32)] * 4
-        + [shape((count, qkv_width + q_width), BF16)] * 8,
-        (place, *first_pieces, *d_pieces, w_qkv, out_rows, cosine_table, sine_table, column, row, *gains, mixed, qkv, lse),
+        + [rows] * 4,
+        (*d_blocks, w_qkv, *tables, *gains, qkv, lse),
         8 * 10**9,
+        [pltpu.VMEM((qkv_width, length), F32)],
+    )
+    d_qkv, send, d_first_mine, d_near, ffn_sum, d_attn = stage(d_qkv, send, d_first_mine, d_near, ffn_sum, d_attn)
+
+    d_pieces = swap_pieces([d_attn, *d_near, move_z(d_attn, 2)])
+    ffn_gate_up, ffn_down = ffn_sum[:, : 2 * ff_width], ffn_sum[:, 2 * ff_width :]
+    ffn_steps = [ffn_gate_up, swap_dp(ffn_gate_up), transpose_mesh(ffn_down), transpose_mesh(ffn_down, 1)]
+    d_first_moves = start_scatter_ctx(d_first_mine, swap_core(send))
+    attn_gain_part, *attn_partial = call(
+        attend_weights,
+        [shape((1, width), F32)] + [shape((count, qkv_width + q_width), BF16)] * 8,
+        (place, *first_pieces, *d_pieces, *mixed_blocks, d_qkv, w_qkv),
+        10**9,
         [
             pltpu.VMEM((length, width), BF16),
-            pltpu.VMEM((length, width), BF16),
-            pltpu.VMEM((qkv_width, length), F32),
+            pltpu.VMEM((length, q_width), BF16),
             pltpu.VMEM((width, qkv_width + q_width), BF16),
         ],
         1,
     )
-    mine, attn_partial = parts[:4], parts[4:]
-    send, attn_partial, block_moves, ffn_steps = lax.optimization_barrier((send, attn_partial, block_moves, ffn_steps))
-    block_out = (residual + end_scatter(block_moves)).astype(BF16)
-    d_first = scatter_ctx(mine, swap_core(send))
-    d_from_first, _ = norm_back(d_first, first_hat, first_scale, attn_gain)
-    grad_in = (d_resid + d_from_first).astype(BF16)
+    attn_partial, attn_gain_part, ffn_steps, mine = stage(attn_partial, attn_gain_part, ffn_steps, mine)
 
     totals = sum_all(
         jnp.concatenate(
-            [
-                attn_gain_part[:, 0] / attn_gain,
-                jnp.sum(ffn_gain_part, axis=0),
-                q_gain_part[:, 0],
-                k_gain_part[:, 0],
-            ]
+            [attn_gain_part[0] / attn_gain, ffn_gain_part[0], q_gain_part[:, 0], k_gain_part[:, 0]]
         ).reshape(-1, 128)
     ).reshape(-1)
     grad_attn_gain = totals[:width]
     grad_ffn_gain = totals[width : 2 * width]
     grad_query_gain = totals[2 * width : 2 * width + head_size]
     grad_key_gain = totals[2 * width + head_size :]
-
+    attn_moved = start_sum_fsdp(attn_partial)
     ffn_steps = [step.astype(F32) for step in ffn_steps]
     ffn_parts = gather_ctx(
         jnp.concatenate([ffn_steps[0] + ffn_steps[1], ffn_steps[2] + ffn_steps[3]], axis=1).astype(BF16)
     )
-    attn_sum = end_sum_fsdp(start_sum_fsdp(attn_partial))
+    attn_sum = end_sum_fsdp(attn_moved)
+    d_from_first, _ = norm_back(end_scatter(d_first_moves), first_hat, first_scale, attn_gain)
+    grad_in = (d_resid + d_from_first).astype(BF16)
+    block_out = (residual + scatter_ctx(mine, received)).astype(BF16)
     attn_parts = gather_ctx(
         jnp.concatenate([sum_dp(attn_sum[:, :qkv_width]), sum_dp_transposed(attn_sum[:, qkv_width:])], axis=1)
     )

time: 431 us -> 421 us (0.977)
  waiting for transfers between devices: 147 us -> 98.2 us
  starting transfers between devices: 171 us -> 203 us
  local copies, waits for them, and re-layouts: 36.7 us -> 51.8 us
  other arithmetic: 21 us -> 13.3 us
    ppermute x33 -> x30, waiting for transfers between devices: 61 us -> 32.9 us  [move_z(): lax.ppermute(value, 'ctx', [(i, (i + 2 * step) % 8) for i in range(8)])]
    ppermute x32 -> x39, waiting for transfers between devices: 73.1 us -> 51.5 us  [move_y(): return lax.ppermute(value, 'fsdp', pairs)]
    ppermute x0 -> x14, starting transfers between devices: none -> 19.5 us  [exchange_ctx(): lax.ppermute(block, 'ctx', pairs)]
    ppermute x32 -> x39, starting transfers between devices: 63.9 us -> 80 us  [move_y(): return lax.ppermute(value, 'fsdp', pairs)]
    ppermute x35 -> x28, starting transfers between devices: 27.8 us -> 38.6 us  [swap_core(): return lax.ppermute(value, 'ctx', [(i, i ^ 1) for i in range(8)])]
    ppermute x6 -> x5, starting transfers between devices: 25.2 us -> 15.3 us  [transpose_mesh(): return lax.ppermute(value, ('dp', 'ctx', 'fsdp'), pairs)]
    unnamed x219 -> x207, local copies, waits for them, and re-layouts: 24.9 us -> 34.3 us
    dynamic_update_slice x15 -> x23, local copies, waits for them, and re-layouts: 0.34 us -> 7.55 us  [join_fsdp(): whole = lax.dynamic_update_slice_in_dim(whole, piece, owner * rows, 0)]
  transfers between devices with their start and end apart: 109 -> 119, of which waited for: 34 -> 37; matrix products, arithmetic and copies ran while one was open for 7% -> 5% of each run, Pallas kernels for 11% -> 7%
where the time goes in v3:
time: 421 us; the launch traced here: 415 us
  starting transfers between devices  203 us (48%)
  waiting for transfers between devices  98.2 us (23%)
  local copies, waits for them, and re-layouts  51.8 us (12%)
  Pallas kernels  46.4 us (11%)
  other arithmetic  13.3 us (3%)
    ppermute x39, starting transfers between devices, move_y(): return lax.ppermute(value, 'fsdp', pairs)  80 us
    ppermute x39, waiting for transfers between devices, move_y(): return lax.ppermute(value, 'fsdp', pairs)  51.5 us
    ppermute x30, starting transfers between devices, move_z(): lax.ppermute(value, 'ctx', [(i, (i + 2 * step) % 8) for i in range(8)])  47.5 us
    pallas_call x9, Pallas kernels, call(): pl.pallas_call(kernel, out_shape=out_shapes, in_specs=[smem] * scalars +...  46.4 us
    ppermute x28, starting transfers between devices, swap_core(): return lax.ppermute(value, 'ctx', [(i, i ^ 1) for i in range(8)])  38.6 us
    unnamed x207, local copies, waits for them, and re-layouts  34.3 us
    ppermute x30, waiting for transfers between devices, move_z(): lax.ppermute(value, 'ctx', [(i, (i + 2 * step) % 8) for i in range(8)])  32.9 us
    ppermute x14, starting transfers between devices, exchange_ctx(): lax.ppermute(block, 'ctx', pairs)  19.5 us
  transfers between devices with their start and end apart: 119, of which 37 were waited for; matrix products, arithmetic and copies ran while one was open for 5% of the time, Pallas kernels for 7%

profile of v3, /device:TPU:1, one launch (start us, length us, event | category | flops | bytes accessed | tf_op | source)
XLA Modules:
  0.0 415.4 jit_solution(12961597982384572839)
XLA Ops:
  3.5 4.5 %collective-permute-start.5 = (bf16[128,1024]{1,0:T(8,128)(2,1)S(1)}, bf16[128,1024]{1,0:T(8,128)(2,1)S(1)}, u32[]{:S(2)}, u32[]{:S(2)}) collective-permute-start(bf16[128,1024]{1,0:T(8,128)(2,1)S(1)} %fusion.3.refs_0_.refs_1_), channel_id=1, source_target_pairs={{0,32},{8,40},{16,48},{24,56},{32,0},{40,8},{48,16},{56,24},{1,33}... | collective-permute-start | bytes 786440 | tf_op jit(solution)/shard_map/ppermute | solution.py:310
  26.4 5.8 %collective-permute-start.15 = (bf16[128,576]{1,0:T(8,128)(2,1)S(1)}, bf16[128,576]{1,0:T(8,128)(2,1)}, u32[]{:S(2)}, u32[]{:S(2)}) collective-permute-start(bf16[128,576]{1,0:T(8,128)(2,1)S(1)} %bitcast.111), channel_id=1, source_target_pairs={{0,0},{1,8},{2,16},{3,24},{4,32},{5,40},{6,48},{7,56},{8,1},{9,9},... | collective-permute-start | bytes 442376 | tf_op jit(solution)/shard_map/ppermute | solution.py:360
  32.3 3.8 collective-permute-start.12
  37.6 5.6 %collective-permute-done.11 = bf16[128,256]{1,0:T(8,128)(2,1)S(1)} collective-permute-done((bf16[128,256]{1,0:T(8,128)(2,1)S(1)}, bf16[128,256]{1,0:T(8,128)(2,1)S(1)}, u32[]{:S(2)}, u32[]{:S(2)}) %collective-permute-start.11) | collective-permute-done | bytes 65568 | tf_op jit(solution)/shard_map/ppermute | solution.py:373
  49.0 6.1 %collective-permute-done.14 = bf16[128,1024]{1,0:T(8,128)(2,1)} collective-permute-done((bf16[128,1024]{1,0:T(8,128)(2,1)}, bf16[128,1024]{1,0:T(8,128)(2,1)}, u32[]{:S(2)}, u32[]{:S(2)}) %collective-permute-start.14) | collective-permute-done | bytes 262176 | tf_op jit(solution)/shard_map/ppermute | solution.py:373
  56.8 4.4 %collective-permute-start.23 = (bf16[128,1024]{1,0:T(8,128)(2,1)}, bf16[128,1024]{1,0:T(8,128)(2,1)}, u32[]{:S(2)}, u32[]{:S(2)}) collective-permute-start(bf16[128,1024]{1,0:T(8,128)(2,1)} %bitcast.22.refs_8_.refs_9_.refs_5_), channel_id=1, source_target_pairs={{0,48},{8,56},{16,0},{24,8},{32,16},{40,24},{48,32},{56,40},{1,49}... | collective-permute-start | bytes 786440 | tf_op jit(solution)/shard_map/ppermute | solution.py:310
  71.2 10.8 %collective-permute-start.19 = (bf16[128,1024]{1,0:T(8,128)(2,1)}, bf16[128,1024]{1,0:T(8,128)(2,1)S(1)}, u32[]{:S(2)}, u32[]{:S(2)}) collective-permute-start(bf16[128,1024]{1,0:T(8,128)(2,1)} %collective-permute-done.14), channel_id=1, source_target_pairs={{0,2},{1,3},{2,4},{3,5},{4,6},{5,7},{6,0},{7,1},{8,10},{9,11},{10,... | collective-permute-start | bytes 786440 | tf_op jit(solution)/shard_map/ppermute | solution.py:373
  83.9 7.5 %shard_map.237 = (f32[256,1024]{1,0:T(8,128)S(1)}, f32[8,1024]{1,0:T(8,128)S(1)}, bf16[128,128]{1,0:T(8,128)(2,1)S(1)}, bf16[128,128]{1,0:T(8,128)(2,1)S(1)}, bf...) custom-call(bf16[128,1024]{1,0:T(8,128)(2,1)S(1)} %fusion.3.refs_0_., ...), custom_call_target="tpu_custom_call" | custom-call | flops 4000000000 | bytes 5280256 | tf_op jit(solution)/shard_map/pallas_call | solution.py:36
  121.9 5.3 %collective-permute-done.40 = bf16[128,1728]{1,0:T(8,128)(2,1)} collective-permute-done((bf16[128,1728]{1,0:T(8,128)(2,1)}, bf16[128,1728]{1,0:T(8,128)(2,1)}, u32[]{:S(2)}, u32[]{:S(2)}) %collective-permute-start.40) | collective-permute-done | bytes 442400 | tf_op jit(solution)/shard_map/ppermute | solution.py:373
  135.0 4.2 collective-permute-done.33.refs_2_.refs_3_
  144.6 6.9 %collective-permute-done.43 = bf16[128,1728]{1,0:T(8,128)(2,1)S(1)} collective-permute-done((bf16[128,1728]{1,0:T(8,128)(2,1)S(1)}, bf16[128,1728]{1,0:T(8,128)(2,1)S(1)}, u32[]{:S(2)}, u32[]{:S(2)}) %collective-permute-start.43) | collective-permute-done | bytes 442400 | tf_op jit(solution)/shard_map/ppermute | solution.py:373
  161.2 12.0 %shard_map.239 = (bf16[1024,576]{1,0:T(8,128)(2,1)S(1)}, bf16[1024,1152]{1,0:T(8,128)(2,1)S(1)}, bf16[4,128,1024]{2,1,0:T(8,128)(2,1)S(1)}, bf16[4,128,1024]{2,1...) custom-call(bf16[128,1024]{1,0:T(8,128)(2,1)S(1)} %get-tuple-element, ...), custom_call_target="tpu_custom_call" | custom-call | flops 8000000000 | bytes 17563648 | tf_op jit(solution)/shard_map/pallas_call | solution.py:36
  180.7 6.2 %shard_map.240 = (bf16[128,1728]{1,0:T(8,128)(2,1)S(1)}, bf16[128,1728]{1,0:T(8,128)(2,1)S(1)}, bf16[128,1728]{1,0:T(8,128)(2,1)S(1)}, bf16[128,1728]{1,0:T(8,12...) custom-call(s32[2]{0:T(128)S(1)} %pad_add_fusion.refs_0_, ...), custom_call_target="tpu_custom_call" | custom-call | flops 4000000000 | bytes 11272200 | tf_op jit(solution)/shard_map/pallas_call | solution.py:36
  186.9 5.3 %collective-permute-done.53.refs_3_ = bf16[128,1024]{1,0:T(8,128)(2,1)S(1)} collective-permute-done((bf16[128,1024]{1,0:T(8,128)(2,1)S(1)}, bf16[128,1024]{1,0:T(8,128)(2,1)S(1)}, u32[]{:S(2)}, u32[]{:S(2)}) %collective-permute-start.53) | collective-permute-done | bytes 262176 | tf_op jit(solution)/shard_map/ppermute | solution.py:310
  218.2 3.4 collective-permute-done.63
  221.7 9.8 %collective-permute-done.64 = bf16[128,1728]{1,0:T(8,128)(2,1)S(1)} collective-permute-done((bf16[128,1728]{1,0:T(8,128)(2,1)S(1)}, bf16[128,1728]{1,0:T(8,128)(2,1)S(1)}, u32[]{:S(2)}, u32[]{:S(2)}) %collective-permute-start.64) | collective-permute-done | bytes 442400 | tf_op jit(solution)/shard_map/ppermute | solution.py:373
  231.5 5.5 %collective-permute-done.66 = bf16[128,1728]{1,0:T(8,128)(2,1)S(1)} collective-permute-done((bf16[128,1728]{1,0:T(8,128)(2,1)S(1)}, bf16[128,1728]{1,0:T(8,128)(2,1)S(1)}, u32[]{:S(2)}, u32[]{:S(2)}) %collective-permute-start.66) | collective-permute-done | bytes 442400 | tf_op jit(solution)/shard_map/ppermute | solution.py:373
  239.1 3.2 collective-permute-start.70
  242.4 8.2 %shard_map.242 = (f32[64,1]{1,0:T(8,128)S(1)}, f32[64,1]{1,0:T(8,128)S(1)}, bf16[1024,256]{1,0:T(8,128)(2,1)S(1)}, bf16[4,128,1024]{2,1,0:T(8,128)(2,1)S(1)}, f3...) custom-call(bf16[128,128]{1,0:T(8,128)(2,1)S(1)} %get-tuple-element.328.refs, ...), custom_call_target="tpu_custom_call" | custom-call | flops 8000000000 | bytes 6853632 | tf_op jit(solution)/shard_map/pallas_call | solution.py:36
  255.9 3.9 collective-permute-start.72
  261.8 4.8 %collective-permute-start.75 = (bf16[128,1024]{1,0:T(8,128)(2,1)}, bf16[128,1024]{1,0:T(8,128)(2,1)}, u32[]{:S(2)}, u32[]{:S(2)}) collective-permute-start(bf16[128,1024]{1,0:T(8,128)(2,1)} %collective-permute-done.74.refs_15_), channel_id=1, source_target_pairs={{0,8},{8,0},{16,24},{24,16},{32,40},{40,32},{48,56},{56,48},{1,9},... | collective-permute-start | bytes 786440 | tf_op jit(solution)/shard_map/ppermute | solution.py:306
  270.5 4.4 %collective-permute-start.77 = (bf16[128,576]{1,0:T(8,128)(2,1)}, bf16[128,576]{1,0:T(8,128)(2,1)}, u32[]{:S(2)}, u32[]{:S(2)}) collective-permute-start(bf16[128,576]{1,0:T(8,128)(2,1)} %slice.31), channel_id=1, source_target_pairs={{0,0},{1,8},{2,16},{3,24},{4,32},{5,40},{6,48},{7,56},{8,1},{9,9},... | collective-permute-start | bytes 442376 | tf_op jit(solution)/shard_map/ppermute | solution.py:360
  295.4 18.5 %collective-permute-start.95 = (bf16[128,384]{1,0:T(8,128)(2,1)}, bf16[128,384]{1,0:T(8,128)(2,1)S(1)}, u32[]{:S(2)}, u32[]{:S(2)}) collective-permute-start(bf16[128,384]{1,0:T(8,128)(2,1)} %copy-done.86), channel_id=1, source_target_pairs={{0,2},{1,3},{2,4},{3,5},{4,6},{5,7},{6,0},{7,1},{8,10},{9,11},{10,... | collective-permute-start | bytes 294920 | tf_op jit(solution)/shard_map/ppermute | solution.py:373
  313.8 3.3 collective-permute-start.96
  338.5 5.1 %collective-permute-start.82 = (bf16[4,128,1024]{2,1,0:T(8,128)(2,1)}, bf16[4,128,1024]{2,1,0:T(8,128)(2,1)S(1)}, u32[]{:S(2)}, u32[]{:S(2)}) collective-permute-start(bf16[4,128,1024]{2,1,0:T(8,128)(2,1)} %copy-done.81), channel_id=1, source_target_pairs={{0,8},{8,0},{16,24},{24,16},{32,40},{40,32},{48,56},{56,48},{1,9},... | collective-permute-start | bytes 3145736 | tf_op jit(solution)/shard_map/ppermute | solution.py:306
  349.6 3.8 collective-permute-start.103
  354.9 6.2 %collective-permute-start.79 = (bf16[128,1024]{1,0:T(8,128)(2,1)S(1)}, bf16[128,1024]{1,0:T(8,128)(2,1)S(1)}, u32[]{:S(2)}, u32[]{:S(2)}) collective-permute-start(bf16[128,1024]{1,0:T(8,128)(2,1)S(1)} %get-tuple-element.412), channel_id=1, source_target_pairs={{0,32},{8,40},{16,48},{24,56},{32,0},{40,8},{48,16},{56,24},{1,33}... | collective-permute-start | bytes 786440 | tf_op jit(solution)/shard_map/ppermute | solution.py:310
  364.7 5.2 %collective-permute-start.80 = (bf16[128,1024]{1,0:T(8,128)(2,1)S(1)}, bf16[128,1024]{1,0:T(8,128)(2,1)S(1)}, u32[]{:S(2)}, u32[]{:S(2)}) collective-permute-start(bf16[128,1024]{1,0:T(8,128)(2,1)S(1)} %get-tuple-element.414), channel_id=1, source_target_pairs={{0,48},{8,56},{16,0},{24,8},{32,16},{40,24},{48,32},{56,40},{1,49}... | collective-permute-start | bytes 786440 | tf_op jit(solution)/shard_map/ppermute | solution.py:310
  373.6 4.4 %collective-permute-done.80 = bf16[128,1024]{1,0:T(8,128)(2,1)S(1)} collective-permute-done((bf16[128,1024]{1,0:T(8,128)(2,1)S(1)}, bf16[128,1024]{1,0:T(8,128)(2,1)S(1)}, u32[]{:S(2)}, u32[]{:S(2)}) %collective-permute-start.80) | collective-permute-done | bytes 262176 | tf_op jit(solution)/shard_map/ppermute | solution.py:310
  399.5 4.2 %collective-permute-start.118 = (bf16[128,1728]{1,0:T(8,128)(2,1)S(1)}, bf16[128,1728]{1,0:T(8,128)(2,1)S(1)}, u32[]{:S(2)}, u32[]{:S(2)}) collective-permute-start(bf16[128,1728]{1,0:T(8,128)(2,1)S(1)} %collective-permute-done.117.refs_7_), channel_id=1, source_target_pairs={{0,8},{8,0},{16,24},{24,16},{32,40},{40,32},{48,56},{56,48},{1,9},... | collective-permute-start | bytes 1327112 | tf_op jit(solution)/shard_map/ppermute | solution.py:306
  404.8 3.5 collective-permute-done.85
  410.7 4.5 %shard_map.245 = (f32[128,4608]{1,0:T(8,128)}, f32[128,4608]{1,0:T(8,128)}, f32[576,1024]{1,0:T(8,128)}) custom-call(s32[8]{0:T(128)S(1)} %stack.62.order.refs_0_, bf16[128,1728]{1,0:T(8,128)(2,1)S(1)} %pad_maximum_fusion.refs_1_, bf16[128,1728]{1,0:T(8,128)(2,1)S(1)} %collective-permute-done.112.refs_2_, ...), custom_call_target="tpu_custom_call" | custom-call | flops 1000000 | bytes 10616864 | tf_op jit(solution)/shard_map/pallas_call | solution.py:36
  (501 shorter events, 222.8 us)
Async XLA Ops:
  3.5 42.8 %collective-permute-start.5 = (bf16[128,1024]{1,0:T(8,128)(2,1)S(1)}, bf16[128,1024]{1,0:T(8,128)(2,1)S(1)}, u32[]{:S(2)}, u32[]{:S(2)}) collective-permute-start(bf16[128,1024]{1,0:T(8,128)(2,1)S(1)} %fusion.3.refs_0_.refs_1_), channel_id=1, source_target_pairs={{0,32},{8,40},{16,48},{24,56},{32,0},{40,8},{48,16},{56,24},{1,33}... | collective-permute-start | bytes 786440 | tf_op jit(solution)/shard_map/ppermute | solution.py:310
  8.0 38.5 %collective-permute-start.3 = (bf16[128,1024]{1,0:T(8,128)(2,1)S(1)}, bf16[128,1024]{1,0:T(8,128)(2,1)S(1)}, u32[]{:S(2)}, u32[]{:S(2)}) collective-permute-start(bf16[128,1024]{1,0:T(8,128)(2,1)S(1)} %fusion.3.refs_0_.refs_1_), channel_id=1, source_target_pairs={{0,48},{8,56},{16,0},{24,8},{32,16},{40,24},{48,32},{56,40},{1,49}... | collective-permute-start | bytes 786440 | tf_op jit(solution)/shard_map/ppermute | solution.py:310
  8.5 38.3 %collective-permute-start.1 = (bf16[128,1024]{1,0:T(8,128)(2,1)S(1)}, bf16[128,1024]{1,0:T(8,128)(2,1)S(1)}, u32[]{:S(2)}, u32[]{:S(2)}) collective-permute-start(bf16[128,1024]{1,0:T(8,128)(2,1)S(1)} %fusion.3.refs_0_.refs_1_), channel_id=1, source_target_pairs={{0,16},{8,24},{16,32},{24,40},{32,48},{40,56},{48,0},{56,8},{1,17}... | collective-permute-start | bytes 786440 | tf_op jit(solution)/shard_map/ppermute | solution.py:310
  26.4 18.9 %collective-permute-start.15 = (bf16[128,576]{1,0:T(8,128)(2,1)S(1)}, bf16[128,576]{1,0:T(8,128)(2,1)}, u32[]{:S(2)}, u32[]{:S(2)}) collective-permute-start(bf16[128,576]{1,0:T(8,128)(2,1)S(1)} %bitcast.111), channel_id=1, source_target_pairs={{0,0},{1,8},{2,16},{3,24},{4,32},{5,40},{6,48},{7,56},{8,1},{9,9},... | collective-permute-start | bytes 442376 | tf_op jit(solution)/shard_map/ppermute | solution.py:360
  62.2 29.4 %collective-permute-start.17 = (bf16[128,1024]{1,0:T(8,128)(2,1)}, bf16[128,1024]{1,0:T(8,128)(2,1)S(1)}, u32[]{:S(2)}, u32[]{:S(2)}) collective-permute-start(bf16[128,1024]{1,0:T(8,128)(2,1)} %param.23), channel_id=1, source_target_pairs={{0,6},{1,7},{2,0},{3,1},{4,2},{5,3},{6,4},{7,5},{8,14},{9,15},{10,... | collective-permute-start | bytes 786440 | tf_op jit(solution)/shard_map/ppermute | solution.py:373
  63.2 28.4 %collective-permute-start.16 = (bf16[128,1024]{1,0:T(8,128)(2,1)}, bf16[128,1024]{1,0:T(8,128)(2,1)S(1)}, u32[]{:S(2)}, u32[]{:S(2)}) collective-permute-start(bf16[128,1024]{1,0:T(8,128)(2,1)} %param.23), channel_id=1, source_target_pairs={{0,2},{1,3},{2,4},{3,5},{4,6},{5,7},{6,0},{7,1},{8,10},{9,11},{10,... | collective-permute-start | bytes 786440 | tf_op jit(solution)/shard_map/ppermute | solution.py:373
  66.3 25.3 %collective-permute-start.21 = (bf16[128,1024]{1,0:T(8,128)(2,1)}, bf16[128,1024]{1,0:T(8,128)(2,1)S(1)}, u32[]{:S(2)}, u32[]{:S(2)}) collective-permute-start(bf16[128,1024]{1,0:T(8,128)(2,1)} %collective-permute-done.14), channel_id=1, source_target_pairs={{0,4},{1,5},{2,6},{3,7},{4,0},{5,1},{6,2},{7,3},{8,12},{9,13},{10,... | collective-permute-start | bytes 786440 | tf_op jit(solution)/shard_map/ppermute | solution.py:373
  69.4 22.2 %collective-permute-start.20 = (bf16[128,1024]{1,0:T(8,128)(2,1)}, bf16[128,1024]{1,0:T(8,128)(2,1)S(1)}, u32[]{:S(2)}, u32[]{:S(2)}) collective-permute-start(bf16[128,1024]{1,0:T(8,128)(2,1)} %collective-permute-done.14), channel_id=1, source_target_pairs={{0,6},{1,7},{2,0},{3,1},{4,2},{5,3},{6,4},{7,5},{8,14},{9,15},{10,... | collective-permute-start | bytes 786440 | tf_op jit(solution)/shard_map/ppermute | solution.py:373
  71.2 20.4 %collective-permute-start.19 = (bf16[128,1024]{1,0:T(8,128)(2,1)}, bf16[128,1024]{1,0:T(8,128)(2,1)S(1)}, u32[]{:S(2)}, u32[]{:S(2)}) collective-permute-start(bf16[128,1024]{1,0:T(8,128)(2,1)} %collective-permute-done.14), channel_id=1, source_target_pairs={{0,2},{1,3},{2,4},{3,5},{4,6},{5,7},{6,0},{7,1},{8,10},{9,11},{10,... | collective-permute-start | bytes 786440 | tf_op jit(solution)/shard_map/ppermute | solution.py:373
  102.7 18.0 %collective-permute-start.41 = (bf16[128,1728]{1,0:T(8,128)(2,1)}, bf16[128,1728]{1,0:T(8,128)(2,1)}, u32[]{:S(2)}, u32[]{:S(2)}) collective-permute-start(bf16[128,1728]{1,0:T(8,128)(2,1)} %concatenate.36), channel_id=1, source_target_pairs={{0,4},{1,5},{2,6},{3,7},{4,0},{5,1},{6,2},{7,3},{8,12},{9,13},{10,... | collective-permute-start | bytes 1327112 | tf_op jit(solution)/shard_map/ppermute | solution.py:373
  110.6 16.7 %collective-permute-start.40 = (bf16[128,1728]{1,0:T(8,128)(2,1)}, bf16[128,1728]{1,0:T(8,128)(2,1)}, u32[]{:S(2)}, u32[]{:S(2)}) collective-permute-start(bf16[128,1728]{1,0:T(8,128)(2,1)} %concatenate.36), channel_id=1, source_target_pairs={{0,6},{1,7},{2,0},{3,1},{4,2},{5,3},{6,4},{7,5},{8,14},{9,15},{10,... | collective-permute-start | bytes 1327112 | tf_op jit(solution)/shard_map/ppermute | solution.py:373
  112.2 16.5 %collective-permute-start.39 = (bf16[128,1728]{1,0:T(8,128)(2,1)}, bf16[128,1728]{1,0:T(8,128)(2,1)}, u32[]{:S(2)}, u32[]{:S(2)}) collective-permute-start(bf16[128,1728]{1,0:T(8,128)(2,1)} %concatenate.36), channel_id=1, source_target_pairs={{0,2},{1,3},{2,4},{3,5},{4,6},{5,7},{6,0},{7,1},{8,10},{9,11},{10,... | collective-permute-start | bytes 1327112 | tf_op jit(solution)/shard_map/ppermute | solution.py:373
  130.0 21.5 %collective-permute-start.43 = (bf16[128,1728]{1,0:T(8,128)(2,1)S(1)}, bf16[128,1728]{1,0:T(8,128)(2,1)S(1)}, u32[]{:S(2)}, u32[]{:S(2)}) collective-permute-start(bf16[128,1728]{1,0:T(8,128)(2,1)S(1)} %copy-done.96), channel_id=1, source_target_pairs={{0,6},{1,7},{2,0},{3,1},{4,2},{5,3},{6,4},{7,5},{8,14},{9,15},{10,... | collective-permute-start | bytes 1327112 | tf_op jit(solution)/shard_map/ppermute | solution.py:373
  134.5 19.0 %collective-permute-start.42 = (bf16[128,1728]{1,0:T(8,128)(2,1)S(1)}, bf16[128,1728]{1,0:T(8,128)(2,1)S(1)}, u32[]{:S(2)}, u32[]{:S(2)}) collective-permute-start(bf16[128,1728]{1,0:T(8,128)(2,1)S(1)} %copy-done.96), channel_id=1, source_target_pairs={{0,2},{1,3},{2,4},{3,5},{4,6},{5,7},{6,0},{7,1},{8,10},{9,11},{10,... | collective-permute-start | bytes 1327112 | tf_op jit(solution)/shard_map/ppermute | solution.py:373
  192.3 44.7 %collective-permute-start.67 = (bf16[4,128,1024]{2,1,0:T(8,128)(2,1)S(1)}, bf16[4,128,1024]{2,1,0:T(8,128)(2,1)}, u32[]{:S(2)}, u32[]{:S(2)}) collective-permute-start(bf16[4,128,1024]{2,1,0:T(8,128)(2,1)S(1)} %get-tuple-element.326), channel_id=1, source_target_pairs={{0,8},{8,0},{16,24},{24,16},{32,40},{40,32},{48,56},{56,48},{1,9},... | collective-permute-start | bytes 3145736 | tf_op jit(solution)/shard_map/ppermute | solution.py:306
  193.5 21.8 %collective-permute-start.61 = (bf16[128,1728]{1,0:T(8,128)(2,1)S(1)}, bf16[128,1728]{1,0:T(8,128)(2,1)S(1)}, u32[]{:S(2)}, u32[]{:S(2)}) collective-permute-start(bf16[128,1728]{1,0:T(8,128)(2,1)S(1)} %get-tuple-element.318), channel_id=1, source_target_pairs={{0,2},{1,3},{2,4},{3,5},{4,6},{5,7},{6,0},{7,1},{8,10},{9,11},{10,... | collective-permute-start | bytes 1327112 | tf_op jit(solution)/shard_map/ppermute | solution.py:373
  193.7 23.7 %collective-permute-start.62 = (bf16[128,1728]{1,0:T(8,128)(2,1)S(1)}, bf16[128,1728]{1,0:T(8,128)(2,1)S(1)}, u32[]{:S(2)}, u32[]{:S(2)}) collective-permute-start(bf16[128,1728]{1,0:T(8,128)(2,1)S(1)} %get-tuple-element.319), channel_id=1, source_target_pairs={{0,2},{1,3},{2,4},{3,5},{4,6},{5,7},{6,0},{7,1},{8,10},{9,11},{10,... | collective-permute-start | bytes 1327112 | tf_op jit(solution)/shard_map/ppermute | solution.py:373
  212.9 18.6 %collective-permute-start.64 = (bf16[128,1728]{1,0:T(8,128)(2,1)S(1)}, bf16[128,1728]{1,0:T(8,128)(2,1)S(1)}, u32[]{:S(2)}, u32[]{:S(2)}) collective-permute-start(bf16[128,1728]{1,0:T(8,128)(2,1)S(1)} %get-tuple-element.321), channel_id=1, source_target_pairs={{0,6},{1,7},{2,0},{3,1},{4,2},{5,3},{6,4},{7,5},{8,14},{9,15},{10,... | collective-permute-start | bytes 1327112 | tf_op jit(solution)/shard_map/ppermute | solution.py:373
  217.3 19.6 %collective-permute-start.66 = (bf16[128,1728]{1,0:T(8,128)(2,1)S(1)}, bf16[128,1728]{1,0:T(8,128)(2,1)S(1)}, u32[]{:S(2)}, u32[]{:S(2)}) collective-permute-start(bf16[128,1728]{1,0:T(8,128)(2,1)S(1)} %get-tuple-element.323), channel_id=1, source_target_pairs={{0,4},{1,5},{2,6},{3,7},{4,0},{5,1},{6,2},{7,3},{8,12},{9,13},{10,... | collective-permute-start | bytes 1327112 | tf_op jit(solution)/shard_map/ppermute | solution.py:373
  237.0 17.2 %collective-permute-start.69 = (bf16[128,1024]{1,0:T(8,128)(2,1)}, bf16[128,1024]{1,0:T(8,128)(2,1)S(1)}, u32[]{:S(2)}, u32[]{:S(2)}) collective-permute-start(bf16[128,1024]{1,0:T(8,128)(2,1)} %get-tuple-element.353.refs_9_), channel_id=1, source_target_pairs={{0,48},{8,56},{16,0},{24,8},{32,16},{40,24},{48,32},{56,40},{1,49}... | collective-permute-start | bytes 786440 | tf_op jit(solution)/shard_map/ppermute | solution.py:310
  267.3 26.8 %collective-permute-start.76 = (bf16[128,1152]{1,0:T(8,128)(2,1)}, bf16[128,1152]{1,0:T(8,128)(2,1)}, u32[]{:S(2)}, u32[]{:S(2)}) collective-permute-start(bf16[128,1152]{1,0:T(8,128)(2,1)} %slice.30), channel_id=1, source_target_pairs={{0,64},{64,0},{1,65},{65,1},{2,66},{66,2},{3,67},{67,3},{4,68},{68... | collective-permute-start | bytes 884744 | tf_op jit(solution)/shard_map/ppermute | solution.py:364
  269.8 24.3 %collective-permute-start.78 = (bf16[128,576]{1,0:T(8,128)(2,1)}, bf16[128,576]{1,0:T(8,128)(2,1)}, u32[]{:S(2)}, u32[]{:S(2)}) collective-permute-start(bf16[128,576]{1,0:T(8,128)(2,1)} %slice.31), channel_id=1, source_target_pairs={{0,64},{1,72},{2,80},{3,88},{4,96},{5,104},{6,112},{7,120},{8,65},... | collective-permute-start | bytes 442376 | tf_op jit(solution)/shard_map/ppermute | solution.py:360
  270.5 23.6 %collective-permute-start.77 = (bf16[128,576]{1,0:T(8,128)(2,1)}, bf16[128,576]{1,0:T(8,128)(2,1)}, u32[]{:S(2)}, u32[]{:S(2)}) collective-permute-start(bf16[128,576]{1,0:T(8,128)(2,1)} %slice.31), channel_id=1, source_target_pairs={{0,0},{1,8},{2,16},{3,24},{4,32},{5,40},{6,48},{7,56},{8,1},{9,9},... | collective-permute-start | bytes 442376 | tf_op jit(solution)/shard_map/ppermute | solution.py:360
  295.0 22.2 %collective-permute-start.86 = (f32[17,128]{1,0:T(8,128)S(1)}, f32[17,128]{1,0:T(8,128)S(1)}, u32[]{:S(2)}, u32[]{:S(2)}) collective-permute-start(f32[17,128]{1,0:T(8,128)S(1)} %bitcast.112), channel_id=1, source_target_pairs={{0,8},{8,0},{16,24},{24,16},{32,40},{40,32},{48,56},{56,48},{1,9},... | collective-permute-start | bytes 26120 | tf_op jit(solution)/shard_map/ppermute | solution.py:306
  295.4 48.2 %collective-permute-start.95 = (bf16[128,384]{1,0:T(8,128)(2,1)}, bf16[128,384]{1,0:T(8,128)(2,1)S(1)}, u32[]{:S(2)}, u32[]{:S(2)}) collective-permute-start(bf16[128,384]{1,0:T(8,128)(2,1)} %copy-done.86), channel_id=1, source_target_pairs={{0,2},{1,3},{2,4},{3,5},{4,6},{5,7},{6,0},{7,1},{8,10},{9,11},{10,... | collective-permute-start | bytes 294920 | tf_op jit(solution)/shard_map/ppermute | solution.py:373
  313.8 31.5 %collective-permute-start.96 = (bf16[128,384]{1,0:T(8,128)(2,1)}, bf16[128,384]{1,0:T(8,128)(2,1)S(1)}, u32[]{:S(2)}, u32[]{:S(2)}) collective-permute-start(bf16[128,384]{1,0:T(8,128)(2,1)} %copy-done.85), channel_id=1, source_target_pairs={{0,6},{1,7},{2,0},{3,1},{4,2},{5,3},{6,4},{7,5},{8,14},{9,15},{10,... | collective-permute-start | bytes 294920 | tf_op jit(solution)/shard_map/ppermute | solution.py:373
  338.5 45.9 %collective-permute-start.82 = (bf16[4,128,1024]{2,1,0:T(8,128)(2,1)}, bf16[4,128,1024]{2,1,0:T(8,128)(2,1)S(1)}, u32[]{:S(2)}, u32[]{:S(2)}) collective-permute-start(bf16[4,128,1024]{2,1,0:T(8,128)(2,1)} %copy-done.81), channel_id=1, source_target_pairs={{0,8},{8,0},{16,24},{24,16},{32,40},{40,32},{48,56},{56,48},{1,9},... | collective-permute-start | bytes 3145736 | tf_op jit(solution)/shard_map/ppermute | solution.py:306
  343.6 40.5 %collective-permute-start.117 = (bf16[128,1728]{1,0:T(8,128)(2,1)S(1)}, bf16[128,1728]{1,0:T(8,128)(2,1)S(1)}, u32[]{:S(2)}, u32[]{:S(2)}) collective-permute-start(bf16[128,1728]{1,0:T(8,128)(2,1)S(1)} %pad_maximum_fusion.refs_1_), channel_id=1, source_target_pairs={{0,32},{8,40},{16,48},{24,56},{32,0},{40,8},{48,16},{56,24},{1,33}... | collective-permute-start | bytes 1327112 | tf_op jit(solution)/shard_map/ppermute | solution.py:310
  379.5 18.5 %collective-permute-start.115 = (bf16[128,1728]{1,0:T(8,128)(2,1)S(1)}, bf16[128,1728]{1,0:T(8,128)(2,1)S(1)}, u32[]{:S(2)}, u32[]{:S(2)}) collective-permute-start(bf16[128,1728]{1,0:T(8,128)(2,1)S(1)} %pad_maximum_fusion.refs_1_), channel_id=1, source_target_pairs={{0,48},{8,56},{16,0},{24,8},{32,16},{40,24},{48,32},{56,40},{1,49}... | collective-permute-start | bytes 1327112 | tf_op jit(solution)/shard_map/ppermute | solution.py:310
  385.2 18.5 %collective-permute-start.83 = (bf16[128,1024]{1,0:T(8,128)(2,1)S(1)}, bf16[128,1024]{1,0:T(8,128)(2,1)S(1)}, u32[]{:S(2)}, u32[]{:S(2)}) collective-permute-start(bf16[128,1024]{1,0:T(8,128)(2,1)S(1)} %get-tuple-element.409), channel_id=1, source_target_pairs={{0,32},{8,40},{16,48},{24,56},{32,0},{40,8},{48,16},{56,24},{1,33}... | collective-permute-start | bytes 786440 | tf_op jit(solution)/shard_map/ppermute | solution.py:310
  388.4 19.9 %collective-permute-start.85 = (bf16[128,1024]{1,0:T(8,128)(2,1)S(1)}, bf16[128,1024]{1,0:T(8,128)(2,1)S(1)}, u32[]{:S(2)}, u32[]{:S(2)}) collective-permute-start(bf16[128,1024]{1,0:T(8,128)(2,1)S(1)} %get-tuple-element.410), channel_id=1, source_target_pairs={{0,16},{8,24},{16,32},{24,40},{32,48},{40,56},{48,0},{56,8},{1,17}... | collective-permute-start | bytes 786440 | tf_op jit(solution)/shard_map/ppermute | solution.py:310
  388.6 20.7 %collective-permute-start.84 = (bf16[128,1024]{1,0:T(8,128)(2,1)S(1)}, bf16[128,1024]{1,0:T(8,128)(2,1)S(1)}, u32[]{:S(2)}, u32[]{:S(2)}) collective-permute-start(bf16[128,1024]{1,0:T(8,128)(2,1)S(1)} %get-tuple-element.411), channel_id=1, source_target_pairs={{0,48},{8,56},{16,0},{24,8},{32,16},{40,24},{48,32},{56,40},{1,49}... | collective-permute-start | bytes 786440 | tf_op jit(solution)/shard_map/ppermute | solution.py:310
  (190 other events, 2473.2 us)

commit v4 on v3

v4 whole, which is shorter than its diff:
```python
import math

import jax
import jax.numpy as jnp
from jax import lax
from jax.experimental import pallas as pl
from jax.experimental.pallas import tpu as pltpu
from jax.sharding import PartitionSpec as P

NORM_EPSILON = 1e-05
ROPE_BASE = 1000000.0
MASKED_SCORE = -1e30
BF16 = jnp.bfloat16
F32 = jnp.float32
STEPS = (0, -1, 1, 2)


def rms_scale(values):
    return lax.rsqrt(jnp.mean(values * values, axis=-1, keepdims=True) + NORM_EPSILON)


def rope_tables(places, head_size):
    half_width = head_size // 2
    pair_index = jnp.arange(half_width, dtype=F32)
    frequency = ROPE_BASE ** (-2.0 * pair_index / head_size)
    angles = frequency[:, None] * places.astype(F32)[None, :]
    return jnp.cos(angles), jnp.sin(angles)


def call(kernel, out_shapes, args, flops, scratch=(), scalars=0):
    vmem = pl.BlockSpec(memory_space=pltpu.VMEM)
    smem = pl.BlockSpec(memory_space=pltpu.SMEM)
    out_bytes = sum(math.prod(o.shape) * o.dtype.itemsize for o in out_shapes)
    in_bytes = sum(math.prod(a.shape) * a.dtype.itemsize for a in args)
    return pl.pallas_call(
        kernel,
        out_shape=out_shapes,
        in_specs=[smem] * scalars + [vmem] * (len(args) - scalars),
        out_specs=[vmem] * len(out_shapes),
        scratch_shapes=list(scratch),
        compiler_params=pltpu.CompilerParams(vmem_limit_bytes=40 * 2**20),
        cost_estimate=pl.CostEstimate(flops=flops, bytes_accessed=in_bytes + out_bytes, transcendentals=0),
    )(*args)


def shape(dims, kind):
    return jax.ShapeDtypeStruct(dims, kind)


def head_forward(values, gain, cosine, sine):
    scale = lax.rsqrt(jnp.mean(values * values, axis=0, keepdims=True) + NORM_EPSILON)
    hat = values * scale
    normed = hat * gain
    half = values.shape[0] // 2
    front, back = normed[:half], normed[half:]
    rotated = jnp.concatenate([front * cosine - back * sine, back * cosine + front * sine], axis=0)
    return scale, hat, rotated


def head_backward(grads, hat, scale, gain, cosine, sine):
    half = grads.shape[0] // 2
    front, back = grads[:half], grads[half:]
    d_normed = jnp.concatenate([front * cosine + back * sine, back * cosine - front * sine], axis=0)
    scaled = d_normed * gain
    inner = jnp.mean(hat * scaled, axis=0, keepdims=True)
    return scale * (scaled - hat * inner), jnp.sum(d_normed * hat, axis=1, keepdims=True)


def norm_back(d_normed, normed_hat, scale_values, gain_vector):
    scaled = d_normed * gain_vector
    inner = jnp.mean(normed_hat * scaled, axis=-1, keepdims=True)
    return (scale_values * (scaled - normed_hat * inner), d_normed * normed_hat)


def mm(left, right):
    return jnp.dot(left, right, preferred_element_type=F32)


def mm_t(left, right):
    return lax.dot_general(left, right, (((1,), (1,)), ((), ())), preferred_element_type=F32)


def outer_sum(left, right):
    return lax.dot_general(left, right, (((0,), (0,)), ((), ())), preferred_element_type=F32)


def swap_core(value):
    return lax.ppermute(value, "ctx", [(i, i ^ 1) for i in range(8)])


def move_z(value, step):
    return lax.ppermute(value, "ctx", [(i, (i + 2 * step) % 8) for i in range(8)])


def gather_ctx(block):
    pieces = []
    for step in STEPS:
        mine = block if step == 0 else move_z(block, -step)
        pieces += [mine, swap_core(mine)]
    return pieces


def start_scatter_ctx(mine, received):
    sums = [own + other.astype(F32) for own, other in zip(mine, received)]
    return [sums[0]] + [move_z(sums[slot].astype(BF16), STEPS[slot]) for slot in (3, 1, 2)]


def exchange_ctx(blocks):
    out = [None] * 8
    for i, step in enumerate(STEPS):
        back = (0, 2, 1, 3)[i]
        for flip in (0, 1):
            pairs = [(c, (c // 2 + step) % 4 * 2 + (c % 2 ^ flip)) for c in range(8)]
            block = blocks[2 * i + flip]
            out[2 * back + flip] = lax.ppermute(block, "ctx", pairs) if step or flip else block
    return out


def stage(*values):
    return lax.optimization_barrier(values)


def transpose_mesh(value, flip=0):
    pairs = [
        ((d * 8 + c) * 8 + f, ((d ^ flip) * 8 + f) * 8 + c) for d in range(2) for c in range(8) for f in range(8)
    ]
    return lax.ppermute(value, ("dp", "ctx", "fsdp"), pairs)


def swap_dp(value):
    return lax.ppermute(value, "dp", [(0, 1), (1, 0)])


def move_y(value, step, flip=0):
    pairs = [(y * 2 + x, (y + step) % 4 * 2 + (x ^ flip)) for y in range(4) for x in range(2)]
    return lax.ppermute(value, "fsdp", pairs)


def pair_x(block):
    other = move_y(block, 0, 1)
    first = lax.axis_index("fsdp") % 2 == 0
    return jnp.concatenate([jnp.where(first, block, other), jnp.where(first, other, block)], axis=0)


def spread_y(pair):
    return [pair] + [move_y(pair, step) for step in (1, 3, 2)]


def join_y(pairs):
    y = lax.axis_index("fsdp") // 2
    rows, columns = pairs[0].shape
    whole = jnp.zeros((4 * rows, columns), BF16)
    for step, pair in zip((0, 1, 3, 2), pairs):
        whole = lax.dynamic_update_slice_in_dim(whole, pair, (y - step) % 4 * rows, 0)
    return whole


def all_to_all(blocks, axis):
    return lax.all_to_all(blocks, axis, split_axis=0, concat_axis=0, tiled=True)


def own_columns(weight, width, index):
    return lax.dynamic_slice_in_dim(weight, index * width, width, 1)


def attend_forward(*refs):
    pieces, refs = refs[:8], refs[8:]
    w_qkv, cos_ref, sin_ref, column_ref, row_ref, q_gain, k_gain = refs[:7]
    qkv_ref, lse_ref, *mixed_refs = refs[7:]
    length = qkv_ref.shape[1]
    count = length // 8
    head = q_gain.shape[0]
    for pair in range(4):
        x = jnp.concatenate([pieces[2 * pair][...], pieces[2 * pair + 1][...]], axis=0)
        qkv_ref[:, pair * 2 * count : (pair + 1) * 2 * count] = jnp.transpose(mm(x, w_qkv[...]))
    cosine, sine = cos_ref[...], sin_ref[...]
    queries = [
        head_forward(qkv_ref[h * head : (h + 1) * head], q_gain[...], cosine, sine)[2].astype(BF16) * BF16(head**-0.5)
        for h in range(2)
    ]
    key = jnp.transpose(head_forward(qkv_ref[2 * head : 3 * head], k_gain[...], cosine, sine)[2]).astype(BF16)
    value = qkv_ref[3 * head :].astype(BF16)
    width = column_ref.shape[1]
    for tile in range(length // width):
        lanes = slice(tile * width, (tile + 1) * width)
        allowed = column_ref[...] <= row_ref[:, lanes]
        outs = []
        for h in range(2):
            scores = jnp.where(allowed, mm(key, queries[h][:, lanes]), MASKED_SCORE)
            top = jnp.max(scores, axis=0, keepdims=True)
            weights = jnp.exp(scores - top)
            total = jnp.sum(weights, axis=0, keepdims=True)
            lse_ref[h : h + 1, lanes] = top + jnp.log(total)
            outs.append(mm(value, (weights * (1.0 / total)).astype(BF16)))
        mixed = jnp.transpose(jnp.concatenate(outs, axis=0)).astype(BF16)
        mixed_refs[2 * tile][...] = mixed[:count]
        mixed_refs[2 * tile + 1][...] = mixed[count:]


def out_project(order, *refs):
    blocks, (w_out, tokens, gain, resid_ref, normed_ref, mixed_ref) = refs[:8], refs[8:]
    count = blocks[0].shape[1]
    for i in range(8):
        mixed_ref[:, pl.ds(pl.multiple_of(order[i] * count, count), count)] = blocks[i][...]
    resid = tokens[...].astype(F32) + mm(mixed_ref[...], w_out[...])
    resid_ref[...] = resid
    normed_ref[...] = (resid * rms_scale(resid) * gain[...]).astype(BF16)


def resid_backward(order, *refs):
    total, move_a, move_b, move_c, resid_ref, cot_ref, gain_ref, w_out = refs[:8]
    d_resid_ref, d_attn_ref, gain_part_ref = refs[8:11]
    block_refs, d_mixed_ref = refs[11:19], refs[19]
    d_second = total[...] + move_a[...].astype(F32) + move_b[...].astype(F32) + move_c[...].astype(F32)
    resid = resid_ref[...]
    scale = rms_scale(resid)
    d_from, gain_part = norm_back(d_second, resid * scale, scale, gain_ref[...])
    gain_part_ref[...] = jnp.sum(gain_part, axis=0, keepdims=True)
    d_resid = cot_ref[...].astype(F32) + d_from
    d_resid_ref[...] = d_resid
    d_attn = d_resid.astype(BF16)
    d_attn_ref[...] = d_attn
    d_mixed_ref[...] = mm_t(d_attn, w_out[...]).astype(BF16)
    count = block_refs[0].shape[1]
    for i in range(8):
        block_refs[i][...] = d_mixed_ref[:, pl.ds(pl.multiple_of(order[i] * count, count), count)]


def attend_backward(*refs):
    order, d_blocks, refs = refs[0], refs[1:9], refs[9:]
    w_qkv, cos_ref, sin_ref, column_ref, row_ref, q_gain, k_gain, qkv_ref, lse_ref = refs[:9]
    q_gain_ref, k_gain_ref, d_low_ref, d_first_ref, d_qkv_ref = refs[9:]
    length = qkv_ref.shape[1]
    head = q_gain.shape[0]
    count = length // 8
    cosine, sine = cos_ref[...], sin_ref[...]
    scales, hats, queries = [], [], []
    for h in range(2):
        scale, hat, rotated = head_forward(qkv_ref[h * head : (h + 1) * head], q_gain[...], cosine, sine)
        scales.append(scale)
        hats.append(hat)
        queries.append(rotated.astype(BF16) * BF16(head**-0.5))
    k_scale, k_hat, rotated = head_forward(qkv_ref[2 * head : 3 * head], k_gain[...], cosine, sine)
    key_rows = rotated.astype(BF16)
    key = jnp.transpose(rotated).astype(BF16)
    value = jnp.transpose(qkv_ref[3 * head :]).astype(BF16)
    width = column_ref.shape[1]
    d_key = jnp.zeros((length, head), F32)
    d_value = jnp.zeros((length, head), F32)
    for tile in range(length // width):
        lanes = slice(tile * width, (tile + 1) * width)
        allowed = column_ref[...] <= row_ref[:, lanes]
        d_mixed = jnp.concatenate([d_blocks[2 * tile][...], d_blocks[2 * tile + 1][...]], axis=0)
        d_mixed = jnp.transpose(d_mixed.astype(F32)).astype(BF16)
        for h in range(2):
            rows = slice(h * head, (h + 1) * head)
            query = queries[h][:, lanes]
            probs = jnp.where(allowed, jnp.exp(mm(key, query) - lse_ref[h : h + 1, lanes]), 0.0)
            d_probs = mm(value, d_mixed[rows])
            inner = jnp.sum(probs * d_probs, axis=0, keepdims=True)
            d_scores = (probs * (d_probs - inner)).astype(BF16)
            d_value += mm_t(probs.astype(BF16), d_mixed[rows])
            d_key += mm_t(d_scores, query)
            d_qkv_ref[rows, lanes] = mm(key_rows, d_scores) * head**-0.5
    for h in range(2):
        rows = slice(h * head, (h + 1) * head)
        d_query, gain_part = head_backward(d_qkv_ref[rows], hats[h], scales[h], q_gain[...], cosine, sine)
        d_qkv_ref[rows] = d_query
        if h == 0:
            q_gain_ref[...] = gain_part
        else:
            q_gain_ref[...] += gain_part
    d_keys, gain_part = head_backward(jnp.transpose(d_key), k_hat, k_scale, k_gain[...], cosine, sine)
    k_gain_ref[...] = gain_part
    d_qkv_ref[2 * head : 3 * head] = d_keys
    d_qkv_ref[3 * head :] = jnp.transpose(d_value)
    for tile in range(4):
        lanes = slice(tile * 2 * count, (tile + 1) * 2 * count)
        d_qkv = jnp.transpose(d_qkv_ref[:, lanes]).astype(BF16)
        d_low_ref[lanes] = d_qkv
        d_first = mm_t(d_qkv, w_qkv[...])
        d_first_ref[order[2 * tile]] = d_first[:count].astype(BF16)
        d_first_ref[order[2 * tile + 1]] = d_first[count:].astype(BF16)


def attend_weights(*refs):
    pieces, d_pieces, blocks = refs[:8], refs[8:16], refs[16:24]
    d_low_ref, w_qkv, attn_gain, ffn_part, q_part, k_part = refs[24:30]
    out_ref, x_ref, mixed_ref = refs[30:]
    count = pieces[0].shape[0]
    width = d_low_ref.shape[1]
    for i in range(8):
        x_ref[i * count : (i + 1) * count] = pieces[i][...]
        mixed_ref[i * count : (i + 1) * count] = blocks[i][...]
    grad_qkv = outer_sum(d_low_ref[...], x_ref[...])
    attn_part = jnp.sum(grad_qkv * jnp.transpose(w_qkv[...].astype(F32)), axis=0, keepdims=True) / attn_gain[...]
    grad_qkv = jnp.transpose(grad_qkv).astype(BF16)
    for i in range(8):
        x_ref[i * count : (i + 1) * count] = d_pieces[i][...]
    grad_out = jnp.transpose(outer_sum(mixed_ref[...], x_ref[...])).astype(BF16)
    lines = [part[:, i * 128 : (i + 1) * 128] for part in (attn_part, ffn_part[...]) for i in range(8)]
    lines.append(jnp.concatenate([jnp.transpose(q_part[...]), jnp.transpose(k_part[...])], axis=1))
    gains = jnp.concatenate(lines + [jnp.zeros((7, 128), F32)], axis=0)
    high = gains.astype(BF16)
    low = (gains - high.astype(F32)).astype(BF16)
    gains = jnp.concatenate([high, low, jnp.zeros((count - 48, 128), BF16)], axis=0)
    for i in range(8):
        rows = slice(i * count, (i + 1) * count)
        out_ref[i, :, :width] = grad_qkv[rows]
        out_ref[i, :, width : width + 128] = gains
        out_ref[i, :, width + 128 :] = grad_out[rows]


def ffn(*refs):
    order, seconds, cots, gate_up, down = refs[0], refs[1:9], refs[9], refs[10], refs[11]
    hidden_ref, d_ffn_ref, block_ref, d_send = refs[12:16]
    d_mine = refs[16:20]
    width = hidden_ref.shape[1]
    count = seconds[0].shape[0]
    for group in (3, 1, 2, 0):
        rows = slice(2 * group * count, 2 * (group + 1) * count)
        x = jnp.concatenate([seconds[2 * group][...], seconds[2 * group + 1][...]], axis=0)
        cot = jnp.concatenate([cots[order[2 * group]], cots[order[2 * group + 1]]], axis=0)
        both = mm(x, gate_up[...])
        gate, up = both[:, :width], both[:, width:]
        sigmoid = 1.0 / (1.0 + jnp.exp(-gate))
        act = gate * sigmoid
        hidden = (act * up).astype(BF16)
        hidden_ref[rows] = hidden
        d_hidden = mm(cot, down[...])
        d_gate = d_hidden * up * sigmoid * (1.0 + gate * (1.0 - sigmoid))
        d_ffn = jnp.concatenate([d_gate, d_hidden * act], axis=1).astype(BF16)
        d_ffn_ref[rows] = d_ffn
        d_second = mm_t(d_ffn, gate_up[...])
        d_mine[group][...] = d_second[:count]
        d_send[group] = d_second[count:].astype(BF16)
        out = mm_t(hidden, down[...])
        block_ref[order[2 * group]] = out[:count].astype(BF16)
        block_ref[order[2 * group + 1]] = out[count:].astype(BF16)


def ffn_weights(*refs):
    order, seconds, cots, hidden_ref, d_ffn_ref, out_ref, x_ref = refs[0], refs[1:9], *refs[9:]
    count = seconds[0].shape[0]
    for lhs, other_ref, columns in ((0, d_ffn_ref, 0), (1, hidden_ref, d_ffn_ref.shape[1])):
        for i in range(8):
            x_ref[i * count : (i + 1) * count] = cots[order[i]] if lhs else seconds[i][...]
        width = other_ref.shape[1]
        for pair in range(4):
            both = outer_sum(x_ref[:, 2 * pair * count : 2 * (pair + 1) * count], other_ref[...]).astype(BF16)
            out_ref[2 * pair, :, columns : columns + width] = both[:count]
            out_ref[2 * pair + 1, :, columns : columns + width] = both[count:]
    used = d_ffn_ref.shape[1] + hidden_ref.shape[1]
    out_ref[:, :, used:] = jnp.zeros((8, count, out_ref.shape[2] - used), BF16)


def sum_ffn(parts, gate_up_ref, down_ref):
    width = gate_up_ref.shape[1]
    total = sum(parts[i].astype(F32) for i in range(8)).astype(BF16)
    gate_up_ref[...] = total[:, :width]
    down_ref[...] = total[:, width : width + down_ref.shape[1]]


def sum_attn(parts, first_ref, out_ref):
    count = out_ref.shape[0]
    width = first_ref.shape[1] - 128
    total = sum(parts[i].astype(F32) for i in range(8))
    first_ref[:, :width] = total[:, :width].astype(BF16)
    pack_gains(first_ref, width, total[:24, width : width + 128] + total[24:48, width : width + 128])
    out_ref[...] = total[:, width + 128 :].astype(BF16)


def pack_gains(ref, width, gains):
    high = gains.astype(BF16)
    low = (gains - high.astype(F32)).astype(BF16)
    rest = jnp.zeros((ref.shape[0] - 48, 128), BF16)
    ref[:, width : width + 128] = jnp.concatenate([high, low, rest], axis=0)


def join_ffn(own, other, down, down_other, out_ref):
    width = own.shape[1]
    out_ref[:, :width] = (own[...].astype(F32) + other[...].astype(F32)).astype(BF16)
    out_ref[:, width:] = (down[...].astype(F32) + down_other[...].astype(F32)).astype(BF16)


def join_attn(own, other, out, out_other, out_ref):
    width = own.shape[1] - 128
    total = own[...].astype(F32) + other[...].astype(F32)
    out_ref[:, :width] = total[:, :width].astype(BF16)
    pack_gains(out_ref, width, total[:24, width:] + total[24:48, width:])
    out_ref[:, width + 128 :] = (out[...].astype(F32) + out_other[...].astype(F32)).astype(BF16)


def assemble_ffn(*refs):
    order, pieces, (gate_ref, up_ref, down_ref, held) = refs[0], refs[1:9], refs[9:]
    width = down_ref.shape[0]
    count = pieces[0].shape[0]
    for i in range(8):
        held[order[i]] = pieces[i][...]
    for owner in range(8):
        columns = slice(owner * width, (owner + 1) * width)
        gate_ref[:, columns] = held[owner, :, :width].astype(F32)
        up_ref[:, columns] = held[owner, :, width : 2 * width].astype(F32)
        down = held[owner, :, 2 * width :].astype(F32)
        down_ref[:, owner * count : (owner + 1) * count] = jnp.transpose(down)


def assemble_attn(*refs):
    order, pieces, (query_ref, key_ref, value_ref, out_ref, gains_ref, held) = refs[0], refs[1:9], refs[9:]
    count = pieces[0].shape[0]
    half = count // 2
    for i in range(8):
        held[order[i]] = pieces[i][...]
    gains = jnp.zeros(gains_ref.shape, F32)
    for owner in range(8):
        columns = slice(owner * count, (owner + 1) * count)
        narrow = slice(owner * half, (owner + 1) * half)
        part = held[owner].astype(F32)
        query_ref[:, columns] = part[:, :count]
        key_ref[:, narrow] = part[:, count : count + half]
        value_ref[:, narrow] = part[:, count + half : 2 * count]
        out_ref[:, columns] = jnp.transpose(part[:, 3 * count :])
        gains += part[:24, 2 * count : 3 * count] + part[24:48, 2 * count : 3 * count]
    gains_ref[...] = gains


def body(
    hidden_in,
    positions,
    cotangent,
    attn_gain,
    w_query,
    w_key,
    w_value,
    query_gain,
    key_gain,
    w_out,
    ffn_gain,
    w_gate,
    w_up,
    w_down,
):
    ctx = lax.axis_index("ctx")
    tokens = hidden_in[0].astype(F32)
    count, width = tokens.shape
    head_size = query_gain.shape[0]
    q_width = w_query.shape[1] // 8
    k_width = w_key.shape[1] // 8
    ff_width = w_gate.shape[1] // 8

    z_index, core = ctx // 2, ctx % 2
    owners = jnp.stack(
        [((z_index + step) % 4) * 2 + (core ^ flip) for step in STEPS for flip in (0, 1)]
    )
    places = positions[0].reshape(8, count)[owners].reshape(8 * count)
    length = 8 * count
    cosine_table, sine_table = rope_tables(places, head_size)
    column = jnp.broadcast_to(places[:, None], (length, 2 * count))
    row = places[None]
    gains = (query_gain[:, None], key_gain[:, None])
    tables = (cosine_table, sine_table, column, row)
    block = shape((count, q_width), BF16)
    low_rows, rows = shape((count, width), BF16), shape((count, width), F32)
    qkv_width = q_width + 2 * k_width

    first_scale = rms_scale(tokens)
    first_hat = tokens * first_scale
    first_normed = (first_hat * attn_gain).astype(BF16)
    gate_up = lax.all_gather(
        jnp.concatenate([own_columns(w_gate, ff_width, ctx), own_columns(w_up, ff_width, ctx)], axis=1),
        "fsdp",
        axis=0,
        tiled=True,
    )
    first_pieces = gather_ctx(first_normed)
    qkv_block = jnp.concatenate(
        [own_columns(w_query, q_width, ctx), own_columns(w_key, k_width, ctx), own_columns(w_value, k_width, ctx)],
        axis=1,
    )
    w_qkv = join_y(spread_y(pair_x(qkv_block)))
    out_pair = pair_x(w_out)
    cot = cotangent[0]
    first_pieces, w_qkv, tables, out_pair, cot, w_down = stage(first_pieces, w_qkv, tables, out_pair, cot, w_down)

    cots = all_to_all(jnp.broadcast_to(cot[None], (8, count, width)), "ctx")
    out_pairs = spread_y(out_pair)
    down_chunk = transpose_mesh(jnp.transpose(own_columns(w_down, width // 8, ctx)))
    qkv, lse, *mixed_blocks = call(
        attend_forward,
        [shape((qkv_width, length), F32), shape((8, length), F32)] + [block] * 8,
        (*first_pieces, w_qkv, *tables, *gains),
        4 * 10**9,
    )
    mixed_blocks, out_pairs, down_chunk = stage(mixed_blocks, out_pairs, down_chunk)

    own_blocks = exchange_ctx(mixed_blocks)
    own_blocks, down_chunk = stage(own_blocks, down_chunk)
    residual, second_normed = call(
        out_project,
        [rows, low_rows],
        (owners, *own_blocks, join_y(out_pairs), hidden_in[0], ffn_gain[None]),
        3 * 10**8,
        [pltpu.VMEM((count, width), BF16)],
        1,
    )

    second_pieces = gather_ctx(second_normed)
    down_t = join_y(spread_y(pair_x(down_chunk)))
    hidden, d_ffn, block_parts, d_send, *d_mine = call(
        ffn,
        [
            shape((length, ff_width), BF16),
            shape((length, 2 * ff_width), BF16),
            shape((8, count, width), BF16),
            shape((4, count, width), BF16),
        ]
        + [rows] * 4,
        (owners, *second_pieces, cots, gate_up, down_t),
        8 * 10**9,
        (),
        1,
    )

    d_moves = start_scatter_ctx(d_mine, swap_core(d_send))
    padded = -(-3 * ff_width // 128) * 128
    (ffn_partial,) = call(
        ffn_weights,
        [shape((8, count, padded), BF16)],
        (owners, *second_pieces, cots, hidden, d_ffn),
        4 * 10**9,
        [pltpu.VMEM((length, width), BF16)],
        1,
    )
    d_moves, ffn_partial = stage(d_moves, ffn_partial)
    ffn_sums = all_to_all(ffn_partial, "fsdp")
    block_sum = lax.psum_scatter(block_parts, "ctx", scatter_dimension=0, tiled=False)
    block_out = (residual + block_sum.astype(F32)).astype(BF16)
    d_resid, d_attn, ffn_gain_part, *d_blocks = call(
        resid_backward,
        [rows, low_rows, shape((1, width), F32)] + [block] * 8,
        (owners, *d_moves, residual, cot, ffn_gain[None], join_y(out_pairs)),
        3 * 10**8,
        [pltpu.VMEM((count, width), BF16)],
        1,
    )

    d_blocks = exchange_ctx(d_blocks)
    d_blocks, d_attn = stage(d_blocks, d_attn)

    d_pieces = gather_ctx(d_attn)
    q_gain_part, k_gain_part, d_qkv, d_first_parts = call(
        attend_backward,
        [
            shape((head_size, 1), F32),
            shape((head_size, 1), F32),
            shape((length, qkv_width), BF16),
            shape((8, count, width), BF16),
        ],
        (owners, *d_blocks, w_qkv, *tables, *gains, qkv, lse),
        8 * 10**9,
        [pltpu.VMEM((qkv_width, length), F32)],
        1,
    )
    d_first = lax.psum_scatter(d_first_parts, "ctx", scatter_dimension=0, tiled=False).astype(F32)
    (attn_partial,) = call(
        attend_weights,
        [shape((8, count, qkv_width + 128 + q_width), BF16)],
        (*first_pieces, *d_pieces, *mixed_blocks, d_qkv, w_qkv, attn_gain[None], ffn_gain_part, q_gain_part, k_gain_part),
        10**9,
        [pltpu.VMEM((length, width), BF16), pltpu.VMEM((length, q_width), BF16)],
    )

    attn_sums = all_to_all(attn_partial, "fsdp")
    own, down = call(
        sum_ffn, [shape((count, 2 * ff_width), BF16), shape((count, ff_width), BF16)], (ffn_sums,), 10**6
    )
    (joined,) = call(
        join_ffn,
        [shape((count, 3 * ff_width), BF16)],
        (own, swap_dp(own), transpose_mesh(down), transpose_mesh(down, 1)),
        10**6,
    )
    ffn_parts = gather_ctx(joined)
    own, out = call(
        sum_attn, [shape((count, qkv_width + 128), BF16), shape((count, q_width), BF16)], (attn_sums,), 10**6
    )
    (joined,) = call(
        join_attn,
        [shape((count, qkv_width + 128 + q_width), BF16)],
        (own, swap_dp(own), transpose_mesh(out), transpose_mesh(out, 1)),
        10**6,
    )
    attn_parts = gather_ctx(joined)
    d_from_first, _ = norm_back(d_first, first_hat, first_scale, attn_gain)
    grad_in = (d_resid + d_from_first).astype(BF16)
    grad_gate, grad_up, grad_down = call(
        assemble_ffn,
        [shape((count, 8 * ff_width), F32)] * 2 + [shape((ff_width, width), F32)],
        (owners, *ffn_parts),
        10**6,
        [pltpu.VMEM((8, count, 3 * ff_width), BF16)],
        1,
    )
    grad_query, grad_key, grad_value, grad_out, totals = call(
        assemble_attn,
        [shape((count, width), F32)] + [shape((count, 8 * k_width), F32)] * 2 + [shape((q_width, width), F32), shape((24, 128), F32)],
        (owners, *attn_parts),
        10**6,
        [pltpu.VMEM((8, count, qkv_width + 128 + q_width), BF16)],
        1,
    )
    totals = totals.reshape(-1)
    grad_attn_gain = totals[:width]
    grad_ffn_gain = totals[width : 2 * width]
    grad_query_gain = totals[2 * width : 2 * width + head_size]
    grad_key_gain = totals[2 * width + head_size : 2 * width + 2 * head_size]
    return (
        block_out[None],
        grad_in[None],
        grad_attn_gain,
        grad_query,
        grad_key,
        grad_value,
        grad_query_gain,
        grad_key_gain,
        grad_out,
        grad_ffn_gain,
        grad_gate,
        grad_up,
        grad_down,
    )


def solution(mesh):
    in_specs = (
        P(("dp", "fsdp"), "ctx", None),
        P(("dp", "fsdp"), None),
        P(("dp", "fsdp"), "ctx", None),
        P(),
        P("fsdp", None),
        P("fsdp", None),
        P("fsdp", None),
        P(),
        P(),
        P("fsdp", None),
        P(),
        P("fsdp", None),
        P("fsdp", None),
        P("fsdp", None),
    )
    out_specs = (
        P(("dp", "fsdp"), "ctx", None),
        P(("dp", "fsdp"), "ctx", None),
        P(),
        P("fsdp", None),
        P("fsdp", None),
        P("fsdp", None),
        P(),
        P(),
        P("fsdp", None),
        P(),
        P("fsdp", None),
        P("fsdp", None),
        P("fsdp", None),
    )
    return jax.shard_map(body, mesh=mesh, in_specs=in_specs, out_specs=out_specs, check_vma=False)
```

time: 421 us -> 392 us (0.931)
  starting transfers between devices: 203 us -> 143 us
  waiting for transfers between devices: 98.2 us -> 114 us
  between operations: 2.29 us -> 15.2 us
    ppermute x39 -> x12, starting transfers between devices: 80 us -> 16.6 us  [move_y(): return lax.ppermute(value, 'fsdp', pairs)]
    ppermute x5, waiting for transfers between devices: 0.01 us -> 44.8 us  [transpose_mesh(): return lax.ppermute(value, ('dp', 'ctx', 'fsdp'), pairs)]
    ppermute x39 -> x12, waiting for transfers between devices: 51.5 us -> 17.1 us  [move_y(): return lax.ppermute(value, 'fsdp', pairs)]
    all_to_all x0 -> x3, waiting for transfers between devices: none -> 16 us  [all_to_all(): return lax.all_to_all(blocks, axis, split_axis=0, concat_axis=0, tiled=True)]
    all_to_all x0 -> x3, starting transfers between devices: none -> 14.8 us  [all_to_all(): return lax.all_to_all(blocks, axis, split_axis=0, concat_axis=0, tiled=True)]
    ppermute x30 -> x18, starting transfers between devices: 47.5 us -> 37.2 us  [move_z(): lax.ppermute(value, 'ctx', [(i, (i + 2 * step) % 8) for i in range(8)])]
    ppermute x30 -> x18, waiting for transfers between devices: 32.9 us -> 27.6 us  [move_z(): lax.ppermute(value, 'ctx', [(i, (i + 2 * step) % 8) for i in range(8)])]
    pallas_call x9 -> x13, Pallas kernels: 46.4 us -> 49.3 us  [call(): pl.pallas_call(kernel, out_shape=out_shapes, in_specs=[smem] * scalars +...]
  transfers between devices with their start and end apart: 119 -> 78, of which waited for: 37 -> 28; matrix products, arithmetic and copies ran while one was open for 5% -> 7% of each run, Pallas kernels for 7% -> 8%
where the time goes in v4:
time: 392 us; the launch traced here: 385 us
  starting transfers between devices  143 us (36%)
  waiting for transfers between devices  114 us (29%)
  local copies, waits for them, and re-layouts  50.1 us (13%)
  Pallas kernels  49.3 us (13%)
  between operations  15.2 us (4%)
  other arithmetic  13.3 us (3%)
    pallas_call x13, Pallas kernels, call(): pl.pallas_call(kernel, out_shape=out_shapes, in_specs=[smem] * scalars +...  49.3 us
    ppermute x5, waiting for transfers between devices, transpose_mesh(): return lax.ppermute(value, ('dp', 'ctx', 'fsdp'), pairs)  44.8 us
    ppermute x21, starting transfers between devices, swap_core(): return lax.ppermute(value, 'ctx', [(i, i ^ 1) for i in range(8)])  38.4 us
    ppermute x18, starting transfers between devices, move_z(): lax.ppermute(value, 'ctx', [(i, (i + 2 * step) % 8) for i in range(8)])  37.2 us
    unnamed x180, local copies, waits for them, and re-layouts  34 us
    ppermute x18, waiting for transfers between devices, move_z(): lax.ppermute(value, 'ctx', [(i, (i + 2 * step) % 8) for i in range(8)])  27.6 us
    ppermute x14, starting transfers between devices, exchange_ctx(): lax.ppermute(block, 'ctx', pairs)  20 us
    ppermute x12, waiting for transfers between devices, move_y(): return lax.ppermute(value, 'fsdp', pairs)  17.1 us
  transfers between devices with their start and end apart: 78, of which 28 were waited for; matrix products, arithmetic and copies ran while one was open for 7% of the time, Pallas kernels for 8%

profile of v4, /device:TPU:1, one launch (start us, length us, event | category | flops | bytes accessed | tf_op | source)
XLA Modules:
  0.0 384.6 jit_solution(5253448645410363998)
XLA Ops:
  9.5 4.5 %collective-permute-start.5 = (bf16[128,1024]{1,0:T(8,128)(2,1)S(1)}, bf16[128,1024]{1,0:T(8,128)(2,1)S(1)}, u32[]{:S(2)}, u32[]{:S(2)}) collective-permute-start(bf16[128,1024]{1,0:T(8,128)(2,1)S(1)} %fusion.3.refs_0_), channel_id=1, source_target_pairs={{0,32},{8,40},{16,48},{24,56},{32,0},{40,8},{48,16},{56,24},{1,33}... | collective-permute-start | bytes 786440 | tf_op jit(solution)/shard_map/ppermute | solution.py:92
  28.2 3.0 collective-permute-start.11
  33.3 3.7 collective-permute-done.10
  37.0 9.1 %collective-permute-start = (bf16[128,1024]{1,0:T(8,128)(2,1)S(1)}, bf16[128,1024]{1,0:T(8,128)(2,1)S(1)}, u32[]{:S(2)}, u32[]{:S(2)}) collective-permute-start(bf16[128,1024]{1,0:T(8,128)(2,1)S(1)} %fusion.3.refs_0_), channel_id=1, source_target_pairs={{0,8},{8,0},{16,24},{24,16},{32,40},{40,32},{48,56},{56,48},{1,9},... | collective-permute-start | bytes 786440 | tf_op jit(solution)/shard_map/ppermute | solution.py:88
  62.3 6.8 %all-to-all-start = ((bf16[8,128,1024]{2,1,0:T(8,128)(2,1)}), bf16[8,128,1024]{2,1,0:T(8,128)(2,1)}, u32[]{:S(2)}, u32[]{:S(2)}) async-start(bf16[8,128,1024]{2,1,0:T(8,128)(2,1)} %broadcast_in_dim.48), calls=%async_computation | async-start | bytes 4194304 | tf_op jit(solution)/shard_map/all_to_all | solution.py:159
  74.5 7.5 %shard_map.237 = (f32[256,1024]{1,0:T(8,128)S(1)}, f32[8,1024]{1,0:T(8,128)S(1)}, bf16[128,128]{1,0:T(8,128)(2,1)S(1)}, bf16[128,128]{1,0:T(8,128)(2,1)S(1)}, bf...) custom-call(bf16[128,1024]{1,0:T(8,128)(2,1)S(1)} %fusion.3.refs_0_,, ...), custom_call_target="tpu_custom_call" | custom-call | flops 4000000000 | bytes 5280256 | tf_op jit(solution)/shard_map/pallas_call | solution.py:35
  83.1 4.0 %collective-permute-done.13 = bf16[256,1024]{1,0:T(8,128)(2,1)} collective-permute-done((bf16[256,1024]{1,0:T(8,128)(2,1)}, bf16[256,1024]{1,0:T(8,128)(2,1)}, u32[]{:S(2)}, u32[]{:S(2)}) %collective-permute-start.13) | collective-permute-done | bytes 524320 | tf_op jit(solution)/shard_map/ppermute | solution.py:136
  87.0 4.6 %collective-permute-done.12 = bf16[256,1024]{1,0:T(8,128)(2,1)} collective-permute-done((bf16[256,1024]{1,0:T(8,128)(2,1)}, bf16[256,1024]{1,0:T(8,128)(2,1)}, u32[]{:S(2)}, u32[]{:S(2)}) %collective-permute-start.12) | collective-permute-done | bytes 524320 | tf_op jit(solution)/shard_map/ppermute | solution.py:136
  94.4 3.3 collective-permute-start.19
  121.5 3.0 collective-permute-done.26.refs_5_
  130.0 6.2 %collective-permute-start.25 = (bf16[128,1024]{1,0:T(8,128)(2,1)S(1)}, bf16[128,1024]{1,0:T(8,128)(2,1)S(1)}, u32[]{:S(2)}, u32[]{:S(2)}) collective-permute-start(bf16[128,1024]{1,0:T(8,128)(2,1)S(1)} %collective-permute-done.24.refs_3_), channel_id=1, source_target_pairs={{0,8},{8,0},{16,24},{24,16},{32,40},{40,32},{48,56},{56,48},{1,9},... | collective-permute-start | bytes 786440 | tf_op jit(solution)/shard_map/ppermute | solution.py:88
  149.1 11.8 %shard_map.239 = (bf16[1024,576]{1,0:T(8,128)(2,1)S(1)}, bf16[1024,1152]{1,0:T(8,128)(2,1)S(1)}, bf16[8,128,1024]{2,1,0:T(8,128)(2,1)S(1)}, bf16[4,128,1024]{2,1...) custom-call(s32[8]{0:T(128)S(1)} %stack.53.order.refs_0_, ...), custom_call_target="tpu_custom_call" | custom-call | flops 8000000000 | bytes 16515104 | tf_op jit(solution)/shard_map/pallas_call | solution.py:35
  179.9 6.2 %shard_map.240 = bf16[8,128,1792]{2,1,0:T(8,128)(2,1)S(1)} custom-call(s32[8]{0:T(128)S(1)} %stack.53.order.refs_0_, bf16[128,1024]{1,0:T(8,128)(2,1)S(1)} %copy-done.56, bf16[128,1024]{1,0:T(8,128)(2,1)S(1)} %copy-done.68, bf16[128,1024]{1,0:T(8,128)(2,1)S(1)} %copy-done.65, bf16[128,1024]{1,0:T(8,128)(2,1)S(1)} %copy-done.77, ...), custom_call_target="tpu_custom_call" | custom-call | flops 4000000000 | bytes 11403296 | tf_op jit(solution)/shard_map/pallas_call | solution.py:35
  188.0 7.1 %collective-permute-done.35.refs_1_ = bf16[128,1024]{1,0:T(8,128)(2,1)S(1)} collective-permute-done((bf16[128,1024]{1,0:T(8,128)(2,1)S(1)}, bf16[128,1024]{1,0:T(8,128)(2,1)S(1)}, u32[]{:S(2)}, u32[]{:S(2)}) %collective-permute-start.35) | collective-permute-done | bytes 262176 | tf_op jit(solution)/shard_map/ppermute | solution.py:92
  203.6 2.9 collective-permute-start.44
  213.8 4.2 %collective-permute-done.50.refs_14_ = bf16[128,1024]{1,0:T(8,128)(2,1)S(1)} collective-permute-done((bf16[128,1024]{1,0:T(8,128)(2,1)S(1)}, bf16[128,1024]{1,0:T(8,128)(2,1)S(1)}, u32[]{:S(2)}, u32[]{:S(2)}) %collective-permute-start.50) | collective-permute-done | bytes 262176 | tf_op jit(solution)/shard_map/ppermute | solution.py:92
  220.0 4.1 %collective-permute-done.48.refs_12_ = bf16[128,1024]{1,0:T(8,128)(2,1)S(1)} collective-permute-done((bf16[128,1024]{1,0:T(8,128)(2,1)S(1)}, bf16[128,1024]{1,0:T(8,128)(2,1)S(1)}, u32[]{:S(2)}, u32[]{:S(2)}) %collective-permute-start.48) | collective-permute-done | bytes 262176 | tf_op jit(solution)/shard_map/ppermute | solution.py:92
  225.6 8.8 %shard_map.242 = (f32[64,1]{1,0:T(8,128)S(1)}, f32[64,1]{1,0:T(8,128)S(1)}, bf16[1024,256]{1,0:T(8,128)(2,1)S(1)}, bf16[8,128,1024]{2,1,0:T(8,128)(2,1)S(1)}) custom-call(s32[8]{0:T(128)S(1)} %stack.53.order.refs_0_, bf16[128,128]{1,0:T(8,128)(2,1)S(1)} %get-tuple-element.182.refs_1_, bf16[128,128]{1,0:T(8,128)(2,1)S(1)} %collective-permute-done.38.refs_2_, ...), custom_call_target="tpu_custom_call" | custom-call | flops 8000000000 | bytes 5805088 | tf_op jit(solution)/shard_map/pallas_call | solution.py:35
  238.0 3.6 all-to-all-start.1
  242.3 16.0 %all-to-all-done.1.parts = bf16[8,128,512]{2,1,0:T(8,128)(2,1)S(1)} async-done(((bf16[8,128,512]{2,1,0:T(8,128)(2,1)}), bf16[8,128,512]{2,1,0:T(8,128)(2,1)S(1)}, u32[]{:S(2)}, u32[]{:S(2)}) %all-to-all-start.1) | async-done | bytes 1048608 | tf_op jit(solution)/shard_map/all_to_all | solution.py:159
  258.4 4.5 %all-to-all-start.2 = ((bf16[8,128,1792]{2,1,0:T(8,128)(2,1)}), bf16[8,128,1792]{2,1,0:T(8,128)(2,1)}, u32[]{:S(2)}, u32[]{:S(2)}) async-start(bf16[8,128,1792]{2,1,0:T(8,128)(2,1)} %copy-done.3), calls=%async_computation.4 | async-start | bytes 7340032 | tf_op jit(solution)/shard_map/all_to_all | solution.py:159
  263.1 4.9 %collective-permute-start.54 = (bf16[128,128]{1,0:T(8,128)(2,1)S(1)}, bf16[128,128]{1,0:T(8,128)(2,1)S(1)}, u32[]{:S(2)}, u32[]{:S(2)}) collective-permute-start(bf16[128,128]{1,0:T(8,128)(2,1)S(1)} %get-tuple-element.199), channel_id=1, source_target_pairs={{0,64},{1,72},{2,80},{3,88},{4,96},{5,104},{6,112},{7,120},{8,65},... | collective-permute-start | bytes 98312 | tf_op jit(solution)/shard_map/ppermute | solution.py:127
  269.9 21.2 %collective-permute-done.54.out_other = bf16[128,128]{1,0:T(8,128)(2,1)S(1)} collective-permute-done((bf16[128,128]{1,0:T(8,128)(2,1)S(1)}, bf16[128,128]{1,0:T(8,128)(2,1)S(1)}, u32[]{:S(2)}, u32[]{:S(2)}) %collective-permute-start.54) | collective-permute-done | bytes 32800 | tf_op jit(solution)/shard_map/ppermute | solution.py:127
  291.1 19.1 %collective-permute-done.53.out = bf16[128,128]{1,0:T(8,128)(2,1)S(1)} collective-permute-done((bf16[128,128]{1,0:T(8,128)(2,1)S(1)}, bf16[128,128]{1,0:T(8,128)(2,1)S(1)}, u32[]{:S(2)}, u32[]{:S(2)}) %collective-permute-start.53) | collective-permute-done | bytes 32800 | tf_op jit(solution)/shard_map/ppermute | solution.py:127
  310.3 4.7 %collective-permute-start.60 = (bf16[128,512]{1,0:T(8,128)(2,1)S(1)}, bf16[128,512]{1,0:T(8,128)(2,1)S(1)}, u32[]{:S(2)}, u32[]{:S(2)}) collective-permute-start(bf16[128,512]{1,0:T(8,128)(2,1)S(1)} %shard_map.245.refs_1_), channel_id=1, source_target_pairs={{0,32},{8,40},{16,48},{24,56},{32,0},{40,8},{48,16},{56,24},{1,33}... | collective-permute-start | bytes 393224 | tf_op jit(solution)/shard_map/ppermute | solution.py:92
  326.6 3.8 collective-permute-start.63
  332.4 3.1 collective-permute-done.63.down
  335.6 12.5 %collective-permute-start.70 = (bf16[128,1728]{1,0:T(8,128)(2,1)S(1)}, bf16[128,1728]{1,0:T(8,128)(2,1)S(1)}, u32[]{:S(2)}, u32[]{:S(2)}) collective-permute-start(bf16[128,1728]{1,0:T(8,128)(2,1)S(1)} %shard_map.248.refs_1_), channel_id=1, source_target_pairs={{0,32},{8,40},{16,48},{24,56},{32,0},{40,8},{48,16},{56,24},{1,33}... | collective-permute-start | bytes 1327112 | tf_op jit(solution)/shard_map/ppermute | solution.py:92
  351.8 4.1 %collective-permute-start.65 = (bf16[128,1728]{1,0:T(8,128)(2,1)S(1)}, bf16[128,1728]{1,0:T(8,128)(2,1)S(1)}, u32[]{:S(2)}, u32[]{:S(2)}) collective-permute-start(bf16[128,1728]{1,0:T(8,128)(2,1)S(1)} %shard_map.248.refs_1_), channel_id=1, source_target_pairs={{0,8},{8,0},{16,24},{24,16},{32,40},{40,32},{48,56},{56,48},{1,9},... | collective-permute-start | bytes 1327112 | tf_op jit(solution)/shard_map/ppermute | solution.py:88
  356.6 5.6 %collective-permute-start.71 = (bf16[128,1728]{1,0:T(8,128)(2,1)S(1)}, bf16[128,1728]{1,0:T(8,128)(2,1)}, u32[]{:S(2)}, u32[]{:S(2)}) collective-permute-start(bf16[128,1728]{1,0:T(8,128)(2,1)S(1)} %collective-permute-done.70.refs_7_), channel_id=1, source_target_pairs={{0,8},{8,0},{16,24},{24,16},{32,40},{40,32},{48,56},{56,48},{1,9},... | collective-permute-start | bytes 1327112 | tf_op jit(solution)/shard_map/ppermute | solution.py:88
  362.2 4.4 %collective-permute-done.68.refs_5_ = bf16[128,1728]{1,0:T(8,128)(2,1)S(1)} collective-permute-done((bf16[128,1728]{1,0:T(8,128)(2,1)S(1)}, bf16[128,1728]{1,0:T(8,128)(2,1)S(1)}, u32[]{:S(2)}, u32[]{:S(2)}) %collective-permute-start.68) | collective-permute-done | bytes 442400 | tf_op jit(solution)/shard_map/ppermute | solution.py:92
  372.5 5.3 %shard_map.249 = (f32[128,4608]{1,0:T(8,128)}, f32[128,4608]{1,0:T(8,128)}, f32[576,1024]{1,0:T(8,128)}) custom-call(s32[8]{0:T(128)S(1)} %stack.53.order.refs_0_, bf16[128,1728]{1,0:T(8,128)(2,1)S(1)} %shard_map.248.refs_1_, bf16[128,1728]{1,0:T(8,128)(2,1)S(1)} %collective-permute-done.65.refs_2_, bf16[128,1728]{1,0:T(8,128)(2,1)S(1)} %collective-permute-done.66.refs_3_, ...), custom_call_target="tpu_custom_call" | custom-call | flops 1000000 | bytes 10616864 | tf_op jit(solution)/shard_map/pallas_call | solution.py:35
  (368 shorter events, 156.0 us)
Async XLA Ops:
  7.2 133.0 %all-gather.2.cloned.1.call-start = ((), (), s32[]{:S(2)}) async-start(), calls=%async_computation.5 | async-start | bytes 2654208 | tf_op jit(solution)/shard_map/all_gather | solution.py:469
  9.5 36.7 %collective-permute-start.5 = (bf16[128,1024]{1,0:T(8,128)(2,1)S(1)}, bf16[128,1024]{1,0:T(8,128)(2,1)S(1)}, u32[]{:S(2)}, u32[]{:S(2)}) collective-permute-start(bf16[128,1024]{1,0:T(8,128)(2,1)S(1)} %fusion.3.refs_0_), channel_id=1, source_target_pairs={{0,32},{8,40},{16,48},{24,56},{32,0},{40,8},{48,16},{56,24},{1,33}... | collective-permute-start | bytes 786440 | tf_op jit(solution)/shard_map/ppermute | solution.py:92
  14.0 32.3 %collective-permute-start.3 = (bf16[128,1024]{1,0:T(8,128)(2,1)S(1)}, bf16[128,1024]{1,0:T(8,128)(2,1)S(1)}, u32[]{:S(2)}, u32[]{:S(2)}) collective-permute-start(bf16[128,1024]{1,0:T(8,128)(2,1)S(1)} %fusion.3.refs_0_), channel_id=1, source_target_pairs={{0,48},{8,56},{16,0},{24,8},{32,16},{40,24},{48,32},{56,40},{1,49}... | collective-permute-start | bytes 786440 | tf_op jit(solution)/shard_map/ppermute | solution.py:92
  14.5 32.3 %collective-permute-start.1 = (bf16[128,1024]{1,0:T(8,128)(2,1)S(1)}, bf16[128,1024]{1,0:T(8,128)(2,1)S(1)}, u32[]{:S(2)}, u32[]{:S(2)}) collective-permute-start(bf16[128,1024]{1,0:T(8,128)(2,1)S(1)} %fusion.3.refs_0_), channel_id=1, source_target_pairs={{0,16},{8,24},{16,32},{24,40},{32,48},{40,56},{48,0},{56,8},{1,17}... | collective-permute-start | bytes 786440 | tf_op jit(solution)/shard_map/ppermute | solution.py:92
  28.2 18.7 %collective-permute-start.11 = (bf16[128,1024]{1,0:T(8,128)(2,1)S(1)}, bf16[128,1024]{1,0:T(8,128)(2,1)S(1)}, u32[]{:S(2)}, u32[]{:S(2)}) collective-permute-start(bf16[128,1024]{1,0:T(8,128)(2,1)S(1)} %copy-done.87), channel_id=1, source_target_pairs={{0,1},{1,0},{2,3},{3,2},{4,5},{5,4},{6,7},{7,6},{8,9},{9,8},{10,11... | collective-permute-start | bytes 786440 | tf_op jit(solution)/shard_map/ppermute | solution.py:136
  49.8 33.2 %collective-permute-start.14 = (bf16[256,1024]{1,0:T(8,128)(2,1)}, bf16[256,1024]{1,0:T(8,128)(2,1)}, u32[]{:S(2)}, u32[]{:S(2)}) collective-permute-start(bf16[256,1024]{1,0:T(8,128)(2,1)} %pad_maximum_fusion), channel_id=1, source_target_pairs={{0,4},{1,5},{2,6},{3,7},{4,0},{5,1},{6,2},{7,3},{8,12},{9,13},{10,... | collective-permute-start | bytes 1572872 | tf_op jit(solution)/shard_map/ppermute | solution.py:136
  49.9 37.1 %collective-permute-start.13 = (bf16[256,1024]{1,0:T(8,128)(2,1)}, bf16[256,1024]{1,0:T(8,128)(2,1)}, u32[]{:S(2)}, u32[]{:S(2)}) collective-permute-start(bf16[256,1024]{1,0:T(8,128)(2,1)} %pad_maximum_fusion), channel_id=1, source_target_pairs={{0,6},{1,7},{2,0},{3,1},{4,2},{5,3},{6,4},{7,5},{8,14},{9,15},{10,... | collective-permute-start | bytes 1572872 | tf_op jit(solution)/shard_map/ppermute | solution.py:136
  52.1 39.6 %collective-permute-start.12 = (bf16[256,1024]{1,0:T(8,128)(2,1)}, bf16[256,1024]{1,0:T(8,128)(2,1)}, u32[]{:S(2)}, u32[]{:S(2)}) collective-permute-start(bf16[256,1024]{1,0:T(8,128)(2,1)} %pad_maximum_fusion), channel_id=1, source_target_pairs={{0,2},{1,3},{2,4},{3,5},{4,6},{5,7},{6,0},{7,1},{8,10},{9,11},{10,... | collective-permute-start | bytes 1572872 | tf_op jit(solution)/shard_map/ppermute | solution.py:136
  57.9 25.2 %collective-permute-start.15 = (bf16[128,576]{1,0:T(8,128)(2,1)}, bf16[128,576]{1,0:T(8,128)(2,1)}, u32[]{:S(2)}, u32[]{:S(2)}) collective-permute-start(bf16[128,576]{1,0:T(8,128)(2,1)} %dynamic-slice_bitcast_fusion), channel_id=1, source_target_pairs={{0,0},{1,8},{2,16},{3,24},{4,32},{5,40},{6,48},{7,56},{8,1},{9,9},... | collective-permute-start | bytes 442376 | tf_op jit(solution)/shard_map/ppermute | solution.py:127
  62.3 77.9 %all-to-all-start = ((bf16[8,128,1024]{2,1,0:T(8,128)(2,1)}), bf16[8,128,1024]{2,1,0:T(8,128)(2,1)}, u32[]{:S(2)}, u32[]{:S(2)}) async-start(bf16[8,128,1024]{2,1,0:T(8,128)(2,1)} %broadcast_in_dim.48), calls=%async_computation | async-start | bytes 4194304 | tf_op jit(solution)/shard_map/all_to_all | solution.py:159
  69.1 281.1 %reduce-scatter.3.cloned.1.call-start = ((), (), s32[]{:S(2)}) async-start(), calls=%async_computation.6 | async-start | bytes 2359296 | tf_op jit(solution)/shard_map/reduce_scatter | solution.py:536
  92.0 14.4 %collective-permute-start.18 = (bf16[128,128]{1,0:T(8,128)(2,1)S(1)}, bf16[128,128]{1,0:T(8,128)(2,1)S(1)}, u32[]{:S(2)}, u32[]{:S(2)}) collective-permute-start(bf16[128,128]{1,0:T(8,128)(2,1)S(1)} %get-tuple-element.138.refs_21_), channel_id=1, source_target_pairs={{0,24},{8,16},{16,40},{24,32},{32,56},{40,48},{48,8},{56,0},{1,25}... | collective-permute-start | bytes 98312 | tf_op jit(solution)/shard_map/ppermute | solution.py:115
  116.9 12.9 %collective-permute-start.32 = (bf16[256,576]{1,0:T(8,128)(2,1)S(1)}, bf16[256,576]{1,0:T(8,128)(2,1)S(1)}, u32[]{:S(2)}, u32[]{:S(2)}) collective-permute-start(bf16[256,576]{1,0:T(8,128)(2,1)S(1)} %get-tuple-element.217), channel_id=1, source_target_pairs={{0,6},{1,7},{2,0},{3,1},{4,2},{5,3},{6,4},{7,5},{8,14},{9,15},{10,... | collective-permute-start | bytes 884744 | tf_op jit(solution)/shard_map/ppermute | solution.py:136
  120.1 16.1 %collective-permute-start.33 = (bf16[256,576]{1,0:T(8,128)(2,1)S(1)}, bf16[256,576]{1,0:T(8,128)(2,1)S(1)}, u32[]{:S(2)}, u32[]{:S(2)}) collective-permute-start(bf16[256,576]{1,0:T(8,128)(2,1)S(1)} %get-tuple-element.217), channel_id=1, source_target_pairs={{0,4},{1,5},{2,6},{3,7},{4,0},{5,1},{6,2},{7,3},{8,12},{9,13},{10,... | collective-permute-start | bytes 884744 | tf_op jit(solution)/shard_map/ppermute | solution.py:136
  174.1 13.9 %collective-permute-start.37 = (bf16[128,1024]{1,0:T(8,128)(2,1)S(1)}, bf16[128,1024]{1,0:T(8,128)(2,1)S(1)}, u32[]{:S(2)}, u32[]{:S(2)}) collective-permute-start(bf16[128,1024]{1,0:T(8,128)(2,1)S(1)} %get-tuple-element.211), channel_id=1, source_target_pairs={{0,16},{8,24},{16,32},{24,40},{32,48},{40,56},{48,0},{56,8},{1,17}... | collective-permute-start | bytes 786440 | tf_op jit(solution)/shard_map/ppermute | solution.py:92
  174.6 13.5 %collective-permute-start.36 = (bf16[128,1024]{1,0:T(8,128)(2,1)S(1)}, bf16[128,1024]{1,0:T(8,128)(2,1)S(1)}, u32[]{:S(2)}, u32[]{:S(2)}) collective-permute-start(bf16[128,1024]{1,0:T(8,128)(2,1)S(1)} %get-tuple-element.212), channel_id=1, source_target_pairs={{0,48},{8,56},{16,0},{24,8},{32,16},{40,24},{48,32},{56,40},{1,49}... | collective-permute-start | bytes 786440 | tf_op jit(solution)/shard_map/ppermute | solution.py:92
  176.9 18.3 %collective-permute-start.35 = (bf16[128,1024]{1,0:T(8,128)(2,1)S(1)}, bf16[128,1024]{1,0:T(8,128)(2,1)S(1)}, u32[]{:S(2)}, u32[]{:S(2)}) collective-permute-start(bf16[128,1024]{1,0:T(8,128)(2,1)S(1)} %get-tuple-element.213), channel_id=1, source_target_pairs={{0,32},{8,40},{16,48},{24,56},{32,0},{40,8},{48,16},{56,24},{1,33}... | collective-permute-start | bytes 786440 | tf_op jit(solution)/shard_map/ppermute | solution.py:92
  211.2 12.9 %collective-permute-start.48 = (bf16[128,1024]{1,0:T(8,128)(2,1)S(1)}, bf16[128,1024]{1,0:T(8,128)(2,1)S(1)}, u32[]{:S(2)}, u32[]{:S(2)}) collective-permute-start(bf16[128,1024]{1,0:T(8,128)(2,1)S(1)} %get-tuple-element.193.refs_8_), channel_id=1, source_target_pairs={{0,48},{8,56},{16,0},{24,8},{32,16},{40,24},{48,32},{56,40},{1,49}... | collective-permute-start | bytes 786440 | tf_op jit(solution)/shard_map/ppermute | solution.py:92
  212.2 13.0 %collective-permute-start.46 = (bf16[128,1024]{1,0:T(8,128)(2,1)S(1)}, bf16[128,1024]{1,0:T(8,128)(2,1)S(1)}, u32[]{:S(2)}, u32[]{:S(2)}) collective-permute-start(bf16[128,1024]{1,0:T(8,128)(2,1)S(1)} %get-tuple-element.193.refs_8_), channel_id=1, source_target_pairs={{0,16},{8,24},{16,32},{24,40},{32,48},{40,56},{48,0},{56,8},{1,17}... | collective-permute-start | bytes 786440 | tf_op jit(solution)/shard_map/ppermute | solution.py:92
  212.7 23.0 %collective-permute-start.45 = (bf16[128,1024]{1,0:T(8,128)(2,1)S(1)}, bf16[128,1024]{1,0:T(8,128)(2,1)S(1)}, u32[]{:S(2)}, u32[]{:S(2)}) collective-permute-start(bf16[128,1024]{1,0:T(8,128)(2,1)S(1)} %get-tuple-element.193.refs_8_), channel_id=1, source_target_pairs={{0,8},{8,0},{16,24},{24,16},{32,40},{40,32},{48,56},{56,48},{1,9},... | collective-permute-start | bytes 786440 | tf_op jit(solution)/shard_map/ppermute | solution.py:88
  218.0 17.7 %collective-permute-start.51 = (bf16[128,1024]{1,0:T(8,128)(2,1)S(1)}, bf16[128,1024]{1,0:T(8,128)(2,1)S(1)}, u32[]{:S(2)}, u32[]{:S(2)}) collective-permute-start(bf16[128,1024]{1,0:T(8,128)(2,1)S(1)} %collective-permute-done.50.refs_14_), channel_id=1, source_target_pairs={{0,8},{8,0},{16,24},{24,16},{32,40},{40,32},{48,56},{56,48},{1,9},... | collective-permute-start | bytes 786440 | tf_op jit(solution)/shard_map/ppermute | solution.py:88
  238.0 20.3 %all-to-all-start.1 = ((bf16[8,128,512]{2,1,0:T(8,128)(2,1)}), bf16[8,128,512]{2,1,0:T(8,128)(2,1)S(1)}, u32[]{:S(2)}, u32[]{:S(2)}) async-start(bf16[8,128,512]{2,1,0:T(8,128)(2,1)} %shard_map.243), calls=%async_computation.3 | async-start | bytes 2097152 | tf_op jit(solution)/shard_map/all_to_all | solution.py:159
  241.6 127.8 %reduce-scatter.5.cloned.1.call-start = ((), (), s32[]{:S(2)}) async-start(), calls=%async_computation.7 | async-start | bytes 2359296 | tf_op jit(solution)/shard_map/reduce_scatter | solution.py:564
  258.4 62.1 %all-to-all-start.2 = ((bf16[8,128,1792]{2,1,0:T(8,128)(2,1)}), bf16[8,128,1792]{2,1,0:T(8,128)(2,1)}, u32[]{:S(2)}, u32[]{:S(2)}) async-start(bf16[8,128,1792]{2,1,0:T(8,128)(2,1)} %copy-done.3), calls=%async_computation.4 | async-start | bytes 7340032 | tf_op jit(solution)/shard_map/all_to_all | solution.py:159
  263.0 47.2 %collective-permute-start.52 = (bf16[128,384]{1,0:T(8,128)(2,1)S(1)}, bf16[128,384]{1,0:T(8,128)(2,1)S(1)}, u32[]{:S(2)}, u32[]{:S(2)}) collective-permute-start(bf16[128,384]{1,0:T(8,128)(2,1)S(1)} %get-tuple-element.198.own), channel_id=1, source_target_pairs={{0,64},{64,0},{1,65},{65,1},{2,66},{66,2},{3,67},{67,3},{4,68},{68... | collective-permute-start | bytes 294920 | tf_op jit(solution)/shard_map/ppermute | solution.py:131
  263.1 28.0 %collective-permute-start.54 = (bf16[128,128]{1,0:T(8,128)(2,1)S(1)}, bf16[128,128]{1,0:T(8,128)(2,1)S(1)}, u32[]{:S(2)}, u32[]{:S(2)}) collective-permute-start(bf16[128,128]{1,0:T(8,128)(2,1)S(1)} %get-tuple-element.199), channel_id=1, source_target_pairs={{0,64},{1,72},{2,80},{3,88},{4,96},{5,104},{6,112},{7,120},{8,65},... | collective-permute-start | bytes 98312 | tf_op jit(solution)/shard_map/ppermute | solution.py:127
  268.0 42.2 %collective-permute-start.53 = (bf16[128,128]{1,0:T(8,128)(2,1)S(1)}, bf16[128,128]{1,0:T(8,128)(2,1)S(1)}, u32[]{:S(2)}, u32[]{:S(2)}) collective-permute-start(bf16[128,128]{1,0:T(8,128)(2,1)S(1)} %get-tuple-element.199), channel_id=1, source_target_pairs={{0,0},{1,8},{2,16},{3,24},{4,32},{5,40},{6,48},{7,56},{8,1},{9,9},... | collective-permute-start | bytes 98312 | tf_op jit(solution)/shard_map/ppermute | solution.py:127
  335.6 21.0 %collective-permute-start.70 = (bf16[128,1728]{1,0:T(8,128)(2,1)S(1)}, bf16[128,1728]{1,0:T(8,128)(2,1)S(1)}, u32[]{:S(2)}, u32[]{:S(2)}) collective-permute-start(bf16[128,1728]{1,0:T(8,128)(2,1)S(1)} %shard_map.248.refs_1_), channel_id=1, source_target_pairs={{0,32},{8,40},{16,48},{24,56},{32,0},{40,8},{48,16},{56,24},{1,33}... | collective-permute-start | bytes 1327112 | tf_op jit(solution)/shard_map/ppermute | solution.py:92
  348.1 18.5 %collective-permute-start.68 = (bf16[128,1728]{1,0:T(8,128)(2,1)S(1)}, bf16[128,1728]{1,0:T(8,128)(2,1)S(1)}, u32[]{:S(2)}, u32[]{:S(2)}) collective-permute-start(bf16[128,1728]{1,0:T(8,128)(2,1)S(1)} %shard_map.248.refs_1_), channel_id=1, source_target_pairs={{0,48},{8,56},{16,0},{24,8},{32,16},{40,24},{48,32},{56,40},{1,49}... | collective-permute-start | bytes 1327112 | tf_op jit(solution)/shard_map/ppermute | solution.py:92
  348.1 20.8 %collective-permute-start.66 = (bf16[128,1728]{1,0:T(8,128)(2,1)S(1)}, bf16[128,1728]{1,0:T(8,128)(2,1)S(1)}, u32[]{:S(2)}, u32[]{:S(2)}) collective-permute-start(bf16[128,1728]{1,0:T(8,128)(2,1)S(1)} %shard_map.248.refs_1_), channel_id=1, source_target_pairs={{0,16},{8,24},{16,32},{24,40},{32,48},{40,56},{48,0},{56,8},{1,17}... | collective-permute-start | bytes 1327112 | tf_op jit(solution)/shard_map/ppermute | solution.py:92
  351.8 20.7 %collective-permute-start.65 = (bf16[128,1728]{1,0:T(8,128)(2,1)S(1)}, bf16[128,1728]{1,0:T(8,128)(2,1)S(1)}, u32[]{:S(2)}, u32[]{:S(2)}) collective-permute-start(bf16[128,1728]{1,0:T(8,128)(2,1)S(1)} %shard_map.248.refs_1_), channel_id=1, source_target_pairs={{0,8},{8,0},{16,24},{24,16},{32,40},{40,32},{48,56},{56,48},{1,9},... | collective-permute-start | bytes 1327112 | tf_op jit(solution)/shard_map/ppermute | solution.py:88
  356.6 15.9 %collective-permute-start.71 = (bf16[128,1728]{1,0:T(8,128)(2,1)S(1)}, bf16[128,1728]{1,0:T(8,128)(2,1)}, u32[]{:S(2)}, u32[]{:S(2)}) collective-permute-start(bf16[128,1728]{1,0:T(8,128)(2,1)S(1)} %collective-permute-done.70.refs_7_), channel_id=1, source_target_pairs={{0,8},{8,0},{16,24},{24,16},{32,40},{40,32},{48,56},{56,48},{1,9},... | collective-permute-start | bytes 1327112 | tf_op jit(solution)/shard_map/ppermute | solution.py:88
  (136 other events, 1327.7 us)
Sparse Core Ops, SparseCore 0:
  17.7 70.8 all-gather.1
  169.2 33.8 reduce-scatter.2
  245.4 32.0 reduce-scatter.4
